TPU v7x, 32 devices: a whole 2x2x4 slice. The times are simulated.
32 devices in a mesh: row: 2 (over core), col: 4 (over y, x), seed: 4 (over z).
Axes of the slice: x: 2, y: 2, z: 4, core: 2. Of those that a mesh axis runs over, the one named last changes fastest.
Arguments:
- tiles: bfloat16 [2, 4, 384, 128, 128], P('row', 'col'), may hold values from -0.0390625 to 0.0390625
- tile_out: int32 [2, 4, 384], P('row', 'col'), may hold values from 0 to 1, as said below
- tile_in: int32 [2, 4, 384], P('row', 'col'), may hold values from 0 to 3
- tile_count: int32 [2, 4], P('row', 'col'), may hold values from 1 to 384, as said below
- out_degree: int32 [1024], P(('row', 'col')), may hold values from 1 to 8
- seed_ids: int32 [512, 16], P('seed'), may hold values from 0 to 1023
- prior: float32 [512, 1024], P('seed', ('row', 'col')), may hold values from -6 to 6
Outputs:
- risk: float32 [512, 1024], P('seed', ('row', 'col'))
Inputs may be any that keep to these rules, and one draw needn't show every extreme that they name: `tile_count`: occupied slots of a device come first; some device has all 384 occupied in every draw. `tile_out`: on every device the output blocks named by the occupied slots never fall from one slot to the next; several occupied slots of one device may name the same output block, and the same pair of blocks.
All inputs are finite; a program needn't handle non-finite values.
Results may differ from a plain program's by a relative error of at most 0.0041.
Values may be sent and summed in bfloat16 or wider, within the bound.
No kernel may reach another device: no remote copies, remote signals or barrier semaphores. Data moves between devices by JAX's collectives and lax.ppermute only.
A program may use at most 64 MiB of HBM per device.

v0:
```python
import math

import jax
import jax.numpy as jnp
from jax import lax
from jax.sharding import PartitionSpec as P

ITERATIONS = 2


damping = 0.85


def products(blocks, tiles_here, out_ids, in_ids, first_slot, end_slot, base_block, block_total):
    slot_total = tiles_here.shape[0]
    group_size = math.gcd(slot_total, 32)
    sets_here = blocks.shape[1]
    block_edge = tiles_here.shape[2]
    offsets = jnp.arange(group_size, dtype=jnp.int32)
    first_group = first_slot // group_size
    end_group = (end_slot + group_size - 1) // group_size

    def advance(group_index, panel_sum):
        slot_start = group_index * group_size
        tile_block = lax.dynamic_slice_in_dim(tiles_here, slot_start, group_size, 0)
        targets = lax.dynamic_slice_in_dim(out_ids, slot_start, group_size, 0) - base_block
        sources = lax.dynamic_slice_in_dim(in_ids, slot_start, group_size, 0)
        gathered = jnp.take(blocks, sources, axis=0)
        product = jnp.einsum(
            "gsk,gkj->gsj", gathered, tile_block, preferred_element_type=jnp.float32
        )
        slot_here = slot_start + offsets
        valid_mask = ((slot_here >= first_slot) & (slot_here < end_slot)).astype(jnp.float32)
        targets = jnp.clip(targets, 0, block_total - 1)
        return panel_sum.at[targets].add(product * valid_mask[:, None, None])

    zero_panel = jnp.zeros((block_total, sets_here, block_edge), jnp.float32)
    return lax.fori_loop(first_group, end_group, advance, zero_panel)


def local(tiles, tile_out, tile_in, tile_count, out_degree, seed_ids, prior):
    tiles_here = tiles[0, 0]
    out_ids = tile_out[0, 0]
    in_ids = tile_in[0, 0]
    occupied = tile_count[0, 0]
    row_devices = lax.axis_size("row")
    col_devices = lax.axis_size("col")
    sets_here, owned_count = prior.shape
    block_edge = tiles_here.shape[1]
    owned_blocks = owned_count // block_edge
    out_blocks = row_devices * owned_blocks
    own_start = (lax.axis_index("row") * col_devices + lax.axis_index("col")) * owned_count
    local_ids = seed_ids - own_start
    positions = jnp.arange(owned_count, dtype=jnp.int32)
    restart_rows = jnp.sum(
        (local_ids[:, :, None] == positions[None, None, :]).astype(jnp.float32), axis=1
    )
    restart = restart_rows.reshape(sets_here, owned_blocks, block_edge).transpose(1, 0, 2)
    degree = out_degree.astype(jnp.float32).reshape(owned_blocks, 1, block_edge)
    risk_now = prior.reshape(sets_here, owned_blocks, block_edge).transpose(1, 0, 2)
    for round_index in range(ITERATIONS):
        scaled = (risk_now / degree).astype(jnp.bfloat16)
        blocks = lax.all_gather(scaled, "col", axis=0, tiled=True)
        partial_value = products(blocks, tiles_here, out_ids, in_ids, 0, occupied, 0, out_blocks)
        incoming = lax.psum_scatter(partial_value, "row", scatter_dimension=0, tiled=True)
        risk_now = (1.0 - damping) * restart + damping * incoming
    return risk_now.transpose(1, 0, 2).reshape(sets_here, owned_count)


def solution(mesh):
    placed = (
        P("row", "col", None, None, None),
        P("row", "col", None),
        P("row", "col", None),
        P("row", "col"),
        P(("row", "col")),
        P("seed", None),
        P("seed", ("row", "col")),
    )
    return jax.shard_map(
        local, mesh=mesh, in_specs=placed, out_specs=P("seed", ("row", "col")), check_vma=False
    )
```

profile of v0, /device:TPU:0, one launch (start us, length us, event | category | flops | bytes accessed | tf_op | source)
XLA Modules:
  0.0 196.8 jit_solution(5287576053337724991)
XLA Ops:
  8.7 9.9 %all-gather = bf16[512,128]{1,0:T(8,128)(2,1)S(1)} all-gather(bf16[128,128]{1,0:T(8,128)(2,1)S(1)} %divide_convert_fusion), channel_id=2, replica_groups=mesh['row'=2,'col'=4,'seed'=4] {'col'}, dimensions={0}, use_global_device_ids=true | all-gather | bytes 163840 | tf_op jit(solution)/shard_map/all_gather | solution.py:63
  20.1 71.9 %while.22 = (s32[]{:T(128)}, f32[2,128,128]{2,1,0:T(8,128)S(1)}, s32[]{:T(128)}, s32[384]{0:T(512)S(1)}, s32[384]{0:T(512)S(1)}, /*index=5*/bf16[4,128,128]{2,1,...) while((s32[]{:T(128)}, f32[2,128,128]{2,1,0:T(8,128)S(1)}, ...), condition=%wide.region_3.5_spmd.clone, body=%wide.region_1.4_spmd.clone.sunk | while | flops 135792096 | bytes 12588407 | solution.py:38
  21.6 1.7 convolution_multiply_fusion.4
  23.4 2.7 %scatter_fusion = f32[2,128,128]{2,1,0:T(8,128)S(1)} fusion(f32[2,128,128]{2,1,0:T(8,128)S(1)} %get-tuple-element.305, s32[32]{0:T(128)S(1)} %compare_select_fusion.8, f32[32,128,128]{2,1,0:T(8,128)S(1)} %convolution_multiply_fusion.4), kind=kCustom, calls=%fused_computation.2.clone.clone.1 | custom fusion | flops 524288 | bytes 6291584 | tf_op jit(solution)/shard_map/while/body/scatter-add | solution.py:35
  27.6 1.7 convolution_multiply_fusion.4
  29.4 2.7 %scatter_fusion = f32[2,128,128]{2,1,0:T(8,128)S(1)} fusion(f32[2,128,128]{2,1,0:T(8,128)S(1)} %get-tuple-element.305, s32[32]{0:T(128)S(1)} %compare_select_fusion.8, f32[32,128,128]{2,1,0:T(8,128)S(1)} %convolution_multiply_fusion.4), kind=kCustom, calls=%fused_computation.2.clone.clone.1 | custom fusion | flops 524288 | bytes 6291584 | tf_op jit(solution)/shard_map/while/body/scatter-add | solution.py:35
  33.6 1.7 convolution_multiply_fusion.4
  35.4 2.7 %scatter_fusion = f32[2,128,128]{2,1,0:T(8,128)S(1)} fusion(f32[2,128,128]{2,1,0:T(8,128)S(1)} %get-tuple-element.305, s32[32]{0:T(128)S(1)} %compare_select_fusion.8, f32[32,128,128]{2,1,0:T(8,128)S(1)} %convolution_multiply_fusion.4), kind=kCustom, calls=%fused_computation.2.clone.clone.1 | custom fusion | flops 524288 | bytes 6291584 | tf_op jit(solution)/shard_map/while/body/scatter-add | solution.py:35
  39.6 1.7 convolution_multiply_fusion.4
  41.4 2.7 %scatter_fusion = f32[2,128,128]{2,1,0:T(8,128)S(1)} fusion(f32[2,128,128]{2,1,0:T(8,128)S(1)} %get-tuple-element.305, s32[32]{0:T(128)S(1)} %compare_select_fusion.8, f32[32,128,128]{2,1,0:T(8,128)S(1)} %convolution_multiply_fusion.4), kind=kCustom, calls=%fused_computation.2.clone.clone.1 | custom fusion | flops 524288 | bytes 6291584 | tf_op jit(solution)/shard_map/while/body/scatter-add | solution.py:35
  47.4 2.7 %scatter_fusion = f32[2,128,128]{2,1,0:T(8,128)S(1)} fusion(f32[2,128,128]{2,1,0:T(8,128)S(1)} %get-tuple-element.305, s32[32]{0:T(128)S(1)} %compare_select_fusion.8, f32[32,128,128]{2,1,0:T(8,128)S(1)} %convolution_multiply_fusion.4), kind=kCustom, calls=%fused_computation.2.clone.clone.1 | custom fusion | flops 524288 | bytes 6291584 | tf_op jit(solution)/shard_map/while/body/scatter-add | solution.py:35
  51.5 1.7 convolution_multiply_fusion.4
  53.3 2.7 %scatter_fusion = f32[2,128,128]{2,1,0:T(8,128)S(1)} fusion(f32[2,128,128]{2,1,0:T(8,128)S(1)} %get-tuple-element.305, s32[32]{0:T(128)S(1)} %compare_select_fusion.8, f32[32,128,128]{2,1,0:T(8,128)S(1)} %convolution_multiply_fusion.4), kind=kCustom, calls=%fused_computation.2.clone.clone.1 | custom fusion | flops 524288 | bytes 6291584 | tf_op jit(solution)/shard_map/while/body/scatter-add | solution.py:35
  57.5 1.7 convolution_multiply_fusion.4
  59.3 2.7 %scatter_fusion = f32[2,128,128]{2,1,0:T(8,128)S(1)} fusion(f32[2,128,128]{2,1,0:T(8,128)S(1)} %get-tuple-element.305, s32[32]{0:T(128)S(1)} %compare_select_fusion.8, f32[32,128,128]{2,1,0:T(8,128)S(1)} %convolution_multiply_fusion.4), kind=kCustom, calls=%fused_computation.2.clone.clone.1 | custom fusion | flops 524288 | bytes 6291584 | tf_op jit(solution)/shard_map/while/body/scatter-add | solution.py:35
  65.3 2.7 %scatter_fusion = f32[2,128,128]{2,1,0:T(8,128)S(1)} fusion(f32[2,128,128]{2,1,0:T(8,128)S(1)} %get-tuple-element.305, s32[32]{0:T(128)S(1)} %compare_select_fusion.8, f32[32,128,128]{2,1,0:T(8,128)S(1)} %convolution_multiply_fusion.4), kind=kCustom, calls=%fused_computation.2.clone.clone.1 | custom fusion | flops 524288 | bytes 6291584 | tf_op jit(solution)/shard_map/while/body/scatter-add | solution.py:35
  69.5 1.7 convolution_multiply_fusion.4
  71.3 2.7 %scatter_fusion = f32[2,128,128]{2,1,0:T(8,128)S(1)} fusion(f32[2,128,128]{2,1,0:T(8,128)S(1)} %get-tuple-element.305, s32[32]{0:T(128)S(1)} %compare_select_fusion.8, f32[32,128,128]{2,1,0:T(8,128)S(1)} %convolution_multiply_fusion.4), kind=kCustom, calls=%fused_computation.2.clone.clone.1 | custom fusion | flops 524288 | bytes 6291584 | tf_op jit(solution)/shard_map/while/body/scatter-add | solution.py:35
  75.5 1.7 convolution_multiply_fusion.4
  77.3 2.7 %scatter_fusion = f32[2,128,128]{2,1,0:T(8,128)S(1)} fusion(f32[2,128,128]{2,1,0:T(8,128)S(1)} %get-tuple-element.305, s32[32]{0:T(128)S(1)} %compare_select_fusion.8, f32[32,128,128]{2,1,0:T(8,128)S(1)} %convolution_multiply_fusion.4), kind=kCustom, calls=%fused_computation.2.clone.clone.1 | custom fusion | flops 524288 | bytes 6291584 | tf_op jit(solution)/shard_map/while/body/scatter-add | solution.py:35
  83.3 2.7 %scatter_fusion = f32[2,128,128]{2,1,0:T(8,128)S(1)} fusion(f32[2,128,128]{2,1,0:T(8,128)S(1)} %get-tuple-element.305, s32[32]{0:T(128)S(1)} %compare_select_fusion.8, f32[32,128,128]{2,1,0:T(8,128)S(1)} %convolution_multiply_fusion.4), kind=kCustom, calls=%fused_computation.2.clone.clone.1 | custom fusion | flops 524288 | bytes 6291584 | tf_op jit(solution)/shard_map/while/body/scatter-add | solution.py:35
  87.5 1.7 convolution_multiply_fusion.4
  89.3 2.7 %scatter_fusion = f32[2,128,128]{2,1,0:T(8,128)S(1)} fusion(f32[2,128,128]{2,1,0:T(8,128)S(1)} %get-tuple-element.305, s32[32]{0:T(128)S(1)} %compare_select_fusion.8, f32[32,128,128]{2,1,0:T(8,128)S(1)} %convolution_multiply_fusion.4), kind=kCustom, calls=%fused_computation.2.clone.clone.1 | custom fusion | flops 524288 | bytes 6291584 | tf_op jit(solution)/shard_map/while/body/scatter-add | solution.py:35
  93.2 6.5 %reduce-scatter.3.cloned.1.call-done = f32[1,128,128]{2,1,0:T(8,128)} async-done(((f32[2,128,128]{2,1,0:T(8,128)}), f32[1,128,128]{2,1,0:T(8,128)}) %reduce-scatter.3.cloned.1.call-update) | async-done | bytes 65552 | tf_op jit(solution)/shard_map/reduce_scatter | solution.py:65
  100.5 8.6 %all_gather.7 = bf16[4,128,128]{2,1,0:T(8,128)(2,1)S(1)} all-gather(bf16[1,128,128]{2,1,0:T(8,128)(2,1)S(1)} %fusion.17), channel_id=1, replica_groups=mesh['row'=2,'col'=4,'seed'=4] {'col'}, dimensions={0}, use_global_device_ids=true | all-gather | bytes 163840 | tf_op jit(solution)/shard_map/all_gather | solution.py:63
  109.2 71.9 %while.23 = (s32[]{:T(128)}, f32[2,128,128]{2,1,0:T(8,128)S(1)}, s32[]{:T(128)}, s32[384]{0:T(512)S(1)}, s32[384]{0:T(512)S(1)}, /*index=5*/bf16[4,128,128]{2,1,...) while((s32[]{:T(128)}, f32[2,128,128]{2,1,0:T(8,128)S(1)}, ...), condition=%wide.region_7.9_spmd.clone, body=%wide.region_5.8_spmd.clone.sunk | while | flops 135792096 | bytes 12588407 | solution.py:38
  110.7 1.7 convolution_multiply_fusion.5
  112.5 2.7 %scatter_fusion.1 = f32[2,128,128]{2,1,0:T(8,128)S(1)} fusion(f32[2,128,128]{2,1,0:T(8,128)S(1)} %get-tuple-element.341, s32[32]{0:T(128)S(1)} %compare_select_fusion.9, f32[32,128,128]{2,1,0:T(8,128)S(1)} %convolution_multiply_fusion.5), kind=kCustom, calls=%fused_computation.3.clone.clone.1 | custom fusion | flops 524288 | bytes 6291584 | tf_op jit(solution)/shard_map/while/body/scatter-add | solution.py:35
  116.7 1.7 convolution_multiply_fusion.5
  118.5 2.7 %scatter_fusion.1 = f32[2,128,128]{2,1,0:T(8,128)S(1)} fusion(f32[2,128,128]{2,1,0:T(8,128)S(1)} %get-tuple-element.341, s32[32]{0:T(128)S(1)} %compare_select_fusion.9, f32[32,128,128]{2,1,0:T(8,128)S(1)} %convolution_multiply_fusion.5), kind=kCustom, calls=%fused_computation.3.clone.clone.1 | custom fusion | flops 524288 | bytes 6291584 | tf_op jit(solution)/shard_map/while/body/scatter-add | solution.py:35
  124.5 2.7 %scatter_fusion.1 = f32[2,128,128]{2,1,0:T(8,128)S(1)} fusion(f32[2,128,128]{2,1,0:T(8,128)S(1)} %get-tuple-element.341, s32[32]{0:T(128)S(1)} %compare_select_fusion.9, f32[32,128,128]{2,1,0:T(8,128)S(1)} %convolution_multiply_fusion.5), kind=kCustom, calls=%fused_computation.3.clone.clone.1 | custom fusion | flops 524288 | bytes 6291584 | tf_op jit(solution)/shard_map/while/body/scatter-add | solution.py:35
  128.7 1.7 convolution_multiply_fusion.5
  130.5 2.7 %scatter_fusion.1 = f32[2,128,128]{2,1,0:T(8,128)S(1)} fusion(f32[2,128,128]{2,1,0:T(8,128)S(1)} %get-tuple-element.341, s32[32]{0:T(128)S(1)} %compare_select_fusion.9, f32[32,128,128]{2,1,0:T(8,128)S(1)} %convolution_multiply_fusion.5), kind=kCustom, calls=%fused_computation.3.clone.clone.1 | custom fusion | flops 524288 | bytes 6291584 | tf_op jit(solution)/shard_map/while/body/scatter-add | solution.py:35
  134.6 1.7 convolution_multiply_fusion.5
  136.5 2.7 %scatter_fusion.1 = f32[2,128,128]{2,1,0:T(8,128)S(1)} fusion(f32[2,128,128]{2,1,0:T(8,128)S(1)} %get-tuple-element.341, s32[32]{0:T(128)S(1)} %compare_select_fusion.9, f32[32,128,128]{2,1,0:T(8,128)S(1)} %convolution_multiply_fusion.5), kind=kCustom, calls=%fused_computation.3.clone.clone.1 | custom fusion | flops 524288 | bytes 6291584 | tf_op jit(solution)/shard_map/while/body/scatter-add | solution.py:35
  142.4 2.7 %scatter_fusion.1 = f32[2,128,128]{2,1,0:T(8,128)S(1)} fusion(f32[2,128,128]{2,1,0:T(8,128)S(1)} %get-tuple-element.341, s32[32]{0:T(128)S(1)} %compare_select_fusion.9, f32[32,128,128]{2,1,0:T(8,128)S(1)} %convolution_multiply_fusion.5), kind=kCustom, calls=%fused_computation.3.clone.clone.1 | custom fusion | flops 524288 | bytes 6291584 | tf_op jit(solution)/shard_map/while/body/scatter-add | solution.py:35
  146.6 1.7 convolution_multiply_fusion.5
  148.4 2.7 %scatter_fusion.1 = f32[2,128,128]{2,1,0:T(8,128)S(1)} fusion(f32[2,128,128]{2,1,0:T(8,128)S(1)} %get-tuple-element.341, s32[32]{0:T(128)S(1)} %compare_select_fusion.9, f32[32,128,128]{2,1,0:T(8,128)S(1)} %convolution_multiply_fusion.5), kind=kCustom, calls=%fused_computation.3.clone.clone.1 | custom fusion | flops 524288 | bytes 6291584 | tf_op jit(solution)/shard_map/while/body/scatter-add | solution.py:35
  152.6 1.7 convolution_multiply_fusion.5
  154.4 2.7 %scatter_fusion.1 = f32[2,128,128]{2,1,0:T(8,128)S(1)} fusion(f32[2,128,128]{2,1,0:T(8,128)S(1)} %get-tuple-element.341, s32[32]{0:T(128)S(1)} %compare_select_fusion.9, f32[32,128,128]{2,1,0:T(8,128)S(1)} %convolution_multiply_fusion.5), kind=kCustom, calls=%fused_computation.3.clone.clone.1 | custom fusion | flops 524288 | bytes 6291584 | tf_op jit(solution)/shard_map/while/body/scatter-add | solution.py:35
  158.6 1.7 convolution_multiply_fusion.5
  160.4 2.7 %scatter_fusion.1 = f32[2,128,128]{2,1,0:T(8,128)S(1)} fusion(f32[2,128,128]{2,1,0:T(8,128)S(1)} %get-tuple-element.341, s32[32]{0:T(128)S(1)} %compare_select_fusion.9, f32[32,128,128]{2,1,0:T(8,128)S(1)} %convolution_multiply_fusion.5), kind=kCustom, calls=%fused_computation.3.clone.clone.1 | custom fusion | flops 524288 | bytes 6291584 | tf_op jit(solution)/shard_map/while/body/scatter-add | solution.py:35
  164.6 1.7 convolution_multiply_fusion.5
  166.4 2.7 %scatter_fusion.1 = f32[2,128,128]{2,1,0:T(8,128)S(1)} fusion(f32[2,128,128]{2,1,0:T(8,128)S(1)} %get-tuple-element.341, s32[32]{0:T(128)S(1)} %compare_select_fusion.9, f32[32,128,128]{2,1,0:T(8,128)S(1)} %convolution_multiply_fusion.5), kind=kCustom, calls=%fused_computation.3.clone.clone.1 | custom fusion | flops 524288 | bytes 6291584 | tf_op jit(solution)/shard_map/while/body/scatter-add | solution.py:35
  170.6 1.7 convolution_multiply_fusion.5
  172.4 2.7 %scatter_fusion.1 = f32[2,128,128]{2,1,0:T(8,128)S(1)} fusion(f32[2,128,128]{2,1,0:T(8,128)S(1)} %get-tuple-element.341, s32[32]{0:T(128)S(1)} %compare_select_fusion.9, f32[32,128,128]{2,1,0:T(8,128)S(1)} %convolution_multiply_fusion.5), kind=kCustom, calls=%fused_computation.3.clone.clone.1 | custom fusion | flops 524288 | bytes 6291584 | tf_op jit(solution)/shard_map/while/body/scatter-add | solution.py:35
  178.4 2.7 %scatter_fusion.1 = f32[2,128,128]{2,1,0:T(8,128)S(1)} fusion(f32[2,128,128]{2,1,0:T(8,128)S(1)} %get-tuple-element.341, s32[32]{0:T(128)S(1)} %compare_select_fusion.9, f32[32,128,128]{2,1,0:T(8,128)S(1)} %convolution_multiply_fusion.5), kind=kCustom, calls=%fused_computation.3.clone.clone.1 | custom fusion | flops 524288 | bytes 6291584 | tf_op jit(solution)/shard_map/while/body/scatter-add | solution.py:35
  181.7 6.7 %reduce-scatter.5.cloned.1.call-done = f32[1,128,128]{2,1,0:T(8,128)} async-done(((f32[2,128,128]{2,1,0:T(8,128)}), f32[1,128,128]{2,1,0:T(8,128)}) %reduce-scatter.5.cloned.1.call-update) | async-done | bytes 65552 | tf_op jit(solution)/shard_map/reduce_scatter | solution.py:65
  (123 shorter events, 55.0 us)
Async XLA Ops:
  6.5 93.1 %reduce-scatter.3.cloned.1.call-start = ((), (), s32[]{:S(2)}) async-start(), calls=%async_computation.2 | async-start | bytes 196608 | tf_op jit(solution)/shard_map/reduce_scatter | solution.py:65
  20.1 72.6 %copy-start.2 = (s32[128,16]{0,1:T(8,128)S(1)}, s32[128,16]{0,1:T(8,128)}, u32[]{:S(2)}) copy-start(s32[128,16]{0,1:T(8,128)} %param.18) | copy-start | bytes 24580
  91.9 0.6 copy-start.1
  92.6 95.8 %reduce-scatter.5.cloned.1.call-start = ((), (), s32[]{:S(2)}) async-start(), calls=%async_computation.3 | async-start | bytes 196608 | tf_op jit(solution)/shard_map/reduce_scatter | solution.py:65
  181.0 0.6 copy-start
Sparse Core Ops, SparseCore 0:
  92.7 6.8 reduce-scatter.2
  181.8 6.5 reduce-scatter.4
where the time goes:
time: 197 us
  other arithmetic  88.9 us (45%)
  matrix products  41.2 us (21%)
  local copies, waits for them, and re-layouts  19.4 us (10%)
  blocking collectives  18.6 us (9%)
  between operations  14.2 us (7%)
  waiting for transfers between devices  13.2 us (7%)
    scatter-add x24, other arithmetic, advance(): return panel_sum.at[targets].add(product * valid_mask[:, None, None])  63.7 us
    dot_general x24, matrix products, advance(): jnp.einsum('gsk,gkj->gsj', gathered, tile_block, preferred_element_type=j...  41.2 us
    all_gather x2, blocking collectives, local(): blocks = lax.all_gather(scaled, 'col', axis=0, tiled=True)  18.6 us
    gather x24, local copies, waits for them, and re-layouts, advance(): gathered = jnp.take(blocks, sources, axis=0)  18 us
    and x24, other arithmetic, advance(): gathered = jnp.take(blocks, sources, axis=0)  17.5 us
    reduce_scatter x2, waiting for transfers between devices, local(): lax.psum_scatter(partial_value, 'row', scatter_dimension=0, tiled=True)  13.2 us
  transfers between devices with their start and end apart: 2, of which 2 were waited for; matrix products, arithmetic and copies ran while one was open for 0% of the time, Pallas kernels for 0%

commit v1 on v0

v1 whole, which is shorter than its diff:
```python
import functools
import math

import jax
import jax.numpy as jnp
from jax import lax
from jax.experimental import pallas as pl
from jax.experimental.pallas import tpu as pltpu
from jax.sharding import PartitionSpec as P

ITERATIONS = 2


damping = 0.85

VMEM = pl.BlockSpec(memory_space=pltpu.VMEM)
SMEM = pl.BlockSpec(memory_space=pltpu.SMEM)
HBM = pl.BlockSpec(memory_space=pl.ANY)

UNROLL = 4
FIELD_BITS = 8
FIELD_MASK = (1 << FIELD_BITS) - 1
WORD_FIELDS = 4


def partner(index, offset, extent):
    if extent & (extent - 1) == 0:
        return index ^ offset
    return (index + offset) % extent


def send_to(value, axes, extents, offsets):
    pairs = []
    for flat in range(math.prod(extents)):
        rest, source = flat, []
        for extent in reversed(extents):
            source.insert(0, rest % extent)
            rest //= extent
        origin = [partner(place, offset, extent) for place, offset, extent in zip(source, offsets, extents)]
        origin_flat = 0
        for place, extent in zip(origin, extents):
            origin_flat = origin_flat * extent + place
        pairs.append((origin_flat, flat))
    return lax.ppermute(value, axes, pairs)


def scale_kernel(prior_ref, degree_ref, scaled_ref):
    scaled_ref[...] = (prior_ref[...] / degree_ref[...].astype(jnp.float32)).astype(jnp.bfloat16)


def sum_kernel(rows, cols, owned_blocks, tiles_ref, out_ref, in_ref, count_ref, seeds_ref, *rest):
    weight_refs, restart_ref = rest[:rows], rest[rows]
    buffer, total, listed, arrived = rest[rows + 1:]
    in_blocks, out_blocks = cols * owned_blocks, rows * owned_blocks
    slots, edge = tiles_ref.shape[2], tiles_ref.shape[3]
    group = slots // arrived.shape[0]
    reach = group + UNROLL
    row, col = lax.axis_index("row"), lax.axis_index("col")

    def arrival(index):
        span = pl.ds(index * group, group)
        return pltpu.make_async_copy(tiles_ref.at[0, 0, span], buffer.at[span], arrived.at[index])

    for index in range(slots // group):
        arrival(index).start()

    buffer[slots] = jnp.zeros((edge, edge), jnp.bfloat16)
    total[...] = jnp.zeros(total.shape, jnp.float32)

    seed_total, sets = seeds_ref.shape
    owned = owned_blocks * edge
    vertex = lax.broadcasted_iota(jnp.int32, (owned, sets), 0) + (row * cols + col) * owned
    restart = jnp.zeros((owned, sets), jnp.float32)
    for seed in range(seed_total):
        restart += (seeds_ref[seed:seed + 1, :] == vertex).astype(jnp.float32)
    restart_ref[...] = (1.0 - damping) * restart.T

    occupied = count_ref[0, 0]

    def add_group(index, carry):
        first = index * group
        end = jnp.minimum(first + group, occupied)
        lowest = out_ref[0, 0, first]
        highest = out_ref[0, 0, jnp.maximum(end - 1, first)]

        def add_target(target, carry):
            def scan(step, words):
                words = list(words)
                for inner in range(8):
                    slot = first + step * 8 + inner
                    source = in_ref[0, 0, slot]
                    valid = (out_ref[0, 0, slot] == target) & (slot < occupied)
                    shift = (source % WORD_FIELDS) * FIELD_BITS
                    word = words[0]
                    for other in range(1, len(words)):
                        word = jnp.where(source // WORD_FIELDS == other, words[other], word)
                    place = (word >> shift) & FIELD_MASK
                    listed[source * reach + place] = slot
                    grown = jnp.where(valid, jnp.int32(1) << shift, 0)
                    if len(words) == 1:
                        words[0] = words[0] + grown
                    else:
                        for other in range(len(words)):
                            words[other] += jnp.where(source // WORD_FIELDS == other, grown, 0)
                return tuple(words)

            word_total = -(-in_blocks // WORD_FIELDS)
            words = lax.fori_loop(0, group // 8, scan, (jnp.int32(0),) * word_total)

            @pl.when(target == lowest)
            def _():
                arrival(index).wait()

            for source in range(in_blocks):
                held = (words[source // WORD_FIELDS] >> (source % WORD_FIELDS * FIELD_BITS)) & FIELD_MASK
                base = source * reach
                for pad in range(UNROLL - 1):
                    listed[base + held + pad] = slots
                pair = target * in_blocks + source

                def add_tiles(step, value):
                    at = base + step * UNROLL
                    parts = [buffer[listed[at + inner]].astype(jnp.float32) for inner in range(UNROLL)]
                    while len(parts) > 1:
                        parts = [a + b for a, b in zip(parts[::2], parts[1::2])]
                    return value + parts[0]

                total[pair] = lax.fori_loop(0, (held + UNROLL - 1) // UNROLL, add_tiles, total[pair])
            return carry

        return lax.fori_loop(lowest, jnp.maximum(highest, lowest) + 1, add_target, carry)

    lax.fori_loop(0, slots // group, add_group, 0)

    for offset in range(rows):
        owner = partner(row, offset, rows)
        for block in range(owned_blocks):
            for source in range(in_blocks):
                pair = (owner * owned_blocks + block) * in_blocks + source
                weight_refs[offset][
                    source * edge:(source + 1) * edge, block * edge:(block + 1) * edge
                ] = total[pair].astype(jnp.bfloat16)


def round_kernel(rows, cols, relative, last, *refs):
    block_total = rows * cols if relative else 1
    blocks, weights = refs[:block_total], refs[block_total:block_total + rows]
    restart_ref, degree_ref, result_ref = refs[block_total + rows:]
    row, col = lax.axis_index("row"), lax.axis_index("col")
    owned = restart_ref.shape[1]
    incoming = jnp.zeros(restart_ref.shape, jnp.float32)
    for row_offset in range(rows):
        for col_offset in range(cols):
            column = partner(col, col_offset, cols)
            if relative:
                scaled = blocks[row_offset * cols + col_offset][...]
            else:
                scaled = blocks[0][partner(row, row_offset, rows) * cols + column]
            weight = weights[row_offset][pl.ds(pl.multiple_of(column * owned, owned), owned), :]
            incoming += jnp.dot(scaled, weight, preferred_element_type=jnp.float32)
    risk = restart_ref[...] + damping * incoming
    if last:
        result_ref[...] = risk
    else:
        result_ref[...] = (risk / degree_ref[...].astype(jnp.float32)).astype(jnp.bfloat16)


def local(tiles, tile_out, tile_in, tile_count, out_degree, seed_ids, prior):
    rows, cols = lax.axis_size("row"), lax.axis_size("col")
    sets, owned = prior.shape
    slots, edge = tiles.shape[2], tiles.shape[3]
    owned_blocks = owned // edge
    in_blocks, out_blocks = cols * owned_blocks, rows * owned_blocks
    group = math.gcd(slots, 64)
    relative = rows * cols <= 8
    degree = out_degree.reshape(1, owned)

    scaled = pl.pallas_call(
        scale_kernel,
        out_shape=jax.ShapeDtypeStruct((sets, owned), jnp.bfloat16),
        in_specs=[VMEM, VMEM],
        out_specs=VMEM,
        cost_estimate=pl.CostEstimate(flops=sets * owned, bytes_accessed=6 * sets * owned, transcendentals=0),
        name="scale",
    )(prior, degree)

    def spread(value):
        if not relative:
            return [lax.all_gather(value, ("row", "col"), axis=0)]
        blocks = []
        for row_offset in range(rows):
            for col_offset in range(cols):
                if row_offset or col_offset:
                    blocks.append(send_to(value, ("row", "col"), (rows, cols), (row_offset, col_offset)))
                else:
                    blocks.append(value)
        return blocks

    blocks = spread(scaled)

    *weights, restart = pl.pallas_call(
        functools.partial(sum_kernel, rows, cols, owned_blocks),
        out_shape=[jax.ShapeDtypeStruct((in_blocks * edge, owned), jnp.bfloat16)] * rows
        + [jax.ShapeDtypeStruct((sets, owned), jnp.float32)],
        in_specs=[HBM, SMEM, SMEM, SMEM, VMEM],
        out_specs=[VMEM] * (rows + 1),
        scratch_shapes=[
            pltpu.VMEM((slots + 1, edge, edge), jnp.bfloat16),
            pltpu.VMEM((out_blocks * in_blocks, edge, edge), jnp.float32),
            pltpu.SMEM((in_blocks * (group + UNROLL),), jnp.int32),
            pltpu.SemaphoreType.DMA((slots // group,)),
        ],
        compiler_params=pltpu.CompilerParams(vmem_limit_bytes=32 * 1024 * 1024),
        cost_estimate=pl.CostEstimate(
            flops=slots * edge * edge, bytes_accessed=2 * slots * edge * edge, transcendentals=0
        ),
        name="sum_tiles",
    )(tiles, tile_out, tile_in, tile_count, seed_ids.T)

    weights = [weights[0]] + [
        send_to(weights[offset], ("row",), (rows,), (offset,)) for offset in range(1, rows)
    ]

    for round_index in range(ITERATIONS):
        last = round_index == ITERATIONS - 1
        value = pl.pallas_call(
            functools.partial(round_kernel, rows, cols, relative, last),
            out_shape=jax.ShapeDtypeStruct((sets, owned), jnp.float32 if last else jnp.bfloat16),
            in_specs=[VMEM] * (len(blocks) + rows + 2),
            out_specs=VMEM,
            compiler_params=pltpu.CompilerParams(vmem_limit_bytes=32 * 1024 * 1024),
            cost_estimate=pl.CostEstimate(
                flops=2 * sets * rows * cols * owned * owned,
                bytes_accessed=2 * rows * cols * owned * (sets + owned),
                transcendentals=0,
            ),
            name="last_round" if last else "first_round",
        )(*blocks, *weights, restart, degree)
        if not last:
            blocks = spread(value)
    return value


def solution(mesh):
    placed = (
        P("row", "col", None, None, None),
        P("row", "col", None),
        P("row", "col", None),
        P("row", "col"),
        P(("row", "col")),
        P("seed", None),
        P("seed", ("row", "col")),
    )
    return jax.shard_map(
        local, mesh=mesh, in_specs=placed, out_specs=P("seed", ("row", "col")), check_vma=False
    )
```

time: 197 us -> 41.2 us (0.21)
  other arithmetic: 88.9 us -> 0 us
  matrix products: 41.2 us -> 0 us
  blocking collectives: 18.6 us -> 0 us
  starting transfers between devices: 0.04 us -> 15.2 us
  between operations: 14.2 us -> 0.73 us
  local copies, waits for them, and re-layouts: 19.4 us -> 7.39 us
  Pallas kernels: 0 us -> 10.6 us
  waiting for transfers between devices: 13.2 us -> 7.47 us
    scatter-add x24 -> x0, other arithmetic: 63.7 us -> none  [advance(): return panel_sum.at[targets].add(product * valid_mask[:, None, None])]
    dot_general x24 -> x0, matrix products: 41.2 us -> none  [advance(): jnp.einsum('gsk,gkj->gsj', gathered, tile_block, preferred_element_type=j...]
    all_gather x2 -> x0, blocking collectives: 18.6 us -> none  [local(): blocks = lax.all_gather(scaled, 'col', axis=0, tiled=True)]
    gather x24 -> x0, local copies, waits for them, and re-layouts: 18 us -> none  [advance(): gathered = jnp.take(blocks, sources, axis=0)]
    and x24 -> x0, other arithmetic: 17.5 us -> none  [advance(): gathered = jnp.take(blocks, sources, axis=0)]
    ppermute x0 -> x15, starting transfers between devices: none -> 15.2 us  [send_to(): return lax.ppermute(value, axes, pairs)]
    reduce_scatter x2 -> x0, waiting for transfers between devices: 13.2 us -> none  [local(): lax.psum_scatter(partial_value, 'row', scatter_dimension=0, tiled=True)]
    pallas_call x0 -> x4, Pallas kernels: none -> 10.6 us  [the longest x1 8 us: local(): pl.pallas_call(functools.partial(sum_kernel, rows, cols, owned_blocks), o...]
  transfers between devices with their start and end apart: 2 -> 15, of which waited for: 2 -> 8; matrix products, arithmetic and copies ran while one was open for 0% -> 0% of each run, Pallas kernels for 0% -> 4%
where the time goes in v1:
time: 41.2 us; the launch traced here: 41.3 us
  starting transfers between devices  15.2 us (37%)
  Pallas kernels  10.6 us (26%)
  waiting for transfers between devices  7.47 us (18%)
  local copies, waits for them, and re-layouts  7.39 us (18%)
  between operations  0.73 us (2%)
    ppermute x15, starting transfers between devices, send_to(): return lax.ppermute(value, axes, pairs)  15.2 us
    pallas_call x1, Pallas kernels, local(): pl.pallas_call(functools.partial(sum_kernel, rows, cols, owned_blocks), o...  8 us
    ppermute x15, waiting for transfers between devices, send_to(): return lax.ppermute(value, axes, pairs)  7.47 us
    unnamed x12, local copies, waits for them, and re-layouts  7.39 us
    pallas_call x1, Pallas kernels, local(): pl.pallas_call(scale_kernel, out_shape=jax.ShapeDtypeStruct((sets, owned)...  1.47 us
    pallas_call x2, Pallas kernels, local(): pl.pallas_call(functools.partial(round_kernel, rows, cols, relative, last...  1.09 us
  transfers between devices with their start and end apart: 15, of which 8 were waited for; matrix products, arithmetic and copies ran while one was open for 0% of the time, Pallas kernels for 4%

profile of v1, /device:TPU:0, one launch (start us, length us, event | category | flops | bytes accessed | tf_op | source)
XLA Modules:
  0.0 41.3 jit_solution(5632847342705516479)
XLA Ops:
  0.0 0.0 copy-start.3
  0.7 0.0 copy-start
  0.7 4.6 %copy-done = bf16[1,1,384,128,128]{4,3,2,1,0:T(8,128)(2,1)S(1)} copy-done((bf16[1,1,384,128,128]{4,3,2,1,0:T(8,128)(2,1)S(1)}, bf16[1,1,384,128,128]{4,3,2,1,0:T(8,128)(2,1)}, u32[]{:S(2)}) %copy-start) | copy-done | bytes 12582936
  5.2 0.0 copy-start.2
  5.2 0.7 %copy-done.2 = s32[128,16]{0,1:T(8,128)S(1)} copy-done((s32[128,16]{0,1:T(8,128)S(1)}, s32[128,16]{0,1:T(8,128)}, u32[]{:S(2)}) %copy-start.2) | copy-done | bytes 8216
  5.9 0.0 copy-start.4
  5.9 0.7 %copy-done.4 = s32[1,1,384]{2,1,0:T(1,128)S(1)} copy-done((s32[1,1,384]{2,1,0:T(1,128)S(1)}, s32[1,1,384]{2,1,0:T(1,128)}, u32[]{:S(2)}) %copy-start.4) | copy-done | bytes 1560
  6.6 0.0 copy-start.5
  6.6 0.7 %copy-done.5 = s32[1,1,384]{2,1,0:T(1,128)S(1)} copy-done((s32[1,1,384]{2,1,0:T(1,128)S(1)}, s32[1,1,384]{2,1,0:T(1,128)}, u32[]{:S(2)}) %copy-start.5) | copy-done | bytes 1560
  7.3 8.0 %sum_tiles.1 = (bf16[512,128]{1,0:T(8,128)(2,1)S(1)}, bf16[512,128]{1,0:T(8,128)(2,1)S(1)}, f32[128,128]{1,0:T(8,128)S(1)}) custom-call(bf16[1,1,384,128,128]{4,3,2,1,0:T(8,128)(2,1)S(1)} %copy-done, s32[1,1,384]{2,1,0:T(1,128)S(1)} %copy-done.4, s32[1,1,384]{2,1,0:T(1,128)S(1)} %copy-done.5, s32[1,1]{1,0:T(1,128)S(6)} %copy.8.count_ref, s32[16,128]{1,0:T(8,128)S(1)} %bitcast.2), custom_call_target="tpu_custom_call" | custom-call | flops 6291456 | bytes 12582912 | tf_op jit(solution)/shard_map/sum_tiles/pallas_call | solution.py:201
  15.3 0.1 collective-permute-start.7
  15.4 1.5 %scale.1.refs_0_ = bf16[128,128]{1,0:T(8,128)(2,1)} custom-call(f32[128,128]{1,0:T(8,128)} %prior_ref.1, s32[1,128]{1,0:T(1,128)} %bitcast.3), custom_call_target="tpu_custom_call" | custom-call | flops 16384 | bytes 98304 | tf_op jit(solution)/shard_map/scale/pallas_call | solution.py:178
  16.9 3.2 %collective-permute-start.6 = (bf16[128,128]{1,0:T(8,128)(2,1)}, bf16[128,128]{1,0:T(8,128)(2,1)S(1)}, u32[]{:S(2)}, u32[]{:S(2)}) collective-permute-start(bf16[128,128]{1,0:T(8,128)(2,1)} %scale.1.refs_0_), channel_id=1, source_target_pairs={{28,0},{24,4},{20,8},{16,12},{12,16},{8,20},{4,24},{0,28},{29,1},{... | collective-permute-start | bytes 98312 | tf_op jit(solution)/shard_map/ppermute | solution.py:44
  20.1 0.9 %collective-permute-start.5 = (bf16[128,128]{1,0:T(8,128)(2,1)}, bf16[128,128]{1,0:T(8,128)(2,1)S(1)}, u32[]{:S(2)}, u32[]{:S(2)}) collective-permute-start(bf16[128,128]{1,0:T(8,128)(2,1)} %scale.1.refs_0_), channel_id=1, source_target_pairs={{24,0},{28,4},{16,8},{20,12},{8,16},{12,20},{0,24},{4,28},{25,1},{... | collective-permute-start | bytes 98312 | tf_op jit(solution)/shard_map/ppermute | solution.py:44
  20.9 0.0 collective-permute-start.4
  20.9 0.5 %collective-permute-start.3 = (bf16[128,128]{1,0:T(8,128)(2,1)}, bf16[128,128]{1,0:T(8,128)(2,1)S(1)}, u32[]{:S(2)}, u32[]{:S(2)}) collective-permute-start(bf16[128,128]{1,0:T(8,128)(2,1)} %scale.1.refs_0_), channel_id=1, source_target_pairs={{16,0},{20,4},{24,8},{28,12},{0,16},{4,20},{8,24},{12,28},{17,1},{... | collective-permute-start | bytes 98312 | tf_op jit(solution)/shard_map/ppermute | solution.py:44
  21.4 0.6 %collective-permute-done.6.refs_7_ = bf16[128,128]{1,0:T(8,128)(2,1)S(1)} collective-permute-done((bf16[128,128]{1,0:T(8,128)(2,1)}, bf16[128,128]{1,0:T(8,128)(2,1)S(1)}, u32[]{:S(2)}, u32[]{:S(2)}) %collective-permute-start.6) | collective-permute-done | bytes 32800 | tf_op jit(solution)/shard_map/ppermute | solution.py:44
  22.0 3.1 %collective-permute-start.2 = (bf16[128,128]{1,0:T(8,128)(2,1)}, bf16[128,128]{1,0:T(8,128)(2,1)S(1)}, u32[]{:S(2)}, u32[]{:S(2)}) collective-permute-start(bf16[128,128]{1,0:T(8,128)(2,1)} %scale.1.refs_0_), channel_id=1, source_target_pairs={{12,0},{8,4},{4,8},{0,12},{28,16},{24,20},{20,24},{16,28},{13,1},{... | collective-permute-start | bytes 98312 | tf_op jit(solution)/shard_map/ppermute | solution.py:44
  25.1 0.0 collective-permute-done.5.refs_6_
  25.1 0.7 %collective-permute-start.1 = (bf16[128,128]{1,0:T(8,128)(2,1)}, bf16[128,128]{1,0:T(8,128)(2,1)S(1)}, u32[]{:S(2)}, u32[]{:S(2)}) collective-permute-start(bf16[128,128]{1,0:T(8,128)(2,1)} %scale.1.refs_0_), channel_id=1, source_target_pairs={{8,0},{12,4},{0,8},{4,12},{24,16},{28,20},{16,24},{20,28},{9,1},{1... | collective-permute-start | bytes 98312 | tf_op jit(solution)/shard_map/ppermute | solution.py:44
  25.8 0.0 collective-permute-done.4.refs_5_
  25.8 0.0 collective-permute-start
  25.8 0.0 collective-permute-done.3.refs_4_
  25.8 1.4 %collective-permute-done.2.refs_3_ = bf16[128,128]{1,0:T(8,128)(2,1)S(1)} collective-permute-done((bf16[128,128]{1,0:T(8,128)(2,1)}, bf16[128,128]{1,0:T(8,128)(2,1)S(1)}, u32[]{:S(2)}, u32[]{:S(2)}) %collective-permute-start.2) | collective-permute-done | bytes 32800 | tf_op jit(solution)/shard_map/ppermute | solution.py:44
  27.2 2.0 %collective-permute-done.1.refs_2_ = bf16[128,128]{1,0:T(8,128)(2,1)S(1)} collective-permute-done((bf16[128,128]{1,0:T(8,128)(2,1)}, bf16[128,128]{1,0:T(8,128)(2,1)S(1)}, u32[]{:S(2)}, u32[]{:S(2)}) %collective-permute-start.1) | collective-permute-done | bytes 32800 | tf_op jit(solution)/shard_map/ppermute | solution.py:44
  29.2 0.7 %collective-permute-done.refs_1_ = bf16[128,128]{1,0:T(8,128)(2,1)S(1)} collective-permute-done((bf16[128,128]{1,0:T(8,128)(2,1)}, bf16[128,128]{1,0:T(8,128)(2,1)S(1)}, u32[]{:S(2)}, u32[]{:S(2)}) %collective-permute-start) | collective-permute-done | bytes 32800 | tf_op jit(solution)/shard_map/ppermute | solution.py:44
  29.9 0.0 collective-permute-done.7.refs_9_
  29.9 0.0 copy-done.3
  29.9 0.0 copy-start.1
  29.9 0.8 %copy-done.1 = bf16[128,128]{1,0:T(8,128)(2,1)S(1)} copy-done((bf16[128,128]{1,0:T(8,128)(2,1)S(1)}, bf16[128,128]{1,0:T(8,128)(2,1)}, u32[]{:S(2)}) %copy-start.1) | copy-done | bytes 32792
  30.7 0.2 first_round.1.refs_0_
  30.9 0.1 collective-permute-start.14
  31.0 1.2 %collective-permute-start.13 = (bf16[128,128]{1,0:T(8,128)(2,1)S(1)}, bf16[128,128]{1,0:T(8,128)(2,1)S(1)}, u32[]{:S(2)}, u32[]{:S(2)}) collective-permute-start(bf16[128,128]{1,0:T(8,128)(2,1)S(1)} %first_round.1.refs_0_), channel_id=1, source_target_pairs={{24,0},{28,4},{16,8},{20,12},{8,16},{12,20},{0,24},{4,28},{25,1},{... | collective-permute-start | bytes 98312 | tf_op jit(solution)/shard_map/ppermute | solution.py:44
  32.2 1.3 %collective-permute-start.12 = (bf16[128,128]{1,0:T(8,128)(2,1)S(1)}, bf16[128,128]{1,0:T(8,128)(2,1)S(1)}, u32[]{:S(2)}, u32[]{:S(2)}) collective-permute-start(bf16[128,128]{1,0:T(8,128)(2,1)S(1)} %first_round.1.refs_0_), channel_id=1, source_target_pairs={{20,0},{16,4},{28,8},{24,12},{4,16},{0,20},{12,24},{8,28},{21,1},{... | collective-permute-start | bytes 98312 | tf_op jit(solution)/shard_map/ppermute | solution.py:44
  33.5 0.8 %collective-permute-start.11 = (bf16[128,128]{1,0:T(8,128)(2,1)S(1)}, bf16[128,128]{1,0:T(8,128)(2,1)S(1)}, u32[]{:S(2)}, u32[]{:S(2)}) collective-permute-start(bf16[128,128]{1,0:T(8,128)(2,1)S(1)} %first_round.1.refs_0_), channel_id=1, source_target_pairs={{16,0},{20,4},{24,8},{28,12},{0,16},{4,20},{8,24},{12,28},{17,1},{... | collective-permute-start | bytes 98312 | tf_op jit(solution)/shard_map/ppermute | solution.py:44
  34.3 0.8 %collective-permute-start.10 = (bf16[128,128]{1,0:T(8,128)(2,1)S(1)}, bf16[128,128]{1,0:T(8,128)(2,1)S(1)}, u32[]{:S(2)}, u32[]{:S(2)}) collective-permute-start(bf16[128,128]{1,0:T(8,128)(2,1)S(1)} %first_round.1.refs_0_), channel_id=1, source_target_pairs={{12,0},{8,4},{4,8},{0,12},{28,16},{24,20},{20,24},{16,28},{13,1},{... | collective-permute-start | bytes 98312 | tf_op jit(solution)/shard_map/ppermute | solution.py:44
  35.1 0.1 collective-permute-done.14.refs_7_
  35.2 1.3 %collective-permute-start.9 = (bf16[128,128]{1,0:T(8,128)(2,1)S(1)}, bf16[128,128]{1,0:T(8,128)(2,1)S(1)}, u32[]{:S(2)}, u32[]{:S(2)}) collective-permute-start(bf16[128,128]{1,0:T(8,128)(2,1)S(1)} %first_round.1.refs_0_), channel_id=1, source_target_pairs={{8,0},{12,4},{0,8},{4,12},{24,16},{28,20},{16,24},{20,28},{9,1},{1... | collective-permute-start | bytes 98312 | tf_op jit(solution)/shard_map/ppermute | solution.py:44
  36.5 0.0 collective-permute-done.13.refs_6_
  36.5 1.3 %collective-permute-start.8 = (bf16[128,128]{1,0:T(8,128)(2,1)S(1)}, bf16[128,128]{1,0:T(8,128)(2,1)S(1)}, u32[]{:S(2)}, u32[]{:S(2)}) collective-permute-start(bf16[128,128]{1,0:T(8,128)(2,1)S(1)} %first_round.1.refs_0_), channel_id=1, source_target_pairs={{4,0},{0,4},{12,8},{8,12},{20,16},{16,20},{28,24},{24,28},{5,1},{1... | collective-permute-start | bytes 98312 | tf_op jit(solution)/shard_map/ppermute | solution.py:44
  37.8 0.0 collective-permute-done.12.refs_5_
  37.8 0.0 collective-permute-done.11.refs_4_
  37.8 1.5 %collective-permute-done.10.refs_3_ = bf16[128,128]{1,0:T(8,128)(2,1)S(1)} collective-permute-done((bf16[128,128]{1,0:T(8,128)(2,1)S(1)}, bf16[128,128]{1,0:T(8,128)(2,1)S(1)}, u32[]{:S(2)}, u32[]{:S(2)}) %collective-permute-start.10) | collective-permute-done | bytes 32800 | tf_op jit(solution)/shard_map/ppermute | solution.py:44
  39.3 0.2 collective-permute-done.9.refs_2_
  39.5 1.0 %collective-permute-done.8.refs_1_ = bf16[128,128]{1,0:T(8,128)(2,1)S(1)} collective-permute-done((bf16[128,128]{1,0:T(8,128)(2,1)S(1)}, bf16[128,128]{1,0:T(8,128)(2,1)S(1)}, u32[]{:S(2)}, u32[]{:S(2)}) %collective-permute-start.8) | collective-permute-done | bytes 32800 | tf_op jit(solution)/shard_map/ppermute | solution.py:44
  40.4 0.9 %last_round.1 = f32[128,128]{1,0:T(8,128)} custom-call(bf16[128,128]{1,0:T(8,128)(2,1)S(1)} %first_round.1.refs_0_, bf16[128,128]{1,0:T(8,128)(2,1)S(1)} %collective-permute-done.8.refs_1_, bf16[128,128]{1,0:T(8,128)(2,1)S(1)} %collective-permute-done.9.refs_2_, bf16[128,128]{1,0:T(8,128)(2,1)S(1)} %collective-permute-done.10.refs_3_, ...), custom_call_target="tpu_custom_call" | custom-call | flops 33554432 | bytes 524288 | tf_op jit(solution)/shard_map/last_round/pallas_call | solution.py:226
Async XLA Ops:
  0.0 29.9 %copy-start.3 = (s32[128]{0:T(128)S(1)}, s32[128]{0:T(128)}, u32[]{:S(2)}) copy-start(s32[128]{0:T(128)} %param.11) | copy-start | bytes 1540
  0.7 4.6 %copy-start = (bf16[1,1,384,128,128]{4,3,2,1,0:T(8,128)(2,1)S(1)}, bf16[1,1,384,128,128]{4,3,2,1,0:T(8,128)(2,1)}, u32[]{:S(2)}) copy-start(bf16[1,1,384,128,128]{4,3,2,1,0:T(8,128)(2,1)} %tiles_ref.1) | copy-start | bytes 37748740
  5.2 0.7 %copy-start.2 = (s32[128,16]{0,1:T(8,128)S(1)}, s32[128,16]{0,1:T(8,128)}, u32[]{:S(2)}) copy-start(s32[128,16]{0,1:T(8,128)} %param.12) | copy-start | bytes 24580
  5.9 0.7 %copy-start.4 = (s32[1,1,384]{2,1,0:T(1,128)S(1)}, s32[1,1,384]{2,1,0:T(1,128)}, u32[]{:S(2)}) copy-start(s32[1,1,384]{2,1,0:T(1,128)} %out_ref.1) | copy-start | bytes 4612
  6.6 0.7 %copy-start.5 = (s32[1,1,384]{2,1,0:T(1,128)S(1)}, s32[1,1,384]{2,1,0:T(1,128)}, u32[]{:S(2)}) copy-start(s32[1,1,384]{2,1,0:T(1,128)} %in_ref.1) | copy-start | bytes 4612
  15.3 14.6 %collective-permute-start.7 = (bf16[512,128]{1,0:T(8,128)(2,1)S(1)}, bf16[512,128]{1,0:T(8,128)(2,1)S(1)}, u32[]{:S(2)}, u32[]{:S(2)}) collective-permute-start(bf16[512,128]{1,0:T(8,128)(2,1)S(1)} %get-tuple-element.9), channel_id=1, source_target_pairs={{16,0},{0,16},{17,1},{1,17},{18,2},{2,18},{19,3},{3,19},{20,4},{4,... | collective-permute-start | bytes 393224 | tf_op jit(solution)/shard_map/ppermute | solution.py:44
  16.9 5.1 %collective-permute-start.6 = (bf16[128,128]{1,0:T(8,128)(2,1)}, bf16[128,128]{1,0:T(8,128)(2,1)S(1)}, u32[]{:S(2)}, u32[]{:S(2)}) collective-permute-start(bf16[128,128]{1,0:T(8,128)(2,1)} %scale.1.refs_0_), channel_id=1, source_target_pairs={{28,0},{24,4},{20,8},{16,12},{12,16},{8,20},{4,24},{0,28},{29,1},{... | collective-permute-start | bytes 98312 | tf_op jit(solution)/shard_map/ppermute | solution.py:44
  20.1 5.0 %collective-permute-start.5 = (bf16[128,128]{1,0:T(8,128)(2,1)}, bf16[128,128]{1,0:T(8,128)(2,1)S(1)}, u32[]{:S(2)}, u32[]{:S(2)}) collective-permute-start(bf16[128,128]{1,0:T(8,128)(2,1)} %scale.1.refs_0_), channel_id=1, source_target_pairs={{24,0},{28,4},{16,8},{20,12},{8,16},{12,20},{0,24},{4,28},{25,1},{... | collective-permute-start | bytes 98312 | tf_op jit(solution)/shard_map/ppermute | solution.py:44
  20.9 4.8 %collective-permute-start.4 = (bf16[128,128]{1,0:T(8,128)(2,1)}, bf16[128,128]{1,0:T(8,128)(2,1)S(1)}, u32[]{:S(2)}, u32[]{:S(2)}) collective-permute-start(bf16[128,128]{1,0:T(8,128)(2,1)} %scale.1.refs_0_), channel_id=1, source_target_pairs={{20,0},{16,4},{28,8},{24,12},{4,16},{0,20},{12,24},{8,28},{21,1},{... | collective-permute-start | bytes 98312 | tf_op jit(solution)/shard_map/ppermute | solution.py:44
  20.9 4.8 %collective-permute-start.3 = (bf16[128,128]{1,0:T(8,128)(2,1)}, bf16[128,128]{1,0:T(8,128)(2,1)S(1)}, u32[]{:S(2)}, u32[]{:S(2)}) collective-permute-start(bf16[128,128]{1,0:T(8,128)(2,1)} %scale.1.refs_0_), channel_id=1, source_target_pairs={{16,0},{20,4},{24,8},{28,12},{0,16},{4,20},{8,24},{12,28},{17,1},{... | collective-permute-start | bytes 98312 | tf_op jit(solution)/shard_map/ppermute | solution.py:44
  22.0 5.2 %collective-permute-start.2 = (bf16[128,128]{1,0:T(8,128)(2,1)}, bf16[128,128]{1,0:T(8,128)(2,1)S(1)}, u32[]{:S(2)}, u32[]{:S(2)}) collective-permute-start(bf16[128,128]{1,0:T(8,128)(2,1)} %scale.1.refs_0_), channel_id=1, source_target_pairs={{12,0},{8,4},{4,8},{0,12},{28,16},{24,20},{20,24},{16,28},{13,1},{... | collective-permute-start | bytes 98312 | tf_op jit(solution)/shard_map/ppermute | solution.py:44
  25.1 4.1 %collective-permute-start.1 = (bf16[128,128]{1,0:T(8,128)(2,1)}, bf16[128,128]{1,0:T(8,128)(2,1)S(1)}, u32[]{:S(2)}, u32[]{:S(2)}) collective-permute-start(bf16[128,128]{1,0:T(8,128)(2,1)} %scale.1.refs_0_), channel_id=1, source_target_pairs={{8,0},{12,4},{0,8},{4,12},{24,16},{28,20},{16,24},{20,28},{9,1},{1... | collective-permute-start | bytes 98312 | tf_op jit(solution)/shard_map/ppermute | solution.py:44
  25.8 4.1 %collective-permute-start = (bf16[128,128]{1,0:T(8,128)(2,1)}, bf16[128,128]{1,0:T(8,128)(2,1)S(1)}, u32[]{:S(2)}, u32[]{:S(2)}) collective-permute-start(bf16[128,128]{1,0:T(8,128)(2,1)} %scale.1.refs_0_), channel_id=1, source_target_pairs={{4,0},{0,4},{12,8},{8,12},{20,16},{16,20},{28,24},{24,28},{5,1},{1... | collective-permute-start | bytes 98312 | tf_op jit(solution)/shard_map/ppermute | solution.py:44
  29.9 0.8 %copy-start.1 = (bf16[128,128]{1,0:T(8,128)(2,1)S(1)}, bf16[128,128]{1,0:T(8,128)(2,1)}, u32[]{:S(2)}) copy-start(bf16[128,128]{1,0:T(8,128)(2,1)} %scale.1.refs_0_) | copy-start | bytes 98308
  30.9 4.3 %collective-permute-start.14 = (bf16[128,128]{1,0:T(8,128)(2,1)S(1)}, bf16[128,128]{1,0:T(8,128)(2,1)S(1)}, u32[]{:S(2)}, u32[]{:S(2)}) collective-permute-start(bf16[128,128]{1,0:T(8,128)(2,1)S(1)} %first_round.1.refs_0_), channel_id=1, source_target_pairs={{28,0},{24,4},{20,8},{16,12},{12,16},{8,20},{4,24},{0,28},{29,1},{... | collective-permute-start | bytes 98312 | tf_op jit(solution)/shard_map/ppermute | solution.py:44
  31.0 5.5 %collective-permute-start.13 = (bf16[128,128]{1,0:T(8,128)(2,1)S(1)}, bf16[128,128]{1,0:T(8,128)(2,1)S(1)}, u32[]{:S(2)}, u32[]{:S(2)}) collective-permute-start(bf16[128,128]{1,0:T(8,128)(2,1)S(1)} %first_round.1.refs_0_), channel_id=1, source_target_pairs={{24,0},{28,4},{16,8},{20,12},{8,16},{12,20},{0,24},{4,28},{25,1},{... | collective-permute-start | bytes 98312 | tf_op jit(solution)/shard_map/ppermute | solution.py:44
  32.2 5.6 %collective-permute-start.12 = (bf16[128,128]{1,0:T(8,128)(2,1)S(1)}, bf16[128,128]{1,0:T(8,128)(2,1)S(1)}, u32[]{:S(2)}, u32[]{:S(2)}) collective-permute-start(bf16[128,128]{1,0:T(8,128)(2,1)S(1)} %first_round.1.refs_0_), channel_id=1, source_target_pairs={{20,0},{16,4},{28,8},{24,12},{4,16},{0,20},{12,24},{8,28},{21,1},{... | collective-permute-start | bytes 98312 | tf_op jit(solution)/shard_map/ppermute | solution.py:44
  33.5 4.3 %collective-permute-start.11 = (bf16[128,128]{1,0:T(8,128)(2,1)S(1)}, bf16[128,128]{1,0:T(8,128)(2,1)S(1)}, u32[]{:S(2)}, u32[]{:S(2)}) collective-permute-start(bf16[128,128]{1,0:T(8,128)(2,1)S(1)} %first_round.1.refs_0_), channel_id=1, source_target_pairs={{16,0},{20,4},{24,8},{28,12},{0,16},{4,20},{8,24},{12,28},{17,1},{... | collective-permute-start | bytes 98312 | tf_op jit(solution)/shard_map/ppermute | solution.py:44
  34.3 5.0 %collective-permute-start.10 = (bf16[128,128]{1,0:T(8,128)(2,1)S(1)}, bf16[128,128]{1,0:T(8,128)(2,1)S(1)}, u32[]{:S(2)}, u32[]{:S(2)}) collective-permute-start(bf16[128,128]{1,0:T(8,128)(2,1)S(1)} %first_round.1.refs_0_), channel_id=1, source_target_pairs={{12,0},{8,4},{4,8},{0,12},{28,16},{24,20},{20,24},{16,28},{13,1},{... | collective-permute-start | bytes 98312 | tf_op jit(solution)/shard_map/ppermute | solution.py:44
  35.2 4.2 %collective-permute-start.9 = (bf16[128,128]{1,0:T(8,128)(2,1)S(1)}, bf16[128,128]{1,0:T(8,128)(2,1)S(1)}, u32[]{:S(2)}, u32[]{:S(2)}) collective-permute-start(bf16[128,128]{1,0:T(8,128)(2,1)S(1)} %first_round.1.refs_0_), channel_id=1, source_target_pairs={{8,0},{12,4},{0,8},{4,12},{24,16},{28,20},{16,24},{20,28},{9,1},{1... | collective-permute-start | bytes 98312 | tf_op jit(solution)/shard_map/ppermute | solution.py:44
  36.5 3.9 %collective-permute-start.8 = (bf16[128,128]{1,0:T(8,128)(2,1)S(1)}, bf16[128,128]{1,0:T(8,128)(2,1)S(1)}, u32[]{:S(2)}, u32[]{:S(2)}) collective-permute-start(bf16[128,128]{1,0:T(8,128)(2,1)S(1)} %first_round.1.refs_0_), channel_id=1, source_target_pairs={{4,0},{0,4},{12,8},{8,12},{20,16},{16,20},{28,24},{24,28},{5,1},{1... | collective-permute-start | bytes 98312 | tf_op jit(solution)/shard_map/ppermute | solution.py:44

commit v2 on v1

--- a/solution.py
+++ b/solution.py
@@ -14,9 +14,10 @@
 damping = 0.85
 
 VMEM = pl.BlockSpec(memory_space=pltpu.VMEM)
-SMEM = pl.BlockSpec(memory_space=pltpu.SMEM)
-HBM = pl.BlockSpec(memory_space=pl.ANY)
-
+HBM = pl.BlockSpec(memory_space=pltpu.HBM)
+
+TILES_VMEM = 50 * 1024 * 1024
+SMALL_VMEM = 8 * 1024 * 1024
 UNROLL = 4
 FIELD_BITS = 8
 FIELD_MASK = (1 << FIELD_BITS) - 1
@@ -44,13 +45,27 @@
     return lax.ppermute(value, axes, pairs)
 
 
-def scale_kernel(prior_ref, degree_ref, scaled_ref):
-    scaled_ref[...] = (prior_ref[...] / degree_ref[...].astype(jnp.float32)).astype(jnp.bfloat16)
-
-
-def sum_kernel(rows, cols, owned_blocks, tiles_ref, out_ref, in_ref, count_ref, seeds_ref, *rest):
+def in_hbm(*arrays):
+    return [pltpu.with_memory_space_constraint(array, pltpu.HBM) for array in arrays]
+
+
+def scale_kernel(prior_hbm, degree_hbm, scaled_ref, prior_ref, degree_ref, arrived):
+    copies = [
+        pltpu.make_async_copy(source, place, arrived.at[index])
+        for index, (source, place) in enumerate(((prior_hbm, prior_ref), (degree_hbm, degree_ref)))
+    ]
+    for copy in copies:
+        copy.start()
+    for copy in copies:
+        copy.wait()
+    scaled = (prior_ref[...] / degree_ref[...].astype(jnp.float32)).astype(jnp.bfloat16)
+    for place in range(scaled_ref.shape[0]):
+        scaled_ref[place] = scaled
+
+
+def sum_kernel(rows, cols, owned_blocks, scaled_ref, count_ref, tiles_ref, out_hbm, in_hbm, seeds_hbm, *rest):
     weight_refs, restart_ref = rest[:rows], rest[rows]
-    buffer, total, listed, arrived = rest[rows + 1:]
+    buffer, total, listed, out_ref, in_ref, seeds_ref, arrived, small = rest[rows + 1:]
     in_blocks, out_blocks = cols * owned_blocks, rows * owned_blocks
     slots, edge = tiles_ref.shape[2], tiles_ref.shape[3]
     group = slots // arrived.shape[0]
@@ -61,12 +76,22 @@
         span = pl.ds(index * group, group)
         return pltpu.make_async_copy(tiles_ref.at[0, 0, span], buffer.at[span], arrived.at[index])
 
+    copies = [
+        pltpu.make_async_copy(source, place, small.at[index])
+        for index, (source, place) in enumerate(
+            ((out_hbm, out_ref), (in_hbm, in_ref), (seeds_hbm, seeds_ref))
+        )
+    ]
+    for copy in copies:
+        copy.start()
     for index in range(slots // group):
         arrival(index).start()
 
     buffer[slots] = jnp.zeros((edge, edge), jnp.bfloat16)
     total[...] = jnp.zeros(total.shape, jnp.float32)
 
+    for copy in copies:
+        copy.wait()
     seed_total, sets = seeds_ref.shape
     owned = owned_blocks * edge
     vertex = lax.broadcasted_iota(jnp.int32, (owned, sets), 0) + (row * cols + col) * owned
@@ -142,27 +167,23 @@
                 ] = total[pair].astype(jnp.bfloat16)
 
 
-def round_kernel(rows, cols, relative, last, *refs):
-    block_total = rows * cols if relative else 1
-    blocks, weights = refs[:block_total], refs[block_total:block_total + rows]
-    restart_ref, degree_ref, result_ref = refs[block_total + rows:]
+def round_kernel(rows, cols, last, blocks_ref, *refs):
+    weights, (restart_ref, degree_ref, result_ref) = refs[:rows], refs[rows:]
     row, col = lax.axis_index("row"), lax.axis_index("col")
     owned = restart_ref.shape[1]
     incoming = jnp.zeros(restart_ref.shape, jnp.float32)
     for row_offset in range(rows):
-        for col_offset in range(cols):
-            column = partner(col, col_offset, cols)
-            if relative:
-                scaled = blocks[row_offset * cols + col_offset][...]
-            else:
-                scaled = blocks[0][partner(row, row_offset, rows) * cols + column]
-            weight = weights[row_offset][pl.ds(pl.multiple_of(column * owned, owned), owned), :]
-            incoming += jnp.dot(scaled, weight, preferred_element_type=jnp.float32)
+        first = partner(row, row_offset, rows) * cols
+        for column in range(cols):
+            weight = weights[row_offset][column * owned:(column + 1) * owned, :]
+            incoming += jnp.dot(blocks_ref[first + column], weight, preferred_element_type=jnp.float32)
     risk = restart_ref[...] + damping * incoming
     if last:
         result_ref[...] = risk
     else:
-        result_ref[...] = (risk / degree_ref[...].astype(jnp.float32)).astype(jnp.bfloat16)
+        scaled = (risk / degree_ref[...].astype(jnp.float32)).astype(jnp.bfloat16)
+        for place in range(result_ref.shape[0]):
+            result_ref[place] = scaled
 
 
 def local(tiles, tile_out, tile_in, tile_count, out_degree, seed_ids, prior):
@@ -172,29 +193,26 @@
     owned_blocks = owned // edge
     in_blocks, out_blocks = cols * owned_blocks, rows * owned_blocks
     group = math.gcd(slots, 64)
-    relative = rows * cols <= 8
+    everyone = rows * cols
     degree = out_degree.reshape(1, owned)
 
     scaled = pl.pallas_call(
         scale_kernel,
-        out_shape=jax.ShapeDtypeStruct((sets, owned), jnp.bfloat16),
-        in_specs=[VMEM, VMEM],
+        out_shape=jax.ShapeDtypeStruct((everyone, sets, owned), jnp.bfloat16),
+        in_specs=[HBM, HBM],
         out_specs=VMEM,
+        scratch_shapes=[
+            pltpu.VMEM((sets, owned), jnp.float32),
+            pltpu.VMEM((1, owned), jnp.int32),
+            pltpu.SemaphoreType.DMA((2,)),
+        ],
+        compiler_params=pltpu.CompilerParams(vmem_limit_bytes=SMALL_VMEM),
         cost_estimate=pl.CostEstimate(flops=sets * owned, bytes_accessed=6 * sets * owned, transcendentals=0),
         name="scale",
-    )(prior, degree)
-
-    def spread(value):
-        if not relative:
-            return [lax.all_gather(value, ("row", "col"), axis=0)]
-        blocks = []
-        for row_offset in range(rows):
-            for col_offset in range(cols):
-                if row_offset or col_offset:
-                    blocks.append(send_to(value, ("row", "col"), (rows, cols), (row_offset, col_offset)))
-                else:
-                    blocks.append(value)
-        return blocks
+    )(*in_hbm(prior, degree))
+
+    def spread(copies):
+        return lax.all_to_all(copies, ("row", "col"), split_axis=0, concat_axis=0, tiled=True)
 
     blocks = spread(scaled)
 
@@ -202,20 +220,24 @@
         functools.partial(sum_kernel, rows, cols, owned_blocks),
         out_shape=[jax.ShapeDtypeStruct((in_blocks * edge, owned), jnp.bfloat16)] * rows
         + [jax.ShapeDtypeStruct((sets, owned), jnp.float32)],
-        in_specs=[HBM, SMEM, SMEM, SMEM, VMEM],
+        in_specs=[pl.BlockSpec(memory_space=pl.ANY), pl.BlockSpec(memory_space=pltpu.SMEM)] + [HBM] * 4,
         out_specs=[VMEM] * (rows + 1),
         scratch_shapes=[
             pltpu.VMEM((slots + 1, edge, edge), jnp.bfloat16),
             pltpu.VMEM((out_blocks * in_blocks, edge, edge), jnp.float32),
             pltpu.SMEM((in_blocks * (group + UNROLL),), jnp.int32),
+            pltpu.SMEM(tile_out.shape, jnp.int32),
+            pltpu.SMEM(tile_in.shape, jnp.int32),
+            pltpu.VMEM((seed_ids.shape[1], sets), jnp.int32),
             pltpu.SemaphoreType.DMA((slots // group,)),
+            pltpu.SemaphoreType.DMA((3,)),
         ],
-        compiler_params=pltpu.CompilerParams(vmem_limit_bytes=32 * 1024 * 1024),
+        compiler_params=pltpu.CompilerParams(vmem_limit_bytes=TILES_VMEM),
         cost_estimate=pl.CostEstimate(
             flops=slots * edge * edge, bytes_accessed=2 * slots * edge * edge, transcendentals=0
         ),
         name="sum_tiles",
-    )(tiles, tile_out, tile_in, tile_count, seed_ids.T)
+    )(scaled, tile_count, *in_hbm(tiles, tile_out, tile_in, seed_ids.T))
 
     weights = [weights[0]] + [
         send_to(weights[offset], ("row",), (rows,), (offset,)) for offset in range(1, rows)
@@ -223,19 +245,20 @@
 
     for round_index in range(ITERATIONS):
         last = round_index == ITERATIONS - 1
+        shape = (sets, owned) if last else (everyone, sets, owned)
         value = pl.pallas_call(
-            functools.partial(round_kernel, rows, cols, relative, last),
-            out_shape=jax.ShapeDtypeStruct((sets, owned), jnp.float32 if last else jnp.bfloat16),
-            in_specs=[VMEM] * (len(blocks) + rows + 2),
+            functools.partial(round_kernel, rows, cols, last),
+            out_shape=jax.ShapeDtypeStruct(shape, jnp.float32 if last else jnp.bfloat16),
+            in_specs=[VMEM] * (rows + 3),
             out_specs=VMEM,
-            compiler_params=pltpu.CompilerParams(vmem_limit_bytes=32 * 1024 * 1024),
+            compiler_params=pltpu.CompilerParams(vmem_limit_bytes=SMALL_VMEM),
             cost_estimate=pl.CostEstimate(
-                flops=2 * sets * rows * cols * owned * owned,
-                bytes_accessed=2 * rows * cols * owned * (sets + owned),
+                flops=2 * sets * everyone * owned * owned,
+                bytes_accessed=2 * everyone * owned * (sets + owned),
                 transcendentals=0,
             ),
             name="last_round" if last else "first_round",
-        )(*blocks, *weights, restart, degree)
+        )(blocks, *weights, restart, degree)
         if not last:
             blocks = spread(value)
     return value

time: 41.2 us -> 31.9 us (0.77)
  blocking collectives: 0 us -> 12.1 us
  starting transfers between devices: 15.2 us -> 5.43 us
  local copies, waits for them, and re-layouts: 7.39 us -> 0.01 us
  waiting for transfers between devices: 7.47 us -> 1.16 us
  Pallas kernels: 10.6 us -> 12.3 us
    ppermute x15 -> x1, starting transfers between devices: 15.2 us -> 0.25 us  [send_to(): return lax.ppermute(value, axes, pairs)]
    all_to_all x0 -> x1, blocking collectives: none -> 12.1 us  [spread(): lax.all_to_all(copies, ('row', 'col'), split_axis=0, concat_axis=0, tiled...]
    unnamed x12 -> x2, local copies, waits for them, and re-layouts: 7.39 us -> 0.01 us
    ppermute x15 -> x1, waiting for transfers between devices: 7.47 us -> 1.16 us  [send_to(): return lax.ppermute(value, axes, pairs)]
    all_to_all x0 -> x1, starting transfers between devices: none -> 5.18 us  [spread(): lax.all_to_all(copies, ('row', 'col'), split_axis=0, concat_axis=0, tiled...]
    pallas_call x1, Pallas kernels: 8 us -> 9.65 us  [local(): pl.pallas_call(functools.partial(sum_kernel, rows, cols, owned_blocks), o...]
  transfers between devices with their start and end apart: 15 -> 2, of which waited for: 8 -> 1; matrix products, arithmetic and copies ran while one was open for 0% -> 0% of each run, Pallas kernels for 4% -> 31%
where the time goes in v2:
time: 31.9 us; the launch traced here: 31.6 us
  Pallas kernels  12.3 us (39%)
  blocking collectives  12.1 us (38%)
  starting transfers between devices  5.43 us (17%)
  waiting for transfers between devices  1.16 us (4%)
  between operations  0.68 us (2%)
    all_to_all x1, blocking collectives, spread(): lax.all_to_all(copies, ('row', 'col'), split_axis=0, concat_axis=0, tiled...  12.1 us
    pallas_call x1, Pallas kernels, local(): pl.pallas_call(functools.partial(sum_kernel, rows, cols, owned_blocks), o...  9.65 us
    all_to_all x1, starting transfers between devices, spread(): lax.all_to_all(copies, ('row', 'col'), split_axis=0, concat_axis=0, tiled...  5.18 us
    pallas_call x1, Pallas kernels, local(): pl.pallas_call(scale_kernel, out_shape=jax.ShapeDtypeStruct((everyone, se...  1.59 us
    ppermute x1, waiting for transfers between devices, send_to(): return lax.ppermute(value, axes, pairs)  1.16 us
    pallas_call x2, Pallas kernels, local(): pl.pallas_call(functools.partial(round_kernel, rows, cols, last), out_sha...  1.08 us
  transfers between devices with their start and end apart: 2, of which 1 were waited for; matrix products, arithmetic and copies ran while one was open for 0% of the time, Pallas kernels for 31%

profile of v2, /device:TPU:0, one launch (start us, length us, event | category | flops | bytes accessed | tf_op | source)
XLA Modules:
  0.0 31.6 jit_solution(14926537188063634367)
XLA Ops:
  0.0 0.0 copy-start
  0.0 1.6 %scale.1.scaled_ref = bf16[8,128,128]{2,1,0:T(8,128)(2,1)} custom-call(f32[128,128]{1,0:T(8,128)} %prior_hbm.1, s32[1,128]{1,0:T(1,128)} %bitcast.2), custom_call_target="tpu_custom_call" | custom-call | flops 16384 | bytes 98304 | tf_op jit(solution)/shard_map/scale/pallas_call | solution.py:199
  1.6 5.2 %all-to-all-start = ((bf16[8,128,128]{2,1,0:T(8,128)(2,1)}), bf16[8,128,128]{2,1,0:T(8,128)(2,1)S(1)}, u32[]{:S(2)}, u32[]{:S(2)}) async-start(bf16[8,128,128]{2,1,0:T(8,128)(2,1)} %scale.1.scaled_ref), calls=%async_computation | async-start | bytes 524288 | tf_op jit(solution)/shard_map/all_to_all | solution.py:215
  7.4 9.6 %sum_tiles.1 = (bf16[512,128]{1,0:T(8,128)(2,1)S(1)}, bf16[512,128]{1,0:T(8,128)(2,1)S(1)}, f32[128,128]{1,0:T(8,128)S(1)}) custom-call(bf16[8,128,128]{2,1,0:T(8,128)(2,1)} %scale.1.scaled_ref, s32[1,1]{1,0:T(1,128)S(6)} %copy.8.count_ref, bf16[1,1,384,128,128]{4,3,2,1,0:T(8,128)(2,1)} %tiles_ref.1, s32[1,1,384]{2,1,0:T(1,128)} %out_hbm.1, ...), custom_call_target="tpu_custom_call" | custom-call | flops 6291456 | bytes 12582912 | tf_op jit(solution)/shard_map/sum_tiles/pallas_call | solution.py:219
  17.1 0.3 collective-permute-start
  17.3 1.2 %collective-permute-done.refs_1_ = bf16[512,128]{1,0:T(8,128)(2,1)S(1)} collective-permute-done((bf16[512,128]{1,0:T(8,128)(2,1)S(1)}, bf16[512,128]{1,0:T(8,128)(2,1)S(1)}, u32[]{:S(2)}, u32[]{:S(2)}) %collective-permute-start) | collective-permute-done | bytes 131104 | tf_op jit(solution)/shard_map/ppermute | solution.py:45
  18.5 0.0 all-to-all-done.blocks_ref
  18.5 0.0 copy-done
  18.5 0.2 first_round.1
  18.7 12.1 %all_to_all.10.blocks_ref = bf16[8,128,128]{2,1,0:T(8,128)(2,1)S(1)} all-to-all(bf16[8,128,128]{2,1,0:T(8,128)(2,1)S(1)} %first_round.1), channel_id=1, replica_groups=mesh['row'=2,'col'=4,'seed'=4] {'row','col'}, dimensions={0} | all-to-all | bytes 524288 | tf_op jit(solution)/shard_map/all_to_all | solution.py:215
  30.8 0.9 %last_round.1 = f32[128,128]{1,0:T(8,128)} custom-call(bf16[8,128,128]{2,1,0:T(8,128)(2,1)S(1)} %all_to_all.10.blocks_ref, bf16[512,128]{1,0:T(8,128)(2,1)S(1)} %get-tuple-element.8.refs_0_, bf16[512,128]{1,0:T(8,128)(2,1)S(1)} %collective-permute-done.refs_1_, f32[128,128]{1,0:T(8,128)S(1)} %get-tuple-element.10.refs_2_, s32[1,128]{1,0:T(1,128)S(1)} %bitcast.4), custom_call_target="tpu_custom_call" | custom-call | flops 33554432 | bytes 524288 | tf_op jit(solution)/shard_map/last_round/pallas_call | solution.py:249
Async XLA Ops:
  0.0 18.5 %copy-start = (s32[128]{0:T(128)S(1)}, s32[128]{0:T(128)}, u32[]{:S(2)}) copy-start(s32[128]{0:T(128)} %param.11) | copy-start | bytes 1540
  1.6 16.9 %all-to-all-start = ((bf16[8,128,128]{2,1,0:T(8,128)(2,1)}), bf16[8,128,128]{2,1,0:T(8,128)(2,1)S(1)}, u32[]{:S(2)}, u32[]{:S(2)}) async-start(bf16[8,128,128]{2,1,0:T(8,128)(2,1)} %scale.1.scaled_ref), calls=%async_computation | async-start | bytes 524288 | tf_op jit(solution)/shard_map/all_to_all | solution.py:215
  17.1 1.4 %collective-permute-start = (bf16[512,128]{1,0:T(8,128)(2,1)S(1)}, bf16[512,128]{1,0:T(8,128)(2,1)S(1)}, u32[]{:S(2)}, u32[]{:S(2)}) collective-permute-start(bf16[512,128]{1,0:T(8,128)(2,1)S(1)} %get-tuple-element.9), channel_id=1, source_target_pairs={{16,0},{0,16},{17,1},{1,17},{18,2},{2,18},{19,3},{3,19},{20,4},{4,... | collective-permute-start | bytes 393224 | tf_op jit(solution)/shard_map/ppermute | solution.py:45

commit v3 on v0

v3 whole, which is shorter than its diff:
```python
import functools
import math

import jax
import jax.numpy as jnp
from jax import lax
from jax.experimental import pallas as pl
from jax.experimental.pallas import tpu as pltpu
from jax.sharding import PartitionSpec as P

ITERATIONS = 2


damping = 0.85

VMEM = pl.BlockSpec(memory_space=pltpu.VMEM)
SMEM = pl.BlockSpec(memory_space=pltpu.SMEM)
HBM = pl.BlockSpec(memory_space=pltpu.HBM)
ANY = pl.BlockSpec(memory_space=pl.ANY)

TILES_VMEM = 50 * 1024 * 1024
SMALL_VMEM = 8 * 1024 * 1024
LANES = 4
FLIGHT = 6


def in_hbm(*arrays):
    return [pltpu.with_memory_space_constraint(array, pltpu.HBM) for array in arrays]


def call(kernel, out_shape, name, **options):
    return pl.pallas_call(
        kernel,
        out_shape=out_shape,
        compiler_params=pltpu.CompilerParams(vmem_limit_bytes=options.pop("vmem", SMALL_VMEM)),
        cost_estimate=pl.CostEstimate(
            flops=options.pop("flops", 0), bytes_accessed=options.pop("size", 0), transcendentals=0
        ),
        name=name,
        **options,
    )


def bit_orders(cols):
    bits = list(range(cols.bit_length() - 1))
    return bits[::-1], bits


def column_masks(cols):
    return [
        [sum((block >> step & 1) << bit for step, bit in enumerate(order)) for block in range(cols)]
        for order in bit_orders(cols)
    ]


def exchange(value, rows, cols, step):
    pairs = []
    for row in range(rows):
        flip = 1 << bit_orders(cols)[row % 2][step]
        pairs += [(row * cols + (col ^ flip), row * cols + col) for col in range(cols)]
    return lax.ppermute(value, ("row", "col"), pairs)


def swap_rows(value):
    return lax.ppermute(value, "row", [(0, 1), (1, 0)])


def scale_kernel(prior_hbm, degree_hbm, scaled_ref, prior_ref, degree_ref, arrived):
    copies = [
        pltpu.make_async_copy(source, place, arrived.at[index])
        for index, (source, place) in enumerate(((prior_hbm, prior_ref), (degree_hbm, degree_ref)))
    ]
    for copy in copies:
        copy.start()
    for copy in copies:
        copy.wait()
    scaled_ref[0] = (prior_ref[...] / degree_ref[...].astype(jnp.float32)).astype(jnp.bfloat16)


def join_kernel(held_ref, received_ref, joined_ref):
    count = held_ref.shape[0]
    joined_ref[:count] = held_ref[...]
    joined_ref[count:] = received_ref[...]


def sum_kernel(
    rows, cols, owned_blocks, scaled_ref, count_ref, tiles_ref, out_hbm, in_hbm, seeds_hbm,
    weight_ref, restart_ref, buffer, total, out_ref, in_ref, seeds_ref, arrived, small,
):
    in_blocks, out_blocks = cols * owned_blocks, rows * owned_blocks
    slots, edge = tiles_ref.shape[2], tiles_ref.shape[3]
    group_total = arrived.shape[0]
    group = slots // group_total
    row, col = lax.axis_index("row"), lax.axis_index("col")

    def arrival(index):
        span = pl.ds(index * group, group)
        return pltpu.make_async_copy(tiles_ref.at[0, 0, span], buffer.at[span], arrived.at[index])

    copies = [
        pltpu.make_async_copy(source, place, small.at[index])
        for index, (source, place) in enumerate(
            ((out_hbm, out_ref), (in_hbm, in_ref), (seeds_hbm, seeds_ref))
        )
    ]
    for copy in copies:
        copy.start()
    for index in range(min(FLIGHT, group_total)):
        arrival(index).start()

    buffer[slots] = jnp.zeros((edge, edge), jnp.bfloat16)
    total[...] = jnp.zeros(total.shape, jnp.float32)

    for copy in copies:
        copy.wait()
    seed_total, sets = seeds_ref.shape
    owned = owned_blocks * edge
    vertex = lax.broadcasted_iota(jnp.int32, (owned, sets), 0) + (row * cols + col) * owned
    restart = jnp.zeros((owned, sets), jnp.float32)
    for seed in range(seed_total):
        restart += (seeds_ref[seed:seed + 1, :] == vertex).astype(jnp.float32)
    restart_ref[...] = (1.0 - damping) * restart.T

    occupied = count_ref[0, 0]

    def add_group(index, carry):
        arrival(index).wait()

        @pl.when(index + FLIGHT < group_total)
        def _():
            arrival(index + FLIGHT).start()

        first = index * group

        def add_tiles(step, carry):
            at = first + step * LANES
            for start in range(0, LANES, 2):
                sums = []
                for lane in range(start, start + 2):
                    slot = at + lane
                    pair = out_ref[0, 0, slot] * in_blocks + in_ref[0, 0, slot]
                    used = jnp.where(slot < occupied, slot, slots)
                    sums.append((lane, pair, total[lane, pair] + buffer[used].astype(jnp.float32)))
                for lane, pair, value in sums:
                    total[lane, pair] = value
            return carry

        here = jnp.clip(occupied - first, 0, group)
        return lax.fori_loop(0, (here + LANES - 1) // LANES, add_tiles, carry)

    lax.fori_loop(0, group_total, add_group, 0)

    for place in range(rows):
        owner = row ^ place if rows == 2 else place
        for block in range(owned_blocks):
            columns = slice(place * owned + block * edge, place * owned + (block + 1) * edge)
            for source in range(in_blocks):
                pair = (owner * owned_blocks + block) * in_blocks + source
                value = (total[0, pair] + total[1, pair]) + (total[2, pair] + total[3, pair])
                high = value.astype(jnp.bfloat16)
                low = (value - high.astype(jnp.float32)).astype(jnp.bfloat16)
                lines = source // owned_blocks, source % owned_blocks * edge
                weight_ref[lines[0], lines[1]:lines[1] + edge, columns] = high
                weight_ref[lines[0], owned + lines[1]:owned + lines[1] + edge, columns] = low


def product_kernel(rows, cols, *refs):
    parts, (weight_ref, *result_refs) = refs[:2], refs[2:]
    row, col = lax.axis_index("row"), lax.axis_index("col")
    even, odd = column_masks(cols)
    incoming = None
    for block in range(cols):
        half = cols // 2
        scaled = parts[block // half][block % half] if half else parts[0][0]
        column = col ^ jnp.where(row % 2 == 0, even[block], odd[block])
        term = jnp.dot(
            jnp.concatenate([scaled, scaled], axis=1), weight_ref[column], preferred_element_type=jnp.float32
        )
        incoming = term if incoming is None else incoming + term
    owned = incoming.shape[1] // rows
    if len(result_refs) == 1:
        for place in range(rows):
            result_refs[0][place] = incoming[:, place * owned:(place + 1) * owned]
    else:
        for place in range(rows):
            result_refs[place][...] = incoming[:, place * owned:(place + 1) * owned]


def finish_kernel(last, *refs):
    *incoming_refs, restart_ref, degree_ref, result_ref = refs
    incoming = sum(ref[...] for ref in incoming_refs)
    risk = restart_ref[...] + damping * incoming
    if last:
        result_ref[...] = risk
    else:
        result_ref[0] = (risk / degree_ref[...].astype(jnp.float32)).astype(jnp.bfloat16)


def local(tiles, tile_out, tile_in, tile_count, out_degree, seed_ids, prior):
    rows, cols = lax.axis_size("row"), lax.axis_size("col")
    sets, owned = prior.shape
    slots, edge = tiles.shape[2], tiles.shape[3]
    owned_blocks = owned // edge
    in_blocks, out_blocks = cols * owned_blocks, rows * owned_blocks
    group = math.gcd(slots, 32)
    degree = out_degree.reshape(1, owned)
    low = jnp.bfloat16

    scaled = call(
        scale_kernel,
        jax.ShapeDtypeStruct((1, sets, owned), low),
        "scale",
        in_specs=[HBM, HBM],
        out_specs=VMEM,
        scratch_shapes=[
            pltpu.VMEM((sets, owned), jnp.float32),
            pltpu.VMEM((1, owned), jnp.int32),
            pltpu.SemaphoreType.DMA((2,)),
        ],
        size=6 * sets * owned,
    )(*in_hbm(prior, degree))

    def spread(held):
        received = None
        for step in range(cols.bit_length() - 1):
            if received is not None:
                held = call(
                    join_kernel,
                    jax.ShapeDtypeStruct((2 * held.shape[0],) + held.shape[1:], low),
                    "join",
                    in_specs=[VMEM, VMEM],
                    out_specs=VMEM,
                    size=8 * held.size,
                )(held, received)
            received = exchange(held, rows, cols, step)
        return held, received

    held, received = spread(scaled)

    weight, restart = call(
        functools.partial(sum_kernel, rows, cols, owned_blocks),
        [
            jax.ShapeDtypeStruct((cols, 2 * owned, rows * owned), low),
            jax.ShapeDtypeStruct((sets, owned), jnp.float32),
        ],
        "sum_tiles",
        in_specs=[ANY, SMEM] + [HBM] * 4,
        out_specs=[VMEM] * 2,
        scratch_shapes=[
            pltpu.VMEM((slots + 1, edge, edge), low),
            pltpu.VMEM((LANES, out_blocks * in_blocks, edge, edge), jnp.float32),
            pltpu.SMEM(tile_out.shape, jnp.int32),
            pltpu.SMEM(tile_in.shape, jnp.int32),
            pltpu.VMEM((seed_ids.shape[1], sets), jnp.int32),
            pltpu.SemaphoreType.DMA((slots // group,)),
            pltpu.SemaphoreType.DMA((3,)),
        ],
        vmem=TILES_VMEM,
        flops=slots * edge * edge,
        size=2 * slots * edge * edge,
    )(held, tile_count, *in_hbm(tiles, tile_out, tile_in, seed_ids.T))

    for round_index in range(ITERATIONS):
        last = round_index == ITERATIONS - 1
        piece = jax.ShapeDtypeStruct((sets, owned), jnp.float32)
        partial_value = call(
            functools.partial(product_kernel, rows, cols),
            [piece] * 2 if rows == 2 else jax.ShapeDtypeStruct((rows, sets, owned), jnp.float32),
            "product",
            in_specs=[VMEM] * 3,
            out_specs=[VMEM] * 2 if rows == 2 else VMEM,
            flops=4 * sets * cols * owned * rows * owned,
            size=2 * cols * owned * (sets + 2 * rows * owned),
        )(held, received, weight)
        if rows == 2:
            incoming = (partial_value[0], swap_rows(partial_value[1]))
        else:
            incoming = (lax.psum_scatter(partial_value, "row", scatter_dimension=0, tiled=False),)
        value = call(
            functools.partial(finish_kernel, last),
            piece if last else jax.ShapeDtypeStruct((1, sets, owned), low),
            "last" if last else "next",
            in_specs=[VMEM] * (len(incoming) + 2),
            out_specs=VMEM,
            size=12 * sets * owned,
        )(*incoming, restart, degree)
        if not last:
            held, received = spread(value)
    return value


def solution(mesh):
    placed = (
        P("row", "col", None, None, None),
        P("row", "col", None),
        P("row", "col", None),
        P("row", "col"),
        P(("row", "col")),
        P("seed", None),
        P("seed", ("row", "col")),
    )
    return jax.shard_map(
        local, mesh=mesh, in_specs=placed, out_specs=P("seed", ("row", "col")), check_vma=False
    )
```

time: 197 us -> 27.1 us (0.14)
  other arithmetic: 88.9 us -> 0 us
  matrix products: 41.2 us -> 0 us
  local copies, waits for them, and re-layouts: 19.4 us -> 0.01 us
  blocking collectives: 18.6 us -> 0 us
  between operations: 14.2 us -> 0.72 us
  Pallas kernels: 0 us -> 8.16 us
  starting transfers between devices: 0.04 us -> 7.6 us
  waiting for transfers between devices: 13.2 us -> 10.5 us
    scatter-add x24 -> x0, other arithmetic: 63.7 us -> none  [advance(): return panel_sum.at[targets].add(product * valid_mask[:, None, None])]
    dot_general x24 -> x0, matrix products: 41.2 us -> none  [advance(): jnp.einsum('gsk,gkj->gsj', gathered, tile_block, preferred_element_type=j...]
    all_gather x2 -> x0, blocking collectives: 18.6 us -> none  [local(): blocks = lax.all_gather(scaled, 'col', axis=0, tiled=True)]
    gather x24 -> x0, local copies, waits for them, and re-layouts: 18 us -> none  [advance(): gathered = jnp.take(blocks, sources, axis=0)]
    and x24 -> x0, other arithmetic: 17.5 us -> none  [advance(): gathered = jnp.take(blocks, sources, axis=0)]
    reduce_scatter x2 -> x0, waiting for transfers between devices: 13.2 us -> none  [local(): lax.psum_scatter(partial_value, 'row', scatter_dimension=0, tiled=True)]
    ppermute x0 -> x6, waiting for transfers between devices: none -> 10.5 us  [the longest x4 8.05 us: exchange(): return lax.ppermute(value, ('row', 'col'), pairs)]
    pallas_call x0 -> x8, Pallas kernels: none -> 8.16 us  [the longest x1 6.11 us: local(): call(functools.partial(sum_kernel, rows, cols, owned_blocks), [jax.ShapeD...]
  transfers between devices with their start and end apart: 2 -> 6, of which waited for: 2 -> 5; matrix products, arithmetic and copies ran while one was open for 0% -> 0% of each run, Pallas kernels for 0% -> 23%
where the time goes in v3:
time: 27.1 us; the launch traced here: 27 us
  waiting for transfers between devices  10.5 us (39%)
  Pallas kernels  8.16 us (30%)
  starting transfers between devices  7.6 us (28%)
  between operations  0.72 us (3%)
    ppermute x4, waiting for transfers between devices, exchange(): return lax.ppermute(value, ('row', 'col'), pairs)  8.05 us
    ppermute x4, starting transfers between devices, exchange(): return lax.ppermute(value, ('row', 'col'), pairs)  7.46 us
    pallas_call x1, Pallas kernels, local(): call(functools.partial(sum_kernel, rows, cols, owned_blocks), [jax.ShapeD...  6.11 us
    ppermute x2, waiting for transfers between devices, swap_rows(): return lax.ppermute(value, 'row', [(0, 1), (1, 0)])  2.48 us
    pallas_call x1, Pallas kernels, local(): call(scale_kernel, jax.ShapeDtypeStruct((1, sets, owned), low), 'scale',...  0.88 us
    pallas_call x2, Pallas kernels, local(): call(functools.partial(finish_kernel, last), piece if last else jax.Shape...  0.66 us
  transfers between devices with their start and end apart: 6, of which 5 were waited for; matrix products, arithmetic and copies ran while one was open for 0% of the time, Pallas kernels for 23%

profile of v3, /device:TPU:0, one launch (start us, length us, event | category | flops | bytes accessed | tf_op | source)
XLA Modules:
  0.0 27.0 jit_solution(6048966709401718122)
XLA Ops:
  0.0 0.0 copy-start
  0.0 0.9 %scale.1.held_ref = bf16[1,128,128]{2,1,0:T(8,128)(2,1)S(1)} custom-call(f32[128,128]{1,0:T(8,128)} %prior_hbm.1, s32[1,128]{1,0:T(1,128)} %bitcast.2), custom_call_target="tpu_custom_call" | custom-call | bytes 98304 | tf_op jit(solution)/shard_map/scale/pallas_call | solution.py:209
  0.9 3.0 %collective-permute-start = (bf16[1,128,128]{2,1,0:T(8,128)(2,1)S(1)}, bf16[1,128,128]{2,1,0:T(8,128)(2,1)S(1)}, u32[]{:S(2)}, u32[]{:S(2)}) collective-permute-start(bf16[1,128,128]{2,1,0:T(8,128)(2,1)S(1)} %scale.1.held_ref), channel_id=1, source_target_pairs={{8,0},{12,4},{0,8},{4,12},{20,16},{16,20},{28,24},{24,28},{9,1},{1... | collective-permute-start | bytes 98312 | tf_op jit(solution)/shard_map/ppermute | solution.py:61
  3.9 1.9 %collective-permute-done.received_ref = bf16[1,128,128]{2,1,0:T(8,128)(2,1)S(1)} collective-permute-done((bf16[1,128,128]{2,1,0:T(8,128)(2,1)S(1)}, bf16[1,128,128]{2,1,0:T(8,128)(2,1)S(1)}, u32[]{:S(2)}, u32[]{:S(2)}) %collective-permute-start) | collective-permute-done | bytes 32800 | tf_op jit(solution)/shard_map/ppermute | solution.py:61
  5.8 2.0 %collective-permute-start.1 = (bf16[2,128,128]{2,1,0:T(8,128)(2,1)S(1)}, bf16[2,128,128]{2,1,0:T(8,128)(2,1)S(1)}, u32[]{:S(2)}, u32[]{:S(2)}) collective-permute-start(bf16[2,128,128]{2,1,0:T(8,128)(2,1)S(1)} %join.2.scaled_ref.refs_0_), channel_id=1, source_target_pairs={{4,0},{0,4},{12,8},{8,12},{24,16},{28,20},{16,24},{20,28},{5,1},{1... | collective-permute-start | bytes 196616 | tf_op jit(solution)/shard_map/ppermute | solution.py:61
  8.5 6.1 %sum_tiles.1 = (bf16[4,256,256]{2,1,0:T(8,128)(2,1)S(1)}, f32[128,128]{1,0:T(8,128)S(1)}) custom-call(bf16[2,128,128]{2,1,0:T(8,128)(2,1)S(1)} %join.2.scaled_ref.refs_0_, s32[1,1]{1,0:T(1,128)S(6)} %copy.8.count_ref, bf16[1,1,384,128,128]{4,3,2,1,0:T(8,128)(2,1)} %tiles_ref.1, s32[1,1,384]{2,1,0:T(1,128)} %out_hbm.1, s32[1,1,384]{2,1,0:T(1,128)} %in_hbm.1, ...), custom_call_target="tpu_custom_call" | custom-call | flops 6291456 | bytes 12582912 | tf_op jit(solution)/shard_map/sum_tiles/pallas_call | solution.py:240
  14.6 0.0 collective-permute-done.1.refs_1_
  14.6 0.3 product.2
  14.9 0.1 collective-permute-start.2
  14.9 1.2 %collective-permute-done.2.refs_1_ = f32[128,128]{1,0:T(8,128)S(1)} collective-permute-done((f32[128,128]{1,0:T(8,128)S(1)}, f32[128,128]{1,0:T(8,128)S(1)}, u32[]{:S(2)}, u32[]{:S(2)}) %collective-permute-start.2) | collective-permute-done | bytes 65568 | tf_op jit(solution)/shard_map/ppermute | solution.py:65
  16.2 0.0 copy-done
  16.2 2.4 %collective-permute-start.3 = (bf16[1,128,128]{2,1,0:T(8,128)(2,1)S(1)}, bf16[1,128,128]{2,1,0:T(8,128)(2,1)S(1)}, u32[]{:S(2)}, u32[]{:S(2)}) collective-permute-start(bf16[1,128,128]{2,1,0:T(8,128)(2,1)S(1)} %next.1.held_ref), channel_id=1, source_target_pairs={{8,0},{12,4},{0,8},{4,12},{20,16},{16,20},{28,24},{24,28},{9,1},{1... | collective-permute-start | bytes 98312 | tf_op jit(solution)/shard_map/ppermute | solution.py:61
  18.6 1.9 %collective-permute-done.3.received_ref = bf16[1,128,128]{2,1,0:T(8,128)(2,1)S(1)} collective-permute-done((bf16[1,128,128]{2,1,0:T(8,128)(2,1)S(1)}, bf16[1,128,128]{2,1,0:T(8,128)(2,1)S(1)}, u32[]{:S(2)}, u32[]{:S(2)}) %collective-permute-start.3) | collective-permute-done | bytes 32800 | tf_op jit(solution)/shard_map/ppermute | solution.py:61
  20.5 0.0 collective-permute-start.4
  20.6 4.3 %collective-permute-done.4.refs_1_ = bf16[2,128,128]{2,1,0:T(8,128)(2,1)S(1)} collective-permute-done((bf16[2,128,128]{2,1,0:T(8,128)(2,1)S(1)}, bf16[2,128,128]{2,1,0:T(8,128)(2,1)S(1)}, u32[]{:S(2)}, u32[]{:S(2)}) %collective-permute-start.4) | collective-permute-done | bytes 65568 | tf_op jit(solution)/shard_map/ppermute | solution.py:61
  24.8 0.2 product.3
  25.1 0.1 collective-permute-start.5
  25.1 1.2 %collective-permute-done.5.refs_1_ = f32[128,128]{1,0:T(8,128)S(1)} collective-permute-done((f32[128,128]{1,0:T(8,128)S(1)}, f32[128,128]{1,0:T(8,128)S(1)}, u32[]{:S(2)}, u32[]{:S(2)}) %collective-permute-start.5) | collective-permute-done | bytes 65568 | tf_op jit(solution)/shard_map/ppermute | solution.py:65
  26.4 0.6 %last.1 = f32[128,128]{1,0:T(8,128)} custom-call(f32[128,128]{1,0:T(8,128)S(1)} %get-tuple-element.15.refs_0_, f32[128,128]{1,0:T(8,128)S(1)} %collective-permute-done.5.refs_1_, f32[128,128]{1,0:T(8,128)S(1)} %get-tuple-element.14.refs_2_, s32[1,128]{1,0:T(1,128)S(1)} %bitcast.4), custom_call_target="tpu_custom_call" | custom-call | bytes 196608 | tf_op jit(solution)/shard_map/last/pallas_call | solution.py:279
  (3 shorter events, 0.0 us)
Async XLA Ops:
  0.0 16.2 %copy-start = (s32[128]{0:T(128)S(1)}, s32[128]{0:T(128)}, u32[]{:S(2)}) copy-start(s32[128]{0:T(128)} %param.11) | copy-start | bytes 1540
  0.9 4.9 %collective-permute-start = (bf16[1,128,128]{2,1,0:T(8,128)(2,1)S(1)}, bf16[1,128,128]{2,1,0:T(8,128)(2,1)S(1)}, u32[]{:S(2)}, u32[]{:S(2)}) collective-permute-start(bf16[1,128,128]{2,1,0:T(8,128)(2,1)S(1)} %scale.1.held_ref), channel_id=1, source_target_pairs={{8,0},{12,4},{0,8},{4,12},{20,16},{16,20},{28,24},{24,28},{9,1},{1... | collective-permute-start | bytes 98312 | tf_op jit(solution)/shard_map/ppermute | solution.py:61
  5.8 8.8 %collective-permute-start.1 = (bf16[2,128,128]{2,1,0:T(8,128)(2,1)S(1)}, bf16[2,128,128]{2,1,0:T(8,128)(2,1)S(1)}, u32[]{:S(2)}, u32[]{:S(2)}) collective-permute-start(bf16[2,128,128]{2,1,0:T(8,128)(2,1)S(1)} %join.2.scaled_ref.refs_0_), channel_id=1, source_target_pairs={{4,0},{0,4},{12,8},{8,12},{24,16},{28,20},{16,24},{20,28},{5,1},{1... | collective-permute-start | bytes 196616 | tf_op jit(solution)/shard_map/ppermute | solution.py:61
  14.9 1.3 %collective-permute-start.2 = (f32[128,128]{1,0:T(8,128)S(1)}, f32[128,128]{1,0:T(8,128)S(1)}, u32[]{:S(2)}, u32[]{:S(2)}) collective-permute-start(f32[128,128]{1,0:T(8,128)S(1)} %get-tuple-element.13), channel_id=1, source_target_pairs={{0,16},{16,0},{1,17},{17,1},{2,18},{18,2},{3,19},{19,3},{4,20},{20... | collective-permute-start | bytes 196616 | tf_op jit(solution)/shard_map/ppermute | solution.py:65
  16.2 4.3 %collective-permute-start.3 = (bf16[1,128,128]{2,1,0:T(8,128)(2,1)S(1)}, bf16[1,128,128]{2,1,0:T(8,128)(2,1)S(1)}, u32[]{:S(2)}, u32[]{:S(2)}) collective-permute-start(bf16[1,128,128]{2,1,0:T(8,128)(2,1)S(1)} %next.1.held_ref), channel_id=1, source_target_pairs={{8,0},{12,4},{0,8},{4,12},{20,16},{16,20},{28,24},{24,28},{9,1},{1... | collective-permute-start | bytes 98312 | tf_op jit(solution)/shard_map/ppermute | solution.py:61
  20.5 4.3 %collective-permute-start.4 = (bf16[2,128,128]{2,1,0:T(8,128)(2,1)S(1)}, bf16[2,128,128]{2,1,0:T(8,128)(2,1)S(1)}, u32[]{:S(2)}, u32[]{:S(2)}) collective-permute-start(bf16[2,128,128]{2,1,0:T(8,128)(2,1)S(1)} %join.3.refs_0_), channel_id=1, source_target_pairs={{4,0},{0,4},{12,8},{8,12},{24,16},{28,20},{16,24},{20,28},{5,1},{1... | collective-permute-start | bytes 196616 | tf_op jit(solution)/shard_map/ppermute | solution.py:61
  25.1 1.3 %collective-permute-start.5 = (f32[128,128]{1,0:T(8,128)S(1)}, f32[128,128]{1,0:T(8,128)S(1)}, u32[]{:S(2)}, u32[]{:S(2)}) collective-permute-start(f32[128,128]{1,0:T(8,128)S(1)} %get-tuple-element.16), channel_id=1, source_target_pairs={{0,16},{16,0},{1,17},{17,1},{2,18},{18,2},{3,19},{19,3},{4,20},{20... | collective-permute-start | bytes 196616 | tf_op jit(solution)/shard_map/ppermute | solution.py:65

commit v4 on v3

--- a/solution.py
+++ b/solution.py
@@ -21,6 +21,7 @@
 TILES_VMEM = 50 * 1024 * 1024
 SMALL_VMEM = 8 * 1024 * 1024
 LANES = 4
+UNROLL = 8
 FLIGHT = 6
 
 
@@ -41,24 +42,14 @@
     )
 
 
-def bit_orders(cols):
-    bits = list(range(cols.bit_length() - 1))
-    return bits[::-1], bits
-
-
-def column_masks(cols):
-    return [
-        [sum((block >> step & 1) << bit for step, bit in enumerate(order)) for block in range(cols)]
-        for order in bit_orders(cols)
-    ]
-
-
-def exchange(value, rows, cols, step):
-    pairs = []
-    for row in range(rows):
-        flip = 1 << bit_orders(cols)[row % 2][step]
-        pairs += [(row * cols + (col ^ flip), row * cols + col) for col in range(cols)]
-    return lax.ppermute(value, ("row", "col"), pairs)
+def partner(index, offset, extent):
+    if extent & (extent - 1) == 0:
+        return index ^ offset
+    return (index + offset) % extent
+
+
+def from_column(value, cols, offset):
+    return lax.ppermute(value, "col", [(partner(col, offset, cols), col) for col in range(cols)])
 
 
 def swap_rows(value):
@@ -74,13 +65,7 @@
         copy.start()
     for copy in copies:
         copy.wait()
-    scaled_ref[0] = (prior_ref[...] / degree_ref[...].astype(jnp.float32)).astype(jnp.bfloat16)
-
-
-def join_kernel(held_ref, received_ref, joined_ref):
-    count = held_ref.shape[0]
-    joined_ref[:count] = held_ref[...]
-    joined_ref[count:] = received_ref[...]
+    scaled_ref[...] = (prior_ref[...] / degree_ref[...].astype(jnp.float32)).astype(jnp.bfloat16)
 
 
 def sum_kernel(
@@ -133,20 +118,23 @@
         first = index * group
 
         def add_tiles(step, carry):
-            at = first + step * LANES
-            for start in range(0, LANES, 2):
-                sums = []
-                for lane in range(start, start + 2):
-                    slot = at + lane
-                    pair = out_ref[0, 0, slot] * in_blocks + in_ref[0, 0, slot]
-                    used = jnp.where(slot < occupied, slot, slots)
-                    sums.append((lane, pair, total[lane, pair] + buffer[used].astype(jnp.float32)))
+            at = first + step * UNROLL
+            places = []
+            for lane in range(UNROLL):
+                slot = at + lane
+                pair = out_ref[0, 0, slot] * in_blocks + in_ref[0, 0, slot]
+                places.append((lane % LANES, pair, jnp.where(slot < occupied, slot, slots)))
+            for start in range(0, UNROLL, 2):
+                sums = [
+                    (lane, pair, total[lane, pair] + buffer[used].astype(jnp.float32))
+                    for lane, pair, used in places[start:start + 2]
+                ]
                 for lane, pair, value in sums:
                     total[lane, pair] = value
             return carry
 
         here = jnp.clip(occupied - first, 0, group)
-        return lax.fori_loop(0, (here + LANES - 1) // LANES, add_tiles, carry)
+        return lax.fori_loop(0, (here + UNROLL - 1) // UNROLL, add_tiles, carry)
 
     lax.fori_loop(0, group_total, add_group, 0)
 
@@ -165,16 +153,15 @@
 
 
 def product_kernel(rows, cols, *refs):
-    parts, (weight_ref, *result_refs) = refs[:2], refs[2:]
-    row, col = lax.axis_index("row"), lax.axis_index("col")
-    even, odd = column_masks(cols)
+    parts, (weight_ref, *result_refs) = refs[:cols], refs[cols:]
+    col = lax.axis_index("col")
     incoming = None
-    for block in range(cols):
-        half = cols // 2
-        scaled = parts[block // half][block % half] if half else parts[0][0]
-        column = col ^ jnp.where(row % 2 == 0, even[block], odd[block])
+    for offset in range(cols):
+        scaled = parts[offset][...]
         term = jnp.dot(
-            jnp.concatenate([scaled, scaled], axis=1), weight_ref[column], preferred_element_type=jnp.float32
+            jnp.concatenate([scaled, scaled], axis=1),
+            weight_ref[partner(col, offset, cols)],
+            preferred_element_type=jnp.float32,
         )
         incoming = term if incoming is None else incoming + term
     owned = incoming.shape[1] // rows
@@ -193,7 +180,7 @@
     if last:
         result_ref[...] = risk
     else:
-        result_ref[0] = (risk / degree_ref[...].astype(jnp.float32)).astype(jnp.bfloat16)
+        result_ref[...] = (risk / degree_ref[...].astype(jnp.float32)).astype(jnp.bfloat16)
 
 
 def local(tiles, tile_out, tile_in, tile_count, out_degree, seed_ids, prior):
@@ -208,7 +195,7 @@
 
     scaled = call(
         scale_kernel,
-        jax.ShapeDtypeStruct((1, sets, owned), low),
+        jax.ShapeDtypeStruct((sets, owned), low),
         "scale",
         in_specs=[HBM, HBM],
         out_specs=VMEM,
@@ -220,22 +207,10 @@
         size=6 * sets * owned,
     )(*in_hbm(prior, degree))
 
-    def spread(held):
-        received = None
-        for step in range(cols.bit_length() - 1):
-            if received is not None:
-                held = call(
-                    join_kernel,
-                    jax.ShapeDtypeStruct((2 * held.shape[0],) + held.shape[1:], low),
-                    "join",
-                    in_specs=[VMEM, VMEM],
-                    out_specs=VMEM,
-                    size=8 * held.size,
-                )(held, received)
-            received = exchange(held, rows, cols, step)
-        return held, received
-
-    held, received = spread(scaled)
+    def spread(value):
+        return [value] + [from_column(value, cols, offset) for offset in range(cols - 1, 0, -1)][::-1]
+
+    parts = spread(scaled)
 
     weight, restart = call(
         functools.partial(sum_kernel, rows, cols, owned_blocks),
@@ -258,7 +233,7 @@
         vmem=TILES_VMEM,
         flops=slots * edge * edge,
         size=2 * slots * edge * edge,
-    )(held, tile_count, *in_hbm(tiles, tile_out, tile_in, seed_ids.T))
+    )(scaled, tile_count, *in_hbm(tiles, tile_out, tile_in, seed_ids.T))
 
     for round_index in range(ITERATIONS):
         last = round_index == ITERATIONS - 1
@@ -267,25 +242,25 @@
             functools.partial(product_kernel, rows, cols),
             [piece] * 2 if rows == 2 else jax.ShapeDtypeStruct((rows, sets, owned), jnp.float32),
             "product",
-            in_specs=[VMEM] * 3,
+            in_specs=[VMEM] * (cols + 1),
             out_specs=[VMEM] * 2 if rows == 2 else VMEM,
             flops=4 * sets * cols * owned * rows * owned,
             size=2 * cols * owned * (sets + 2 * rows * owned),
-        )(held, received, weight)
+        )(*parts, weight)
         if rows == 2:
             incoming = (partial_value[0], swap_rows(partial_value[1]))
         else:
             incoming = (lax.psum_scatter(partial_value, "row", scatter_dimension=0, tiled=False),)
         value = call(
             functools.partial(finish_kernel, last),
-            piece if last else jax.ShapeDtypeStruct((1, sets, owned), low),
+            piece if last else jax.ShapeDtypeStruct((sets, owned), low),
             "last" if last else "next",
             in_specs=[VMEM] * (len(incoming) + 2),
             out_specs=VMEM,
             size=12 * sets * owned,
         )(*incoming, restart, degree)
         if not last:
-            held, received = spread(value)
+            parts = spread(value)
     return value
 
 

time: 27.1 us -> 23.7 us (0.87)
  waiting for transfers between devices: 10.5 us -> 5.71 us
  starting transfers between devices: 7.6 us -> 8.86 us
    ppermute x4 -> x6, waiting for transfers between devices: 8.05 us -> 3.22 us  [from_column(): lax.ppermute(value, 'col', [(partner(col, offset, cols), col) for col in...]
    ppermute x4 -> x6, starting transfers between devices: 7.46 us -> 8.72 us  [from_column(): lax.ppermute(value, 'col', [(partner(col, offset, cols), col) for col in...]
    pallas_call x3 -> x1, Pallas kernels: 0.9 us -> 0.88 us  [local(): call(scale_kernel, jax.ShapeDtypeStruct((sets, owned), low), 'scale', in_...]
  transfers between devices with their start and end apart: 6 -> 8, of which waited for: 5 -> 5; matrix products, arithmetic and copies ran while one was open for 0% -> 0% of each run, Pallas kernels for 23% -> 26%
where the time goes in v4:
time: 23.7 us; the launch traced here: 23.4 us
  starting transfers between devices  8.86 us (37%)
  Pallas kernels  8.08 us (34%)
  waiting for transfers between devices  5.71 us (24%)
  between operations  0.73 us (3%)
    ppermute x6, starting transfers between devices, from_column(): lax.ppermute(value, 'col', [(partner(col, offset, cols), col) for col in...  8.72 us
    pallas_call x1, Pallas kernels, local(): call(functools.partial(sum_kernel, rows, cols, owned_blocks), [jax.ShapeD...  6.05 us
    ppermute x6, waiting for transfers between devices, from_column(): lax.ppermute(value, 'col', [(partner(col, offset, cols), col) for col in...  3.22 us
    ppermute x2, waiting for transfers between devices, swap_rows(): return lax.ppermute(value, 'row', [(0, 1), (1, 0)])  2.48 us
    pallas_call x1, Pallas kernels, local(): call(scale_kernel, jax.ShapeDtypeStruct((sets, owned), low), 'scale', in_...  0.88 us
    pallas_call x2, Pallas kernels, local(): call(functools.partial(finish_kernel, last), piece if last else jax.Shape...  0.67 us
    pallas_call x2, Pallas kernels, local(): call(functools.partial(product_kernel, rows, cols), [piece] * 2 if rows =...  0.48 us
  transfers between devices with their start and end apart: 8, of which 5 were waited for; matrix products, arithmetic and copies ran while one was open for 0% of the time, Pallas kernels for 26%

profile of v4, /device:TPU:0, one launch (start us, length us, event | category | flops | bytes accessed | tf_op | source)
XLA Modules:
  0.0 23.4 jit_solution(14249144833059594461)
XLA Ops:
  0.0 0.0 copy-start
  0.0 0.9 %scale.1.scaled_ref.refs_0_ = bf16[128,128]{1,0:T(8,128)(2,1)S(1)} custom-call(f32[128,128]{1,0:T(8,128)} %prior_hbm.1, s32[1,128]{1,0:T(1,128)} %bitcast.2), custom_call_target="tpu_custom_call" | custom-call | bytes 98304 | tf_op jit(solution)/shard_map/scale/pallas_call | solution.py:196
  0.9 4.0 %collective-permute-start.2 = (bf16[128,128]{1,0:T(8,128)(2,1)S(1)}, bf16[128,128]{1,0:T(8,128)(2,1)S(1)}, u32[]{:S(2)}, u32[]{:S(2)}) collective-permute-start(bf16[128,128]{1,0:T(8,128)(2,1)S(1)} %scale.1.scaled_ref.refs_0_), channel_id=1, source_target_pairs={{12,0},{8,4},{4,8},{0,12},{13,1},{9,5},{5,9},{1,13},{14,2},{10,6},... | collective-permute-start | bytes 98312 | tf_op jit(solution)/shard_map/ppermute | solution.py:52
  4.9 0.5 %collective-permute-start.1 = (bf16[128,128]{1,0:T(8,128)(2,1)S(1)}, bf16[128,128]{1,0:T(8,128)(2,1)S(1)}, u32[]{:S(2)}, u32[]{:S(2)}) collective-permute-start(bf16[128,128]{1,0:T(8,128)(2,1)S(1)} %scale.1.scaled_ref.refs_0_), channel_id=1, source_target_pairs={{8,0},{12,4},{0,8},{4,12},{9,1},{13,5},{1,9},{5,13},{10,2},{14,6},... | collective-permute-start | bytes 98312 | tf_op jit(solution)/shard_map/ppermute | solution.py:52
  5.4 0.1 collective-permute-start
  6.1 6.0 %sum_tiles.1 = (bf16[4,256,256]{2,1,0:T(8,128)(2,1)S(1)}, f32[128,128]{1,0:T(8,128)S(1)}) custom-call(bf16[128,128]{1,0:T(8,128)(2,1)S(1)} %scale.1.scaled_ref.refs_0_, s32[1,1]{1,0:T(1,128)S(6)} %copy.8.count_ref, bf16[1,1,384,128,128]{4,3,2,1,0:T(8,128)(2,1)} %tiles_ref.1, s32[1,1,384]{2,1,0:T(1,128)} %out_hbm.1, s32[1,1,384]{2,1,0:T(1,128)} %in_hbm.1, ...), custom_call_target="tpu_custom_call" | custom-call | flops 6291456 | bytes 12582912 | tf_op jit(solution)/shard_map/sum_tiles/pallas_call | solution.py:215
  12.2 0.0 collective-permute-done.2.refs_3_
  12.2 0.0 collective-permute-done.1.refs_2_
  12.2 0.0 collective-permute-done.refs_1_
  12.2 0.2 %product.2 = (f32[128,128]{1,0:T(8,128)S(1)}, f32[128,128]{1,0:T(8,128)S(1)}) custom-call(bf16[128,128]{1,0:T(8,128)(2,1)S(1)} %scale.1.scaled_ref.refs_0_, bf16[128,128]{1,0:T(8,128)(2,1)S(1)} %collective-permute-done.refs_1_, bf16[128,128]{1,0:T(8,128)(2,1)S(1)} %collective-permute-done.1.refs_2_, bf16[128,128]{1,0:T(8,128)(2,1)S(1)} %collective-permute-done.2.refs_3_, ...), custom_call_target="tpu_custom_call" | custom-call | flops 67108864 | bytes 655360 | tf_op jit(solution)/shard_map/product/pallas_call | solution.py:241
  12.5 0.1 collective-permute-start.3
  12.6 1.2 %collective-permute-done.3.refs_1_ = f32[128,128]{1,0:T(8,128)S(1)} collective-permute-done((f32[128,128]{1,0:T(8,128)S(1)}, f32[128,128]{1,0:T(8,128)S(1)}, u32[]{:S(2)}, u32[]{:S(2)}) %collective-permute-start.3) | collective-permute-done | bytes 65568 | tf_op jit(solution)/shard_map/ppermute | solution.py:56
  13.8 0.0 copy-done
  13.8 2.9 %collective-permute-start.6 = (bf16[128,128]{1,0:T(8,128)(2,1)S(1)}, bf16[128,128]{1,0:T(8,128)(2,1)S(1)}, u32[]{:S(2)}, u32[]{:S(2)}) collective-permute-start(bf16[128,128]{1,0:T(8,128)(2,1)S(1)} %next.1.refs_0_), channel_id=1, source_target_pairs={{12,0},{8,4},{4,8},{0,12},{13,1},{9,5},{5,9},{1,13},{14,2},{10,6},... | collective-permute-start | bytes 98312 | tf_op jit(solution)/shard_map/ppermute | solution.py:52
  16.8 0.5 %collective-permute-start.5 = (bf16[128,128]{1,0:T(8,128)(2,1)S(1)}, bf16[128,128]{1,0:T(8,128)(2,1)S(1)}, u32[]{:S(2)}, u32[]{:S(2)}) collective-permute-start(bf16[128,128]{1,0:T(8,128)(2,1)S(1)} %next.1.refs_0_), channel_id=1, source_target_pairs={{8,0},{12,4},{0,8},{4,12},{9,1},{13,5},{1,9},{5,13},{10,2},{14,6},... | collective-permute-start | bytes 98312 | tf_op jit(solution)/shard_map/ppermute | solution.py:52
  17.3 0.7 %collective-permute-start.4 = (bf16[128,128]{1,0:T(8,128)(2,1)S(1)}, bf16[128,128]{1,0:T(8,128)(2,1)S(1)}, u32[]{:S(2)}, u32[]{:S(2)}) collective-permute-start(bf16[128,128]{1,0:T(8,128)(2,1)S(1)} %next.1.refs_0_), channel_id=1, source_target_pairs={{4,0},{0,4},{12,8},{8,12},{5,1},{1,5},{13,9},{9,13},{6,2},{2,6},{1... | collective-permute-start | bytes 98312 | tf_op jit(solution)/shard_map/ppermute | solution.py:52
  17.9 0.8 %collective-permute-done.6.refs_3_ = bf16[128,128]{1,0:T(8,128)(2,1)S(1)} collective-permute-done((bf16[128,128]{1,0:T(8,128)(2,1)S(1)}, bf16[128,128]{1,0:T(8,128)(2,1)S(1)}, u32[]{:S(2)}, u32[]{:S(2)}) %collective-permute-start.6) | collective-permute-done | bytes 32800 | tf_op jit(solution)/shard_map/ppermute | solution.py:52
  18.7 2.0 %collective-permute-done.5.refs_2_ = bf16[128,128]{1,0:T(8,128)(2,1)S(1)} collective-permute-done((bf16[128,128]{1,0:T(8,128)(2,1)S(1)}, bf16[128,128]{1,0:T(8,128)(2,1)S(1)}, u32[]{:S(2)}, u32[]{:S(2)}) %collective-permute-start.5) | collective-permute-done | bytes 32800 | tf_op jit(solution)/shard_map/ppermute | solution.py:52
  20.7 0.5 %collective-permute-done.4.refs_1_ = bf16[128,128]{1,0:T(8,128)(2,1)S(1)} collective-permute-done((bf16[128,128]{1,0:T(8,128)(2,1)S(1)}, bf16[128,128]{1,0:T(8,128)(2,1)S(1)}, u32[]{:S(2)}, u32[]{:S(2)}) %collective-permute-start.4) | collective-permute-done | bytes 32800 | tf_op jit(solution)/shard_map/ppermute | solution.py:52
  21.2 0.2 %product.3 = (f32[128,128]{1,0:T(8,128)S(1)}, f32[128,128]{1,0:T(8,128)S(1)}) custom-call(bf16[128,128]{1,0:T(8,128)(2,1)S(1)} %next.1.refs_0_, bf16[128,128]{1,0:T(8,128)(2,1)S(1)} %collective-permute-done.4.refs_1_, bf16[128,128]{1,0:T(8,128)(2,1)S(1)} %collective-permute-done.5.refs_2_, bf16[128,128]{1,0:T(8,128)(2,1)S(1)} %collective-permute-done.6.refs_3_, ...), custom_call_target="tpu_custom_call" | custom-call | flops 67108864 | bytes 655360 | tf_op jit(solution)/shard_map/product/pallas_call | solution.py:241
  21.4 0.1 collective-permute-start.7
  21.5 1.2 %collective-permute-done.7.refs_1_ = f32[128,128]{1,0:T(8,128)S(1)} collective-permute-done((f32[128,128]{1,0:T(8,128)S(1)}, f32[128,128]{1,0:T(8,128)S(1)}, u32[]{:S(2)}, u32[]{:S(2)}) %collective-permute-start.7) | collective-permute-done | bytes 65568 | tf_op jit(solution)/shard_map/ppermute | solution.py:56
  22.7 0.6 %last.1 = f32[128,128]{1,0:T(8,128)} custom-call(f32[128,128]{1,0:T(8,128)S(1)} %get-tuple-element.15.refs_0_, f32[128,128]{1,0:T(8,128)S(1)} %collective-permute-done.7.refs_1_, f32[128,128]{1,0:T(8,128)S(1)} %get-tuple-element.14.refs_2_, s32[1,128]{1,0:T(1,128)S(1)} %bitcast.4), custom_call_target="tpu_custom_call" | custom-call | bytes 196608 | tf_op jit(solution)/shard_map/last/pallas_call | solution.py:254
  (1 shorter events, 0.0 us)
Async XLA Ops:
  0.0 13.8 %copy-start = (s32[128]{0:T(128)S(1)}, s32[128]{0:T(128)}, u32[]{:S(2)}) copy-start(s32[128]{0:T(128)} %param.11) | copy-start | bytes 1540
  0.9 11.3 %collective-permute-start.2 = (bf16[128,128]{1,0:T(8,128)(2,1)S(1)}, bf16[128,128]{1,0:T(8,128)(2,1)S(1)}, u32[]{:S(2)}, u32[]{:S(2)}) collective-permute-start(bf16[128,128]{1,0:T(8,128)(2,1)S(1)} %scale.1.scaled_ref.refs_0_), channel_id=1, source_target_pairs={{12,0},{8,4},{4,8},{0,12},{13,1},{9,5},{5,9},{1,13},{14,2},{10,6},... | collective-permute-start | bytes 98312 | tf_op jit(solution)/shard_map/ppermute | solution.py:52
  4.9 7.4 %collective-permute-start.1 = (bf16[128,128]{1,0:T(8,128)(2,1)S(1)}, bf16[128,128]{1,0:T(8,128)(2,1)S(1)}, u32[]{:S(2)}, u32[]{:S(2)}) collective-permute-start(bf16[128,128]{1,0:T(8,128)(2,1)S(1)} %scale.1.scaled_ref.refs_0_), channel_id=1, source_target_pairs={{8,0},{12,4},{0,8},{4,12},{9,1},{13,5},{1,9},{5,13},{10,2},{14,6},... | collective-permute-start | bytes 98312 | tf_op jit(solution)/shard_map/ppermute | solution.py:52
  5.4 6.9 %collective-permute-start = (bf16[128,128]{1,0:T(8,128)(2,1)S(1)}, bf16[128,128]{1,0:T(8,128)(2,1)S(1)}, u32[]{:S(2)}, u32[]{:S(2)}) collective-permute-start(bf16[128,128]{1,0:T(8,128)(2,1)S(1)} %scale.1.scaled_ref.refs_0_), channel_id=1, source_target_pairs={{4,0},{0,4},{12,8},{8,12},{5,1},{1,5},{13,9},{9,13},{6,2},{2,6},{1... | collective-permute-start | bytes 98312 | tf_op jit(solution)/shard_map/ppermute | solution.py:52
  12.5 1.3 %collective-permute-start.3 = (f32[128,128]{1,0:T(8,128)S(1)}, f32[128,128]{1,0:T(8,128)S(1)}, u32[]{:S(2)}, u32[]{:S(2)}) collective-permute-start(f32[128,128]{1,0:T(8,128)S(1)} %get-tuple-element.13), channel_id=1, source_target_pairs={{0,16},{16,0},{1,17},{17,1},{2,18},{18,2},{3,19},{19,3},{4,20},{20... | collective-permute-start | bytes 196616 | tf_op jit(solution)/shard_map/ppermute | solution.py:56
  13.8 4.9 %collective-permute-start.6 = (bf16[128,128]{1,0:T(8,128)(2,1)S(1)}, bf16[128,128]{1,0:T(8,128)(2,1)S(1)}, u32[]{:S(2)}, u32[]{:S(2)}) collective-permute-start(bf16[128,128]{1,0:T(8,128)(2,1)S(1)} %next.1.refs_0_), channel_id=1, source_target_pairs={{12,0},{8,4},{4,8},{0,12},{13,1},{9,5},{5,9},{1,13},{14,2},{10,6},... | collective-permute-start | bytes 98312 | tf_op jit(solution)/shard_map/ppermute | solution.py:52
  16.8 3.9 %collective-permute-start.5 = (bf16[128,128]{1,0:T(8,128)(2,1)S(1)}, bf16[128,128]{1,0:T(8,128)(2,1)S(1)}, u32[]{:S(2)}, u32[]{:S(2)}) collective-permute-start(bf16[128,128]{1,0:T(8,128)(2,1)S(1)} %next.1.refs_0_), channel_id=1, source_target_pairs={{8,0},{12,4},{0,8},{4,12},{9,1},{13,5},{1,9},{5,13},{10,2},{14,6},... | collective-permute-start | bytes 98312 | tf_op jit(solution)/shard_map/ppermute | solution.py:52
  17.3 3.9 %collective-permute-start.4 = (bf16[128,128]{1,0:T(8,128)(2,1)S(1)}, bf16[128,128]{1,0:T(8,128)(2,1)S(1)}, u32[]{:S(2)}, u32[]{:S(2)}) collective-permute-start(bf16[128,128]{1,0:T(8,128)(2,1)S(1)} %next.1.refs_0_), channel_id=1, source_target_pairs={{4,0},{0,4},{12,8},{8,12},{5,1},{1,5},{13,9},{9,13},{6,2},{2,6},{1... | collective-permute-start | bytes 98312 | tf_op jit(solution)/shard_map/ppermute | solution.py:52
  21.4 1.3 %collective-permute-start.7 = (f32[128,128]{1,0:T(8,128)S(1)}, f32[128,128]{1,0:T(8,128)S(1)}, u32[]{:S(2)}, u32[]{:S(2)}) collective-permute-start(f32[128,128]{1,0:T(8,128)S(1)} %get-tuple-element.16), channel_id=1, source_target_pairs={{0,16},{16,0},{1,17},{17,1},{2,18},{18,2},{3,19},{19,3},{4,20},{20... | collective-permute-start | bytes 196616 | tf_op jit(solution)/shard_map/ppermute | solution.py:56

commit v5 on v4

--- a/solution.py
+++ b/solution.py
@@ -1,5 +1,4 @@
 import functools
-import math
 
 import jax
 import jax.numpy as jnp
@@ -18,11 +17,10 @@
 HBM = pl.BlockSpec(memory_space=pltpu.HBM)
 ANY = pl.BlockSpec(memory_space=pl.ANY)
 
-TILES_VMEM = 50 * 1024 * 1024
+TILES_VMEM = 32 * 1024 * 1024
 SMALL_VMEM = 8 * 1024 * 1024
 LANES = 4
 UNROLL = 8
-FLIGHT = 6
 
 
 def in_hbm(*arrays):
@@ -56,48 +54,37 @@
     return lax.ppermute(value, "row", [(0, 1), (1, 0)])
 
 
-def scale_kernel(prior_hbm, degree_hbm, scaled_ref, prior_ref, degree_ref, arrived):
+def scale_kernel(
+    prior_hbm, degree_hbm, out_hbm, in_hbm, seeds_hbm,
+    scaled_ref, out_ref, in_ref, seeds_ref, prior_ref, degree_ref, arrived,
+):
+    moves = (
+        (prior_hbm, prior_ref), (degree_hbm, degree_ref),
+        (out_hbm, out_ref), (in_hbm, in_ref), (seeds_hbm, seeds_ref),
+    )
     copies = [
         pltpu.make_async_copy(source, place, arrived.at[index])
-        for index, (source, place) in enumerate(((prior_hbm, prior_ref), (degree_hbm, degree_ref)))
+        for index, (source, place) in enumerate(moves)
     ]
     for copy in copies:
         copy.start()
-    for copy in copies:
+    for copy in copies[:2]:
         copy.wait()
     scaled_ref[...] = (prior_ref[...] / degree_ref[...].astype(jnp.float32)).astype(jnp.bfloat16)
+    for copy in copies[2:]:
+        copy.wait()
 
 
 def sum_kernel(
-    rows, cols, owned_blocks, scaled_ref, count_ref, tiles_ref, out_hbm, in_hbm, seeds_hbm,
-    weight_ref, restart_ref, buffer, total, out_ref, in_ref, seeds_ref, arrived, small,
+    rows, cols, owned_blocks, scaled_ref, count_ref, out_ref, in_ref, tiles_ref, seeds_ref,
+    weight_ref, restart_ref, total,
 ):
-    in_blocks, out_blocks = cols * owned_blocks, rows * owned_blocks
+    in_blocks = cols * owned_blocks
     slots, edge = tiles_ref.shape[2], tiles_ref.shape[3]
-    group_total = arrived.shape[0]
-    group = slots // group_total
     row, col = lax.axis_index("row"), lax.axis_index("col")
 
-    def arrival(index):
-        span = pl.ds(index * group, group)
-        return pltpu.make_async_copy(tiles_ref.at[0, 0, span], buffer.at[span], arrived.at[index])
-
-    copies = [
-        pltpu.make_async_copy(source, place, small.at[index])
-        for index, (source, place) in enumerate(
-            ((out_hbm, out_ref), (in_hbm, in_ref), (seeds_hbm, seeds_ref))
-        )
-    ]
-    for copy in copies:
-        copy.start()
-    for index in range(min(FLIGHT, group_total)):
-        arrival(index).start()
-
-    buffer[slots] = jnp.zeros((edge, edge), jnp.bfloat16)
     total[...] = jnp.zeros(total.shape, jnp.float32)
 
-    for copy in copies:
-        copy.wait()
     seed_total, sets = seeds_ref.shape
     owned = owned_blocks * edge
     vertex = lax.broadcasted_iota(jnp.int32, (owned, sets), 0) + (row * cols + col) * owned
@@ -107,36 +94,25 @@
     restart_ref[...] = (1.0 - damping) * restart.T
 
     occupied = count_ref[0, 0]
-
-    def add_group(index, carry):
-        arrival(index).wait()
-
-        @pl.when(index + FLIGHT < group_total)
-        def _():
-            arrival(index + FLIGHT).start()
-
-        first = index * group
-
-        def add_tiles(step, carry):
-            at = first + step * UNROLL
-            places = []
-            for lane in range(UNROLL):
-                slot = at + lane
-                pair = out_ref[0, 0, slot] * in_blocks + in_ref[0, 0, slot]
-                places.append((lane % LANES, pair, jnp.where(slot < occupied, slot, slots)))
-            for start in range(0, UNROLL, 2):
-                sums = [
-                    (lane, pair, total[lane, pair] + buffer[used].astype(jnp.float32))
-                    for lane, pair, used in places[start:start + 2]
-                ]
-                for lane, pair, value in sums:
-                    total[lane, pair] = value
-            return carry
-
-        here = jnp.clip(occupied - first, 0, group)
-        return lax.fori_loop(0, (here + UNROLL - 1) // UNROLL, add_tiles, carry)
-
-    lax.fori_loop(0, group_total, add_group, 0)
+    spare = total.shape[1] - 1
+
+    def add_tiles(step, carry):
+        at = step * UNROLL
+        places = []
+        for lane in range(UNROLL):
+            slot = at + lane
+            pair = out_ref[0, 0, slot] * in_blocks + in_ref[0, 0, slot]
+            places.append((lane % LANES, jnp.where(slot < occupied, pair, spare), slot))
+        for start in range(0, UNROLL, 2):
+            sums = [
+                (lane, pair, total[lane, pair] + tiles_ref[0, 0, slot].astype(jnp.float32))
+                for lane, pair, slot in places[start:start + 2]
+            ]
+            for lane, pair, value in sums:
+                total[lane, pair] = value
+        return carry
+
+    lax.fori_loop(0, (occupied + UNROLL - 1) // UNROLL, add_tiles, 0)
 
     for place in range(rows):
         owner = row ^ place if rows == 2 else place
@@ -189,23 +165,28 @@
     slots, edge = tiles.shape[2], tiles.shape[3]
     owned_blocks = owned // edge
     in_blocks, out_blocks = cols * owned_blocks, rows * owned_blocks
-    group = math.gcd(slots, 32)
     degree = out_degree.reshape(1, owned)
     low = jnp.bfloat16
 
-    scaled = call(
+    scaled, out_ids, in_ids, seeds = call(
         scale_kernel,
-        jax.ShapeDtypeStruct((sets, owned), low),
+        [
+            jax.ShapeDtypeStruct((sets, owned), low),
+            pltpu.SMEM(tile_out.shape, jnp.int32),
+            pltpu.SMEM(tile_in.shape, jnp.int32),
+            jax.ShapeDtypeStruct((seed_ids.shape[1], sets), jnp.int32),
+        ],
         "scale",
-        in_specs=[HBM, HBM],
-        out_specs=VMEM,
+        in_specs=[HBM] * 5,
+        out_specs=[VMEM, SMEM, SMEM, VMEM],
         scratch_shapes=[
             pltpu.VMEM((sets, owned), jnp.float32),
             pltpu.VMEM((1, owned), jnp.int32),
-            pltpu.SemaphoreType.DMA((2,)),
+            pltpu.SemaphoreType.DMA((5,)),
         ],
+        flops=16 * slots * edge**3,
         size=6 * sets * owned,
-    )(*in_hbm(prior, degree))
+    )(*in_hbm(prior, degree, tile_out, tile_in, seed_ids.T))
 
     def spread(value):
         return [value] + [from_column(value, cols, offset) for offset in range(cols - 1, 0, -1)][::-1]
@@ -219,21 +200,16 @@
             jax.ShapeDtypeStruct((sets, owned), jnp.float32),
         ],
         "sum_tiles",
-        in_specs=[ANY, SMEM] + [HBM] * 4,
+        in_specs=[ANY] + [SMEM] * 3 + [VMEM] * 2,
         out_specs=[VMEM] * 2,
-        scratch_shapes=[
-            pltpu.VMEM((slots + 1, edge, edge), low),
-            pltpu.VMEM((LANES, out_blocks * in_blocks, edge, edge), jnp.float32),
-            pltpu.SMEM(tile_out.shape, jnp.int32),
-            pltpu.SMEM(tile_in.shape, jnp.int32),
-            pltpu.VMEM((seed_ids.shape[1], sets), jnp.int32),
-            pltpu.SemaphoreType.DMA((slots // group,)),
-            pltpu.SemaphoreType.DMA((3,)),
-        ],
+        scratch_shapes=[pltpu.VMEM((LANES, out_blocks * in_blocks + 1, edge, edge), jnp.float32)],
         vmem=TILES_VMEM,
         flops=slots * edge * edge,
         size=2 * slots * edge * edge,
-    )(scaled, tile_count, *in_hbm(tiles, tile_out, tile_in, seed_ids.T))
+    )(
+        scaled, tile_count, out_ids, in_ids,
+        tiles, seeds,
+    )
 
     for round_index in range(ITERATIONS):
         last = round_index == ITERATIONS - 1

time: 23.7 us -> 21.3 us (0.90)
  Pallas kernels: 8.08 us -> 4.04 us
  waiting for transfers between devices: 5.71 us -> 7.6 us
    pallas_call x1, Pallas kernels: 6.05 us -> 1.83 us  [local(): call(functools.partial(sum_kernel, rows, cols, owned_blocks), [jax.ShapeD...]
    ppermute x6, waiting for transfers between devices: 3.22 us -> 5.11 us  [from_column(): lax.ppermute(value, 'col', [(partner(col, offset, cols), col) for col in...]
  transfers between devices with their start and end apart: 8 -> 8, of which waited for: 5 -> 7; matrix products, arithmetic and copies ran while one was open for 0% -> 0% of each run, Pallas kernels for 26% -> 9%
where the time goes in v5:
time: 21.3 us; the launch traced here: 21.2 us
  starting transfers between devices  8.78 us (41%)
  waiting for transfers between devices  7.6 us (36%)
  Pallas kernels  4.04 us (19%)
  between operations  0.73 us (3%)
    ppermute x6, starting transfers between devices, from_column(): lax.ppermute(value, 'col', [(partner(col, offset, cols), col) for col in...  8.64 us
    ppermute x6, waiting for transfers between devices, from_column(): lax.ppermute(value, 'col', [(partner(col, offset, cols), col) for col in...  5.11 us
    ppermute x2, waiting for transfers between devices, swap_rows(): return lax.ppermute(value, 'row', [(0, 1), (1, 0)])  2.48 us
    pallas_call x1, Pallas kernels, local(): call(functools.partial(sum_kernel, rows, cols, owned_blocks), [jax.ShapeD...  1.83 us
    pallas_call x1, Pallas kernels, local(): call(scale_kernel, [jax.ShapeDtypeStruct((sets, owned), low), pltpu.SMEM(...  1.07 us
    pallas_call x2, Pallas kernels, local(): call(functools.partial(finish_kernel, last), piece if last else jax.Shape...  0.67 us
    pallas_call x2, Pallas kernels, local(): call(functools.partial(product_kernel, rows, cols), [piece] * 2 if rows =...  0.47 us
  transfers between devices with their start and end apart: 8, of which 7 were waited for; matrix products, arithmetic and copies ran while one was open for 0% of the time, Pallas kernels for 9%

profile of v5, /device:TPU:0, one launch (start us, length us, event | category | flops | bytes accessed | tf_op | source)
XLA Modules:
  0.0 21.2 jit_solution(14000738368368212933)
XLA Ops:
  0.0 0.0 copy-start
  0.0 1.1 %scale.1 = (bf16[128,128]{1,0:T(8,128)(2,1)S(1)}, s32[1,1,384]{2,1,0:T(1,128)S(4)}, s32[1,1,384]{2,1,0:T(1,128)S(4)}, s32[16,128]{1,0:T(8,128)S(1)}) custom-call(f32[128,128]{1,0:T(8,128)} %prior_hbm.1, s32[1,128]{1,0:T(1,128)} %bitcast.2, s32[1,1,384]{2,1,0:T(1,128)} %out_hbm.1, s32[1,1,384]{2,1,0:T(1,128)} %in_hbm.1, s32[16,128]{1,0:T(8,128)} %bitcast.5), custom_call_target="tpu_custom_call" | custom-call | flops 12884901888 | bytes 98304 | tf_op jit(solution)/shard_map/scale/pallas_call | solution.py:171
  1.1 0.0 copy-start.1
  1.1 4.0 %collective-permute-start.2 = (bf16[128,128]{1,0:T(8,128)(2,1)S(1)}, bf16[128,128]{1,0:T(8,128)(2,1)S(1)}, u32[]{:S(2)}, u32[]{:S(2)}) collective-permute-start(bf16[128,128]{1,0:T(8,128)(2,1)S(1)} %get-tuple-element.15.scaled_ref.refs_0_), channel_id=1, source_target_pairs={{12,0},{8,4},{4,8},{0,12},{13,1},{9,5},{5,9},{1,13},{14,2},{10,6},... | collective-permute-start | bytes 98312 | tf_op jit(solution)/shard_map/ppermute | solution.py:50
  5.0 0.5 %collective-permute-start.1 = (bf16[128,128]{1,0:T(8,128)(2,1)S(1)}, bf16[128,128]{1,0:T(8,128)(2,1)S(1)}, u32[]{:S(2)}, u32[]{:S(2)}) collective-permute-start(bf16[128,128]{1,0:T(8,128)(2,1)S(1)} %get-tuple-element.15.scaled_ref.refs_0_), channel_id=1, source_target_pairs={{8,0},{12,4},{0,8},{4,12},{9,1},{13,5},{1,9},{5,13},{10,2},{14,6},... | collective-permute-start | bytes 98312 | tf_op jit(solution)/shard_map/ppermute | solution.py:50
  5.6 0.1 collective-permute-start
  6.3 0.0 copy-done
  6.4 1.8 %sum_tiles.1 = (bf16[4,256,256]{2,1,0:T(8,128)(2,1)S(1)}, f32[128,128]{1,0:T(8,128)S(1)}) custom-call(bf16[128,128]{1,0:T(8,128)(2,1)S(1)} %get-tuple-element.15.scaled_ref.refs_0_, s32[1,1]{1,0:T(1,128)S(6)} %copy.8.count_ref, s32[1,1,384]{2,1,0:T(1,128)S(4)} %get-tuple-element.16.out_ref, s32[1,1,384]{2,1,0:T(1,128)S(4)} %get-tuple-element.17.in_ref, ...), custom_call_target="tpu_custom_call" | custom-call | flops 6291456 | bytes 12582912 | tf_op jit(solution)/shard_map/sum_tiles/pallas_call | solution.py:196
  8.2 0.0 collective-permute-done.2.refs_3_
  8.2 0.8 %collective-permute-done.1.refs_2_ = bf16[128,128]{1,0:T(8,128)(2,1)S(1)} collective-permute-done((bf16[128,128]{1,0:T(8,128)(2,1)S(1)}, bf16[128,128]{1,0:T(8,128)(2,1)S(1)}, u32[]{:S(2)}, u32[]{:S(2)}) %collective-permute-start.1) | collective-permute-done | bytes 32800 | tf_op jit(solution)/shard_map/ppermute | solution.py:50
  9.0 0.5 %collective-permute-done.refs_1_ = bf16[128,128]{1,0:T(8,128)(2,1)S(1)} collective-permute-done((bf16[128,128]{1,0:T(8,128)(2,1)S(1)}, bf16[128,128]{1,0:T(8,128)(2,1)S(1)}, u32[]{:S(2)}, u32[]{:S(2)}) %collective-permute-start) | collective-permute-done | bytes 32800 | tf_op jit(solution)/shard_map/ppermute | solution.py:50
  9.5 0.2 %product.2 = (f32[128,128]{1,0:T(8,128)S(1)}, f32[128,128]{1,0:T(8,128)S(1)}) custom-call(bf16[128,128]{1,0:T(8,128)(2,1)S(1)} %get-tuple-element.15.scaled_ref.refs_0_, bf16[128,128]{1,0:T(8,128)(2,1)S(1)} %collective-permute-done.refs_1_, bf16[128,128]{1,0:T(8,128)(2,1)S(1)} %collective-permute-done.1.refs_2_, ...), custom_call_target="tpu_custom_call" | custom-call | flops 67108864 | bytes 655360 | tf_op jit(solution)/shard_map/product/pallas_call | solution.py:217
  9.7 0.1 collective-permute-start.3
  9.8 1.2 %collective-permute-done.3.refs_1_ = f32[128,128]{1,0:T(8,128)S(1)} collective-permute-done((f32[128,128]{1,0:T(8,128)S(1)}, f32[128,128]{1,0:T(8,128)S(1)}, u32[]{:S(2)}, u32[]{:S(2)}) %collective-permute-start.3) | collective-permute-done | bytes 65568 | tf_op jit(solution)/shard_map/ppermute | solution.py:54
  11.0 0.0 copy-done.1
  11.1 3.4 %collective-permute-start.6 = (bf16[128,128]{1,0:T(8,128)(2,1)S(1)}, bf16[128,128]{1,0:T(8,128)(2,1)S(1)}, u32[]{:S(2)}, u32[]{:S(2)}) collective-permute-start(bf16[128,128]{1,0:T(8,128)(2,1)S(1)} %next.1.refs_0_), channel_id=1, source_target_pairs={{12,0},{8,4},{4,8},{0,12},{13,1},{9,5},{5,9},{1,13},{14,2},{10,6},... | collective-permute-start | bytes 98312 | tf_op jit(solution)/shard_map/ppermute | solution.py:50
  14.5 0.6 %collective-permute-start.5 = (bf16[128,128]{1,0:T(8,128)(2,1)S(1)}, bf16[128,128]{1,0:T(8,128)(2,1)S(1)}, u32[]{:S(2)}, u32[]{:S(2)}) collective-permute-start(bf16[128,128]{1,0:T(8,128)(2,1)S(1)} %next.1.refs_0_), channel_id=1, source_target_pairs={{8,0},{12,4},{0,8},{4,12},{9,1},{13,5},{1,9},{5,13},{10,2},{14,6},... | collective-permute-start | bytes 98312 | tf_op jit(solution)/shard_map/ppermute | solution.py:50
  15.0 0.1 collective-permute-start.4
  15.1 1.3 %collective-permute-done.6.refs_3_ = bf16[128,128]{1,0:T(8,128)(2,1)S(1)} collective-permute-done((bf16[128,128]{1,0:T(8,128)(2,1)S(1)}, bf16[128,128]{1,0:T(8,128)(2,1)S(1)}, u32[]{:S(2)}, u32[]{:S(2)}) %collective-permute-start.6) | collective-permute-done | bytes 32800 | tf_op jit(solution)/shard_map/ppermute | solution.py:50
  16.4 2.0 %collective-permute-done.5.refs_2_ = bf16[128,128]{1,0:T(8,128)(2,1)S(1)} collective-permute-done((bf16[128,128]{1,0:T(8,128)(2,1)S(1)}, bf16[128,128]{1,0:T(8,128)(2,1)S(1)}, u32[]{:S(2)}, u32[]{:S(2)}) %collective-permute-start.5) | collective-permute-done | bytes 32800 | tf_op jit(solution)/shard_map/ppermute | solution.py:50
  18.4 0.6 %collective-permute-done.4.refs_1_ = bf16[128,128]{1,0:T(8,128)(2,1)S(1)} collective-permute-done((bf16[128,128]{1,0:T(8,128)(2,1)S(1)}, bf16[128,128]{1,0:T(8,128)(2,1)S(1)}, u32[]{:S(2)}, u32[]{:S(2)}) %collective-permute-start.4) | collective-permute-done | bytes 32800 | tf_op jit(solution)/shard_map/ppermute | solution.py:50
  18.9 0.2 %product.3 = (f32[128,128]{1,0:T(8,128)S(1)}, f32[128,128]{1,0:T(8,128)S(1)}) custom-call(bf16[128,128]{1,0:T(8,128)(2,1)S(1)} %next.1.refs_0_, bf16[128,128]{1,0:T(8,128)(2,1)S(1)} %collective-permute-done.4.refs_1_, bf16[128,128]{1,0:T(8,128)(2,1)S(1)} %collective-permute-done.5.refs_2_, bf16[128,128]{1,0:T(8,128)(2,1)S(1)} %collective-permute-done.6.refs_3_, ...), custom_call_target="tpu_custom_call" | custom-call | flops 67108864 | bytes 655360 | tf_op jit(solution)/shard_map/product/pallas_call | solution.py:217
  19.2 0.1 collective-permute-start.7
  19.3 1.2 %collective-permute-done.7.refs_1_ = f32[128,128]{1,0:T(8,128)S(1)} collective-permute-done((f32[128,128]{1,0:T(8,128)S(1)}, f32[128,128]{1,0:T(8,128)S(1)}, u32[]{:S(2)}, u32[]{:S(2)}) %collective-permute-start.7) | collective-permute-done | bytes 65568 | tf_op jit(solution)/shard_map/ppermute | solution.py:54
  20.5 0.7 %last.1 = f32[128,128]{1,0:T(8,128)} custom-call(f32[128,128]{1,0:T(8,128)S(1)} %get-tuple-element.23.refs_0_, f32[128,128]{1,0:T(8,128)S(1)} %collective-permute-done.7.refs_1_, f32[128,128]{1,0:T(8,128)S(1)} %get-tuple-element.22.refs_2_, s32[1,128]{1,0:T(1,128)S(1)} %bitcast.4), custom_call_target="tpu_custom_call" | custom-call | bytes 196608 | tf_op jit(solution)/shard_map/last/pallas_call | solution.py:230
  (1 shorter events, 0.0 us)
Async XLA Ops:
  0.0 6.3 %copy-start = (bf16[1,1,384,128,128]{4,3,2,1,0:T(8,128)(2,1)S(1)}, bf16[1,1,384,128,128]{4,3,2,1,0:T(8,128)(2,1)}, u32[]{:S(2)}) copy-start(bf16[1,1,384,128,128]{4,3,2,1,0:T(8,128)(2,1)} %tiles_ref.1) | copy-start | bytes 37748740
  1.1 10.0 %copy-start.1 = (s32[128]{0:T(128)S(1)}, s32[128]{0:T(128)}, u32[]{:S(2)}) copy-start(s32[128]{0:T(128)} %param.11) | copy-start | bytes 1540
  1.1 7.1 %collective-permute-start.2 = (bf16[128,128]{1,0:T(8,128)(2,1)S(1)}, bf16[128,128]{1,0:T(8,128)(2,1)S(1)}, u32[]{:S(2)}, u32[]{:S(2)}) collective-permute-start(bf16[128,128]{1,0:T(8,128)(2,1)S(1)} %get-tuple-element.15.scaled_ref.refs_0_), channel_id=1, source_target_pairs={{12,0},{8,4},{4,8},{0,12},{13,1},{9,5},{5,9},{1,13},{14,2},{10,6},... | collective-permute-start | bytes 98312 | tf_op jit(solution)/shard_map/ppermute | solution.py:50
  5.0 3.9 %collective-permute-start.1 = (bf16[128,128]{1,0:T(8,128)(2,1)S(1)}, bf16[128,128]{1,0:T(8,128)(2,1)S(1)}, u32[]{:S(2)}, u32[]{:S(2)}) collective-permute-start(bf16[128,128]{1,0:T(8,128)(2,1)S(1)} %get-tuple-element.15.scaled_ref.refs_0_), channel_id=1, source_target_pairs={{8,0},{12,4},{0,8},{4,12},{9,1},{13,5},{1,9},{5,13},{10,2},{14,6},... | collective-permute-start | bytes 98312 | tf_op jit(solution)/shard_map/ppermute | solution.py:50
  5.6 3.9 %collective-permute-start = (bf16[128,128]{1,0:T(8,128)(2,1)S(1)}, bf16[128,128]{1,0:T(8,128)(2,1)S(1)}, u32[]{:S(2)}, u32[]{:S(2)}) collective-permute-start(bf16[128,128]{1,0:T(8,128)(2,1)S(1)} %get-tuple-element.15.scaled_ref.refs_0_), channel_id=1, source_target_pairs={{4,0},{0,4},{12,8},{8,12},{5,1},{1,5},{13,9},{9,13},{6,2},{2,6},{1... | collective-permute-start | bytes 98312 | tf_op jit(solution)/shard_map/ppermute | solution.py:50
  9.7 1.3 %collective-permute-start.3 = (f32[128,128]{1,0:T(8,128)S(1)}, f32[128,128]{1,0:T(8,128)S(1)}, u32[]{:S(2)}, u32[]{:S(2)}) collective-permute-start(f32[128,128]{1,0:T(8,128)S(1)} %get-tuple-element.21), channel_id=1, source_target_pairs={{0,16},{16,0},{1,17},{17,1},{2,18},{18,2},{3,19},{19,3},{4,20},{20... | collective-permute-start | bytes 196616 | tf_op jit(solution)/shard_map/ppermute | solution.py:54
  11.1 5.3 %collective-permute-start.6 = (bf16[128,128]{1,0:T(8,128)(2,1)S(1)}, bf16[128,128]{1,0:T(8,128)(2,1)S(1)}, u32[]{:S(2)}, u32[]{:S(2)}) collective-permute-start(bf16[128,128]{1,0:T(8,128)(2,1)S(1)} %next.1.refs_0_), channel_id=1, source_target_pairs={{12,0},{8,4},{4,8},{0,12},{13,1},{9,5},{5,9},{1,13},{14,2},{10,6},... | collective-permute-start | bytes 98312 | tf_op jit(solution)/shard_map/ppermute | solution.py:50
  14.5 3.9 %collective-permute-start.5 = (bf16[128,128]{1,0:T(8,128)(2,1)S(1)}, bf16[128,128]{1,0:T(8,128)(2,1)S(1)}, u32[]{:S(2)}, u32[]{:S(2)}) collective-permute-start(bf16[128,128]{1,0:T(8,128)(2,1)S(1)} %next.1.refs_0_), channel_id=1, source_target_pairs={{8,0},{12,4},{0,8},{4,12},{9,1},{13,5},{1,9},{5,13},{10,2},{14,6},... | collective-permute-start | bytes 98312 | tf_op jit(solution)/shard_map/ppermute | solution.py:50
  15.0 3.9 %collective-permute-start.4 = (bf16[128,128]{1,0:T(8,128)(2,1)S(1)}, bf16[128,128]{1,0:T(8,128)(2,1)S(1)}, u32[]{:S(2)}, u32[]{:S(2)}) collective-permute-start(bf16[128,128]{1,0:T(8,128)(2,1)S(1)} %next.1.refs_0_), channel_id=1, source_target_pairs={{4,0},{0,4},{12,8},{8,12},{5,1},{1,5},{13,9},{9,13},{6,2},{2,6},{1... | collective-permute-start | bytes 98312 | tf_op jit(solution)/shard_map/ppermute | solution.py:50
  19.2 1.3 %collective-permute-start.7 = (f32[128,128]{1,0:T(8,128)S(1)}, f32[128,128]{1,0:T(8,128)S(1)}, u32[]{:S(2)}, u32[]{:S(2)}) collective-permute-start(f32[128,128]{1,0:T(8,128)S(1)} %get-tuple-element.24), channel_id=1, source_target_pairs={{0,16},{16,0},{1,17},{17,1},{2,18},{18,2},{3,19},{19,3},{4,20},{20... | collective-permute-start | bytes 196616 | tf_op jit(solution)/shard_map/ppermute | solution.py:54

commit v6 on v5

--- a/solution.py
+++ b/solution.py
@@ -1,4 +1,5 @@
 import functools
+import math
 
 import jax
 import jax.numpy as jnp
@@ -75,35 +76,46 @@
         copy.wait()
 
 
+def first_at_least(ids_ref, block, end):
+    def halve(step, bounds):
+        low, high = bounds
+        middle = (low + high) // 2
+        below = ids_ref[0, 0, jnp.minimum(middle, ids_ref.shape[2] - 1)] < block
+        searching = low < high
+        return (
+            jnp.where(searching & below, middle + 1, low),
+            jnp.where(searching & ~below, middle, high),
+        )
+
+    return lax.fori_loop(0, ids_ref.shape[2].bit_length(), halve, (jnp.int32(0), end))[0]
+
+
 def sum_kernel(
-    rows, cols, owned_blocks, scaled_ref, count_ref, out_ref, in_ref, tiles_ref, seeds_ref,
-    weight_ref, restart_ref, total,
+    rows, cols, owned_blocks, place, after_ref, count_ref, out_ref, in_ref, tiles_ref, weight_ref, total
 ):
     in_blocks = cols * owned_blocks
     slots, edge = tiles_ref.shape[2], tiles_ref.shape[3]
-    row, col = lax.axis_index("row"), lax.axis_index("col")
+    owned = owned_blocks * edge
+    spare = total.shape[1] - 1
+    unroll = math.gcd(slots, UNROLL)
 
     total[...] = jnp.zeros(total.shape, jnp.float32)
 
-    seed_total, sets = seeds_ref.shape
-    owned = owned_blocks * edge
-    vertex = lax.broadcasted_iota(jnp.int32, (owned, sets), 0) + (row * cols + col) * owned
-    restart = jnp.zeros((owned, sets), jnp.float32)
-    for seed in range(seed_total):
-        restart += (seeds_ref[seed:seed + 1, :] == vertex).astype(jnp.float32)
-    restart_ref[...] = (1.0 - damping) * restart.T
-
-    occupied = count_ref[0, 0]
-    spare = total.shape[1] - 1
+    first_block, begin, end = 0, 0, count_ref[0, 0]
+    if place is not None:
+        first_block = partner(lax.axis_index("row"), place, rows) * owned_blocks
+        begin = first_at_least(out_ref, first_block, end)
+        end = first_at_least(out_ref, first_block + owned_blocks, end)
 
     def add_tiles(step, carry):
-        at = step * UNROLL
+        at = step * unroll
         places = []
-        for lane in range(UNROLL):
+        for lane in range(unroll):
             slot = at + lane
-            pair = out_ref[0, 0, slot] * in_blocks + in_ref[0, 0, slot]
-            places.append((lane % LANES, jnp.where(slot < occupied, pair, spare), slot))
-        for start in range(0, UNROLL, 2):
+            pair = (out_ref[0, 0, slot] - first_block) * in_blocks + in_ref[0, 0, slot]
+            used = (slot >= begin) & (slot < end)
+            places.append((lane % LANES, jnp.where(used, pair, spare), slot))
+        for start in range(0, unroll, 2):
             sums = [
                 (lane, pair, total[lane, pair] + tiles_ref[0, 0, slot].astype(jnp.float32))
                 for lane, pair, slot in places[start:start + 2]
@@ -112,24 +124,33 @@
                 total[lane, pair] = value
         return carry
 
-    lax.fori_loop(0, (occupied + UNROLL - 1) // UNROLL, add_tiles, 0)
-
-    for place in range(rows):
-        owner = row ^ place if rows == 2 else place
-        for block in range(owned_blocks):
-            columns = slice(place * owned + block * edge, place * owned + (block + 1) * edge)
-            for source in range(in_blocks):
-                pair = (owner * owned_blocks + block) * in_blocks + source
-                value = (total[0, pair] + total[1, pair]) + (total[2, pair] + total[3, pair])
-                high = value.astype(jnp.bfloat16)
-                low = (value - high.astype(jnp.float32)).astype(jnp.bfloat16)
-                lines = source // owned_blocks, source % owned_blocks * edge
-                weight_ref[lines[0], lines[1]:lines[1] + edge, columns] = high
-                weight_ref[lines[0], owned + lines[1]:owned + lines[1] + edge, columns] = low
-
-
-def product_kernel(rows, cols, *refs):
-    parts, (weight_ref, *result_refs) = refs[:cols], refs[cols:]
+    lax.fori_loop(begin // unroll, (end + unroll - 1) // unroll, add_tiles, 0)
+
+    for block in range(spare // in_blocks):
+        columns = slice(block * edge, (block + 1) * edge)
+        for source in range(in_blocks):
+            pair = block * in_blocks + source
+            value = (total[0, pair] + total[1, pair]) + (total[2, pair] + total[3, pair])
+            high = value.astype(jnp.bfloat16)
+            low = (value - high.astype(jnp.float32)).astype(jnp.bfloat16)
+            column, line = source // owned_blocks, source % owned_blocks * edge
+            weight_ref[column, line:line + edge, columns] = high
+            weight_ref[column, owned + line:owned + line + edge, columns] = low
+
+
+def restart_kernel(rows, cols, after_ref, seeds_ref, restart_ref):
+    seed_total, sets = seeds_ref.shape
+    owned = restart_ref.shape[1]
+    first = (lax.axis_index("row") * cols + lax.axis_index("col")) * owned
+    vertex = lax.broadcasted_iota(jnp.int32, (owned, sets), 0) + first
+    restart = jnp.zeros((owned, sets), jnp.float32)
+    for seed in range(seed_total):
+        restart += (seeds_ref[seed:seed + 1, :] == vertex).astype(jnp.float32)
+    restart_ref[...] = (1.0 - damping) * restart.T
+
+
+def product_kernel(cols, after, *refs):
+    *parts, weight_ref, result_ref = refs[after:]
     col = lax.axis_index("col")
     incoming = None
     for offset in range(cols):
@@ -140,13 +161,12 @@
             preferred_element_type=jnp.float32,
         )
         incoming = term if incoming is None else incoming + term
-    owned = incoming.shape[1] // rows
-    if len(result_refs) == 1:
-        for place in range(rows):
-            result_refs[0][place] = incoming[:, place * owned:(place + 1) * owned]
+    if len(result_ref.shape) == 2:
+        result_ref[...] = incoming
     else:
-        for place in range(rows):
-            result_refs[place][...] = incoming[:, place * owned:(place + 1) * owned]
+        owned = result_ref.shape[2]
+        for place in range(result_ref.shape[0]):
+            result_ref[place] = incoming[:, place * owned:(place + 1) * owned]
 
 
 def finish_kernel(last, *refs):
@@ -193,48 +213,69 @@
 
     parts = spread(scaled)
 
-    weight, restart = call(
-        functools.partial(sum_kernel, rows, cols, owned_blocks),
-        [
-            jax.ShapeDtypeStruct((cols, 2 * owned, rows * owned), low),
+    def add_up(place, after):
+        pair_total = in_blocks * (owned_blocks if place is not None else out_blocks)
+        return call(
+            functools.partial(sum_kernel, rows, cols, owned_blocks, place),
+            jax.ShapeDtypeStruct((cols, 2 * owned, pair_total // in_blocks * edge), low),
+            "sum_tiles",
+            in_specs=[ANY] + [SMEM] * 3 + [VMEM],
+            out_specs=VMEM,
+            scratch_shapes=[pltpu.VMEM((LANES, pair_total + 1, edge, edge), jnp.float32)],
+            vmem=TILES_VMEM,
+            flops=slots * edge * edge,
+            size=2 * slots * edge * edge,
+        )(after, tile_count, out_ids, in_ids, tiles)
+
+    def multiply(parts, weight, after=()):
+        shape = (sets, owned) if weight.shape[2] == owned else (rows, sets, owned)
+        return call(
+            functools.partial(product_kernel, cols, len(after)),
+            jax.ShapeDtypeStruct(shape, jnp.float32),
+            "product",
+            in_specs=[ANY] * len(after) + [VMEM] * (cols + 1),
+            out_specs=VMEM,
+            flops=2 * sets * weight.size,
+            size=2 * weight.size,
+        )(*after, *parts, weight)
+
+    def count_restart(after):
+        return call(
+            functools.partial(restart_kernel, rows, cols),
             jax.ShapeDtypeStruct((sets, owned), jnp.float32),
-        ],
-        "sum_tiles",
-        in_specs=[ANY] + [SMEM] * 3 + [VMEM] * 2,
-        out_specs=[VMEM] * 2,
-        scratch_shapes=[pltpu.VMEM((LANES, out_blocks * in_blocks + 1, edge, edge), jnp.float32)],
-        vmem=TILES_VMEM,
-        flops=slots * edge * edge,
-        size=2 * slots * edge * edge,
-    )(
-        scaled, tile_count, out_ids, in_ids,
-        tiles, seeds,
-    )
-
+            "restart",
+            in_specs=[ANY, VMEM],
+            out_specs=VMEM,
+            flops=2 * sets * owned * seed_ids.shape[1],
+            size=4 * sets * owned,
+        )(after, seeds)
+
+    def finish(incoming, restart, last):
+        return call(
+            functools.partial(finish_kernel, last),
+            jax.ShapeDtypeStruct((sets, owned), jnp.float32 if last else low),
+            "last" if last else "next",
+            in_specs=[VMEM] * (len(incoming) + 2),
+            out_specs=VMEM,
+            size=12 * sets * owned,
+        )(*incoming, restart, degree)
+
+    paired = rows == 2
+    weight = add_up(1 if paired else None, scaled)
     for round_index in range(ITERATIONS):
         last = round_index == ITERATIONS - 1
-        piece = jax.ShapeDtypeStruct((sets, owned), jnp.float32)
-        partial_value = call(
-            functools.partial(product_kernel, rows, cols),
-            [piece] * 2 if rows == 2 else jax.ShapeDtypeStruct((rows, sets, owned), jnp.float32),
-            "product",
-            in_specs=[VMEM] * (cols + 1),
-            out_specs=[VMEM] * 2 if rows == 2 else VMEM,
-            flops=4 * sets * cols * owned * rows * owned,
-            size=2 * cols * owned * (sets + 2 * rows * owned),
-        )(*parts, weight)
-        if rows == 2:
-            incoming = (partial_value[0], swap_rows(partial_value[1]))
+        partial_value = multiply(parts, weight)
+        if paired:
+            received = swap_rows(partial_value)
+            if not round_index:
+                own_weight = add_up(0, partial_value)
+                restart = count_restart(own_weight)
+            incoming = (multiply(parts, own_weight, (partial_value,)), received)
         else:
+            if not round_index:
+                restart = count_restart(weight)
             incoming = (lax.psum_scatter(partial_value, "row", scatter_dimension=0, tiled=False),)
-        value = call(
-            functools.partial(finish_kernel, last),
-            piece if last else jax.ShapeDtypeStruct((sets, owned), low),
-            "last" if last else "next",
-            in_specs=[VMEM] * (len(incoming) + 2),
-            out_specs=VMEM,
-            size=12 * sets * owned,
-        )(*incoming, restart, degree)
+        value = finish(incoming, restart, last)
         if not last:
             parts = spread(value)
     return value

time: 21.3 us -> 21.2 us (level)
  Pallas kernels: 4.04 us -> 7.09 us
  waiting for transfers between devices: 7.6 us -> 4.96 us
  starting transfers between devices: 8.78 us -> 8.24 us
    pallas_call x5 -> x9, Pallas kernels: 2.97 us -> 6.02 us  [the longest x2 4.28 us: add_up(): call(functools.partial(sum_kernel, rows, cols, owned_blocks, place), jax....]
    ppermute x2, waiting for transfers between devices: 2.48 us -> 1.01 us  [swap_rows(): return lax.ppermute(value, 'row', [(0, 1), (1, 0)])]
    ppermute x6, waiting for transfers between devices: 5.11 us -> 3.95 us  [from_column(): lax.ppermute(value, 'col', [(partner(col, offset, cols), col) for col in...]
    ppermute x6, starting transfers between devices: 8.64 us -> 8.1 us  [from_column(): lax.ppermute(value, 'col', [(partner(col, offset, cols), col) for col in...]
  transfers between devices with their start and end apart: 8 -> 8, of which waited for: 7 -> 5; matrix products, arithmetic and copies ran while one was open for 0% -> 0% of each run, Pallas kernels for 9% -> 23%
where the time goes in v6:
time: 21.2 us; the launch traced here: 21.1 us
  starting transfers between devices  8.24 us (39%)
  Pallas kernels  7.09 us (33%)
  waiting for transfers between devices  4.96 us (23%)
  between operations  0.78 us (4%)
    ppermute x6, starting transfers between devices, from_column(): lax.ppermute(value, 'col', [(partner(col, offset, cols), col) for col in...  8.1 us
    pallas_call x2, Pallas kernels, add_up(): call(functools.partial(sum_kernel, rows, cols, owned_blocks, place), jax....  4.28 us
    ppermute x6, waiting for transfers between devices, from_column(): lax.ppermute(value, 'col', [(partner(col, offset, cols), col) for col in...  3.95 us
    pallas_call x1, Pallas kernels, local(): call(scale_kernel, [jax.ShapeDtypeStruct((sets, owned), low), pltpu.SMEM(...  1.07 us
    ppermute x2, waiting for transfers between devices, swap_rows(): return lax.ppermute(value, 'row', [(0, 1), (1, 0)])  1.01 us
    pallas_call x4, Pallas kernels, multiply(): call(functools.partial(product_kernel, cols, len(after)), jax.ShapeDtypeS...  0.89 us
    pallas_call x2, Pallas kernels, finish(): call(functools.partial(finish_kernel, last), jax.ShapeDtypeStruct((sets,...  0.66 us
  transfers between devices with their start and end apart: 8, of which 5 were waited for; matrix products, arithmetic and copies ran while one was open for 0% of the time, Pallas kernels for 23%

profile of v6, /device:TPU:0, one launch (start us, length us, event | category | flops | bytes accessed | tf_op | source)
XLA Modules:
  0.0 21.1 jit_solution(4118950016771245202)
XLA Ops:
  0.0 0.0 copy-start
  0.0 1.1 %scale.1 = (bf16[128,128]{1,0:T(8,128)(2,1)S(1)}, s32[1,1,384]{2,1,0:T(1,128)S(4)}, s32[1,1,384]{2,1,0:T(1,128)S(4)}, s32[16,128]{1,0:T(8,128)S(1)}) custom-call(f32[128,128]{1,0:T(8,128)} %prior_hbm.1, s32[1,128]{1,0:T(1,128)} %bitcast.2, s32[1,1,384]{2,1,0:T(1,128)} %out_hbm.1, s32[1,1,384]{2,1,0:T(1,128)} %in_hbm.1, s32[16,128]{1,0:T(8,128)} %bitcast.5), custom_call_target="tpu_custom_call" | custom-call | flops 12884901888 | bytes 98304 | tf_op jit(solution)/shard_map/scale/pallas_call | solution.py:191
  1.1 3.0 %collective-permute-start = (bf16[128,128]{1,0:T(8,128)(2,1)S(1)}, bf16[128,128]{1,0:T(8,128)(2,1)S(1)}, u32[]{:S(2)}, u32[]{:S(2)}) collective-permute-start(bf16[128,128]{1,0:T(8,128)(2,1)S(1)} %get-tuple-element.9.after_ref.refs_0_.refs_1_), channel_id=1, source_target_pairs={{4,0},{0,4},{12,8},{8,12},{5,1},{1,5},{13,9},{9,13},{6,2},{2,6},{1... | collective-permute-start | bytes 98312 | tf_op jit(solution)/shard_map/ppermute | solution.py:51
  4.1 1.5 %collective-permute-start.1 = (bf16[128,128]{1,0:T(8,128)(2,1)S(1)}, bf16[128,128]{1,0:T(8,128)(2,1)S(1)}, u32[]{:S(2)}, u32[]{:S(2)}) collective-permute-start(bf16[128,128]{1,0:T(8,128)(2,1)S(1)} %get-tuple-element.9.after_ref.refs_0_.refs_1_), channel_id=1, source_target_pairs={{8,0},{12,4},{0,8},{4,12},{9,1},{13,5},{1,9},{5,13},{10,2},{14,6},... | collective-permute-start | bytes 98312 | tf_op jit(solution)/shard_map/ppermute | solution.py:51
  5.6 0.0 collective-permute-start.2
  6.3 0.0 copy-done
  6.3 0.0 copy-start.1
  6.3 2.0 %sum_tiles.2.refs_4_ = bf16[4,256,128]{2,1,0:T(8,128)(2,1)S(1)} custom-call(bf16[128,128]{1,0:T(8,128)(2,1)S(1)} %get-tuple-element.9.after_ref.refs_0_.refs_1_, s32[1,1]{1,0:T(1,128)S(6)} %copy.8.count_ref, s32[1,1,384]{2,1,0:T(1,128)S(4)} %get-tuple-element.10.out_ref, s32[1,1,384]{2,1,0:T(1,128)S(4)} %get-tuple-element.11.in_ref, ...), custom_call_target="tpu_custom_call" | custom-call | flops 6291456 | bytes 12582912 | tf_op jit(solution)/shard_map/sum_tiles/pallas_call | solution.py:218
  8.3 0.0 collective-permute-done.refs_1_.refs_2_
  8.4 0.0 collective-permute-done.1.refs_2_.refs_3_
  8.4 2.1 %collective-permute-done.2.refs_3_.refs_4_ = bf16[128,128]{1,0:T(8,128)(2,1)S(1)} collective-permute-done((bf16[128,128]{1,0:T(8,128)(2,1)S(1)}, bf16[128,128]{1,0:T(8,128)(2,1)S(1)}, u32[]{:S(2)}, u32[]{:S(2)}) %collective-permute-start.2) | collective-permute-done | bytes 32800 | tf_op jit(solution)/shard_map/ppermute | solution.py:51
  10.4 0.2 %product.4.after_ref.refs_0_ = f32[128,128]{1,0:T(8,128)S(1)} custom-call(bf16[128,128]{1,0:T(8,128)(2,1)S(1)} %get-tuple-element.9.after_ref.refs_0_.refs_1_, bf16[128,128]{1,0:T(8,128)(2,1)S(1)} %collective-permute-done.refs_1_.refs_2_, bf16[128,128]{1,0:T(8,128)(2,1)S(1)} %collective-permute-done.1.refs_2_.refs_3_, ...), custom_call_target="tpu_custom_call" | custom-call | flops 33554432 | bytes 262144 | tf_op jit(solution)/shard_map/product/pallas_call | solution.py:232
  10.6 0.1 collective-permute-start.3
  10.7 2.2 %sum_tiles.3.refs_5_.after_ref = bf16[4,256,128]{2,1,0:T(8,128)(2,1)S(1)} custom-call(f32[128,128]{1,0:T(8,128)S(1)} %product.4.after_ref.refs_0_, s32[1,1]{1,0:T(1,128)S(6)} %copy.8.count_ref, s32[1,1,384]{2,1,0:T(1,128)S(4)} %get-tuple-element.10.out_ref, s32[1,1,384]{2,1,0:T(1,128)S(4)} %get-tuple-element.11.in_ref, bf16[1,1,384,128,128]{4,3,2,1,0:T(8,128)(2,1)S(1)} %copy-done), custom_call_target="tpu_custom_call" | custom-call | flops 6291456 | bytes 12582912 | tf_op jit(solution)/shard_map/sum_tiles/pallas_call | solution.py:218
  13.0 0.2 restart.1.refs_2_
  13.2 0.2 %product.5.refs_0_ = f32[128,128]{1,0:T(8,128)S(1)} custom-call(f32[128,128]{1,0:T(8,128)S(1)} %product.4.after_ref.refs_0_, bf16[128,128]{1,0:T(8,128)(2,1)S(1)} %get-tuple-element.9.after_ref.refs_0_.refs_1_, bf16[128,128]{1,0:T(8,128)(2,1)S(1)} %collective-permute-done.refs_1_.refs_2_, bf16[128,128]{1,0:T(8,128)(2,1)S(1)} %collective-permute-done.1.refs_2_.refs_3_, ...), custom_call_target="tpu_custom_call" | custom-call | flops 33554432 | bytes 262144 | tf_op jit(solution)/shard_map/product/pallas_call | solution.py:232
  13.4 0.0 collective-permute-done.3.refs_1_
  13.4 0.0 copy-done.1
  13.4 0.4 %collective-permute-start.4 = (bf16[128,128]{1,0:T(8,128)(2,1)S(1)}, bf16[128,128]{1,0:T(8,128)(2,1)S(1)}, u32[]{:S(2)}, u32[]{:S(2)}) collective-permute-start(bf16[128,128]{1,0:T(8,128)(2,1)S(1)} %next.1.refs_0_.refs_1_), channel_id=1, source_target_pairs={{4,0},{0,4},{12,8},{8,12},{5,1},{1,5},{13,9},{9,13},{6,2},{2,6},{1... | collective-permute-start | bytes 98312 | tf_op jit(solution)/shard_map/ppermute | solution.py:51
  13.8 0.0 collective-permute-start.5
  13.8 3.2 %collective-permute-start.6 = (bf16[128,128]{1,0:T(8,128)(2,1)S(1)}, bf16[128,128]{1,0:T(8,128)(2,1)S(1)}, u32[]{:S(2)}, u32[]{:S(2)}) collective-permute-start(bf16[128,128]{1,0:T(8,128)(2,1)S(1)} %next.1.refs_0_.refs_1_), channel_id=1, source_target_pairs={{12,0},{8,4},{4,8},{0,12},{13,1},{9,5},{5,9},{1,13},{14,2},{10,6},... | collective-permute-start | bytes 98312 | tf_op jit(solution)/shard_map/ppermute | solution.py:51
  17.0 0.4 %collective-permute-done.4.refs_1_.refs_2_ = bf16[128,128]{1,0:T(8,128)(2,1)S(1)} collective-permute-done((bf16[128,128]{1,0:T(8,128)(2,1)S(1)}, bf16[128,128]{1,0:T(8,128)(2,1)S(1)}, u32[]{:S(2)}, u32[]{:S(2)}) %collective-permute-start.4) | collective-permute-done | bytes 32800 | tf_op jit(solution)/shard_map/ppermute | solution.py:51
  17.4 0.3 %collective-permute-done.5.refs_2_.refs_3_ = bf16[128,128]{1,0:T(8,128)(2,1)S(1)} collective-permute-done((bf16[128,128]{1,0:T(8,128)(2,1)S(1)}, bf16[128,128]{1,0:T(8,128)(2,1)S(1)}, u32[]{:S(2)}, u32[]{:S(2)}) %collective-permute-start.5) | collective-permute-done | bytes 32800 | tf_op jit(solution)/shard_map/ppermute | solution.py:51
  17.8 1.1 %collective-permute-done.6.refs_3_.refs_4_ = bf16[128,128]{1,0:T(8,128)(2,1)S(1)} collective-permute-done((bf16[128,128]{1,0:T(8,128)(2,1)S(1)}, bf16[128,128]{1,0:T(8,128)(2,1)S(1)}, u32[]{:S(2)}, u32[]{:S(2)}) %collective-permute-start.6) | collective-permute-done | bytes 32800 | tf_op jit(solution)/shard_map/ppermute | solution.py:51
  18.9 0.2 %product.6.refs_0_ = f32[128,128]{1,0:T(8,128)S(1)} custom-call(bf16[128,128]{1,0:T(8,128)(2,1)S(1)} %next.1.refs_0_.refs_1_, bf16[128,128]{1,0:T(8,128)(2,1)S(1)} %collective-permute-done.4.refs_1_.refs_2_, bf16[128,128]{1,0:T(8,128)(2,1)S(1)} %collective-permute-done.5.refs_2_.refs_3_, bf16[128,128]{1,0:T(8,128)(2,1)S(1)} %collective-permute-done.6.refs_3_.refs_4_, ...), custom_call_target="tpu_custom_call" | custom-call | flops 33554432 | bytes 262144 | tf_op jit(solution)/shard_map/product/pallas_call | solution.py:232
  19.1 0.1 collective-permute-start.7
  19.2 0.2 %product.7.refs_0_ = f32[128,128]{1,0:T(8,128)S(1)} custom-call(f32[128,128]{1,0:T(8,128)S(1)} %product.6.refs_0_, bf16[128,128]{1,0:T(8,128)(2,1)S(1)} %next.1.refs_0_.refs_1_, bf16[128,128]{1,0:T(8,128)(2,1)S(1)} %collective-permute-done.4.refs_1_.refs_2_, bf16[128,128]{1,0:T(8,128)(2,1)S(1)} %collective-permute-done.5.refs_2_.refs_3_, ...), custom_call_target="tpu_custom_call" | custom-call | flops 33554432 | bytes 262144 | tf_op jit(solution)/shard_map/product/pallas_call | solution.py:232
  19.4 1.0 %collective-permute-done.7.refs_1_ = f32[128,128]{1,0:T(8,128)S(1)} collective-permute-done((f32[128,128]{1,0:T(8,128)S(1)}, f32[128,128]{1,0:T(8,128)S(1)}, u32[]{:S(2)}, u32[]{:S(2)}) %collective-permute-start.7) | collective-permute-done | bytes 65568 | tf_op jit(solution)/shard_map/ppermute | solution.py:55
  20.4 0.6 %last.1 = f32[128,128]{1,0:T(8,128)} custom-call(f32[128,128]{1,0:T(8,128)S(1)} %product.7.refs_0_, f32[128,128]{1,0:T(8,128)S(1)} %collective-permute-done.7.refs_1_, f32[128,128]{1,0:T(8,128)S(1)} %restart.1.refs_2_, s32[1,128]{1,0:T(1,128)S(1)} %bitcast.4), custom_call_target="tpu_custom_call" | custom-call | bytes 196608 | tf_op jit(solution)/shard_map/last/pallas_call | solution.py:254
  (1 shorter events, 0.0 us)
Async XLA Ops:
  0.0 6.3 %copy-start = (bf16[1,1,384,128,128]{4,3,2,1,0:T(8,128)(2,1)S(1)}, bf16[1,1,384,128,128]{4,3,2,1,0:T(8,128)(2,1)}, u32[]{:S(2)}) copy-start(bf16[1,1,384,128,128]{4,3,2,1,0:T(8,128)(2,1)} %tiles_ref.3) | copy-start | bytes 37748740
  1.1 7.3 %collective-permute-start = (bf16[128,128]{1,0:T(8,128)(2,1)S(1)}, bf16[128,128]{1,0:T(8,128)(2,1)S(1)}, u32[]{:S(2)}, u32[]{:S(2)}) collective-permute-start(bf16[128,128]{1,0:T(8,128)(2,1)S(1)} %get-tuple-element.9.after_ref.refs_0_.refs_1_), channel_id=1, source_target_pairs={{4,0},{0,4},{12,8},{8,12},{5,1},{1,5},{13,9},{9,13},{6,2},{2,6},{1... | collective-permute-start | bytes 98312 | tf_op jit(solution)/shard_map/ppermute | solution.py:51
  4.1 4.3 %collective-permute-start.1 = (bf16[128,128]{1,0:T(8,128)(2,1)S(1)}, bf16[128,128]{1,0:T(8,128)(2,1)S(1)}, u32[]{:S(2)}, u32[]{:S(2)}) collective-permute-start(bf16[128,128]{1,0:T(8,128)(2,1)S(1)} %get-tuple-element.9.after_ref.refs_0_.refs_1_), channel_id=1, source_target_pairs={{8,0},{12,4},{0,8},{4,12},{9,1},{13,5},{1,9},{5,13},{10,2},{14,6},... | collective-permute-start | bytes 98312 | tf_op jit(solution)/shard_map/ppermute | solution.py:51
  5.6 4.8 %collective-permute-start.2 = (bf16[128,128]{1,0:T(8,128)(2,1)S(1)}, bf16[128,128]{1,0:T(8,128)(2,1)S(1)}, u32[]{:S(2)}, u32[]{:S(2)}) collective-permute-start(bf16[128,128]{1,0:T(8,128)(2,1)S(1)} %get-tuple-element.9.after_ref.refs_0_.refs_1_), channel_id=1, source_target_pairs={{12,0},{8,4},{4,8},{0,12},{13,1},{9,5},{5,9},{1,13},{14,2},{10,6},... | collective-permute-start | bytes 98312 | tf_op jit(solution)/shard_map/ppermute | solution.py:51
  6.3 7.1 %copy-start.1 = (s32[128]{0:T(128)S(1)}, s32[128]{0:T(128)}, u32[]{:S(2)}) copy-start(s32[128]{0:T(128)} %param.11) | copy-start | bytes 1540
  10.6 2.8 %collective-permute-start.3 = (f32[128,128]{1,0:T(8,128)S(1)}, f32[128,128]{1,0:T(8,128)S(1)}, u32[]{:S(2)}, u32[]{:S(2)}) collective-permute-start(f32[128,128]{1,0:T(8,128)S(1)} %product.4.after_ref.refs_0_), channel_id=1, source_target_pairs={{0,16},{16,0},{1,17},{17,1},{2,18},{18,2},{3,19},{19,3},{4,20},{20... | collective-permute-start | bytes 196616 | tf_op jit(solution)/shard_map/ppermute | solution.py:55
  13.4 4.0 %collective-permute-start.4 = (bf16[128,128]{1,0:T(8,128)(2,1)S(1)}, bf16[128,128]{1,0:T(8,128)(2,1)S(1)}, u32[]{:S(2)}, u32[]{:S(2)}) collective-permute-start(bf16[128,128]{1,0:T(8,128)(2,1)S(1)} %next.1.refs_0_.refs_1_), channel_id=1, source_target_pairs={{4,0},{0,4},{12,8},{8,12},{5,1},{1,5},{13,9},{9,13},{6,2},{2,6},{1... | collective-permute-start | bytes 98312 | tf_op jit(solution)/shard_map/ppermute | solution.py:51
  13.8 3.9 %collective-permute-start.5 = (bf16[128,128]{1,0:T(8,128)(2,1)S(1)}, bf16[128,128]{1,0:T(8,128)(2,1)S(1)}, u32[]{:S(2)}, u32[]{:S(2)}) collective-permute-start(bf16[128,128]{1,0:T(8,128)(2,1)S(1)} %next.1.refs_0_.refs_1_), channel_id=1, source_target_pairs={{8,0},{12,4},{0,8},{4,12},{9,1},{13,5},{1,9},{5,13},{10,2},{14,6},... | collective-permute-start | bytes 98312 | tf_op jit(solution)/shard_map/ppermute | solution.py:51
  13.8 5.0 %collective-permute-start.6 = (bf16[128,128]{1,0:T(8,128)(2,1)S(1)}, bf16[128,128]{1,0:T(8,128)(2,1)S(1)}, u32[]{:S(2)}, u32[]{:S(2)}) collective-permute-start(bf16[128,128]{1,0:T(8,128)(2,1)S(1)} %next.1.refs_0_.refs_1_), channel_id=1, source_target_pairs={{12,0},{8,4},{4,8},{0,12},{13,1},{9,5},{5,9},{1,13},{14,2},{10,6},... | collective-permute-start | bytes 98312 | tf_op jit(solution)/shard_map/ppermute | solution.py:51
  19.1 1.3 %collective-permute-start.7 = (f32[128,128]{1,0:T(8,128)S(1)}, f32[128,128]{1,0:T(8,128)S(1)}, u32[]{:S(2)}, u32[]{:S(2)}) collective-permute-start(f32[128,128]{1,0:T(8,128)S(1)} %product.6.refs_0_), channel_id=1, source_target_pairs={{0,16},{16,0},{1,17},{17,1},{2,18},{18,2},{3,19},{19,3},{4,20},{20... | collective-permute-start | bytes 196616 | tf_op jit(solution)/shard_map/ppermute | solution.py:55

commit v7 on v5

v7 whole, which is shorter than its diff:
```python
import functools
import math

import jax
import jax.numpy as jnp
from jax import lax
from jax.experimental import pallas as pl
from jax.experimental.pallas import tpu as pltpu
from jax.sharding import PartitionSpec as P

ITERATIONS = 2


damping = 0.85

VMEM = pl.BlockSpec(memory_space=pltpu.VMEM)
SMEM = pl.BlockSpec(memory_space=pltpu.SMEM)
HBM = pl.BlockSpec(memory_space=pltpu.HBM)
ANY = pl.BlockSpec(memory_space=pl.ANY)

TILES_VMEM = 32 * 1024 * 1024
SMALL_VMEM = 8 * 1024 * 1024
LANES = 4
UNROLL = 8
DEGREE_LINES = 8


def in_hbm(*arrays):
    return [pltpu.with_memory_space_constraint(array, pltpu.HBM) for array in arrays]


def call(kernel, out_shape, name, **options):
    return pl.pallas_call(
        kernel,
        out_shape=out_shape,
        compiler_params=pltpu.CompilerParams(vmem_limit_bytes=options.pop("vmem", SMALL_VMEM)),
        cost_estimate=pl.CostEstimate(
            flops=options.pop("flops", 0), bytes_accessed=options.pop("size", 0), transcendentals=0
        ),
        name=name,
        **options,
    )


def partner(index, offset, extent):
    if extent & (extent - 1) == 0:
        return index ^ offset
    return (index + offset) % extent


def offsets(cols):
    return list(range(cols))


def from_column(value, cols, offset):
    return lax.ppermute(value, "col", [(partner(col, offset, cols), col) for col in range(cols)])


def swap_rows(value):
    return lax.ppermute(value, "row", [(0, 1), (1, 0)])


def scale_kernel(
    prior_hbm, degree_hbm, out_hbm, in_hbm, seeds_hbm,
    scaled_ref, out_ref, in_ref, seeds_ref, prior_ref, degree_ref, arrived,
):
    moves = (
        (prior_hbm, prior_ref), (degree_hbm, degree_ref),
        (out_hbm, out_ref), (in_hbm, in_ref), (seeds_hbm, seeds_ref),
    )
    copies = [
        pltpu.make_async_copy(source, place, arrived.at[index])
        for index, (source, place) in enumerate(moves)
    ]
    for copy in copies:
        copy.start()
    for copy in copies[:2]:
        copy.wait()
    scaled_ref[...] = (prior_ref[...] / degree_ref[...].astype(jnp.float32)).astype(jnp.bfloat16)
    for copy in copies[2:]:
        copy.wait()


def sum_kernel(
    rows, cols, owned_blocks, after_ref, count_ref, out_ref, in_ref, tiles_ref, *rest
):
    *weight_refs, total = rest
    in_blocks = cols * owned_blocks
    slots, edge = tiles_ref.shape[2], tiles_ref.shape[3]
    owned = owned_blocks * edge
    spare = total.shape[1] - 1
    unroll = math.gcd(slots, UNROLL)
    row = lax.axis_index("row")
    occupied = count_ref[0, 0]

    total[...] = jnp.zeros(total.shape, jnp.float32)

    def add_tiles(step, carry):
        at = step * unroll
        places = []
        for lane in range(unroll):
            slot = at + lane
            pair = out_ref[0, 0, slot] * in_blocks + in_ref[0, 0, slot]
            places.append((lane % LANES, jnp.where(slot < occupied, pair, spare), slot))
        for start in range(0, unroll, 2):
            sums = [
                (lane, pair, total[lane, pair] + tiles_ref[0, 0, slot].astype(jnp.float32))
                for lane, pair, slot in places[start:start + 2]
            ]
            for lane, pair, value in sums:
                total[lane, pair] = value
        return carry

    lax.fori_loop(0, (occupied + unroll - 1) // unroll, add_tiles, 0)

    for place in range(rows):
        owner = partner(row, place, rows) if rows == 2 else place
        for block in range(owned_blocks):
            columns = slice(block * edge, (block + 1) * edge)
            for source in range(in_blocks):
                pair = (owner * owned_blocks + block) * in_blocks + source
                value = (total[0, pair] + total[1, pair]) + (total[2, pair] + total[3, pair])
                high = value.astype(jnp.bfloat16)
                low = (value - high.astype(jnp.float32)).astype(jnp.bfloat16)
                column, line = source // owned_blocks, source % owned_blocks * edge
                weight_refs[place][column, line:line + edge, columns] = high
                weight_refs[place][column, owned + line:owned + line + edge, columns] = low


def restart_kernel(rows, cols, places, after_ref, seeds_ref, restart_ref):
    seed_total, sets = seeds_ref.shape
    owned = restart_ref.shape[2]
    for place in range(places):
        row = partner(lax.axis_index("row"), place, rows)
        first = (row * cols + lax.axis_index("col")) * owned
        vertex = lax.broadcasted_iota(jnp.int32, (owned, sets), 0) + first
        restart = jnp.zeros((owned, sets), jnp.float32)
        for seed in range(seed_total):
            restart += (seeds_ref[seed:seed + 1, :] == vertex).astype(jnp.float32)
        restart_ref[place] = (1.0 - damping) * restart.T


def times_weight(col, cols, parts, weight_ref):
    incoming = None
    for part, offset in zip(parts, offsets(cols)):
        term = jnp.dot(
            jnp.concatenate([part] * 2, axis=1),
            weight_ref[partner(col, offset, cols)],
            preferred_element_type=jnp.float32,
        )
        incoming = term if incoming is None else incoming + term
    return incoming


def product_kernel(rows, cols, *refs):
    part_refs, weight_refs, (degree_ref, result_ref) = refs[:cols], refs[cols:cols + rows], refs[cols + rows:]
    col = lax.axis_index("col")
    parts = [ref[...] for ref in part_refs]
    sets, owned = parts[0].shape
    for place in range(rows):
        result_ref[place, :sets] = times_weight(col, cols, parts, weight_refs[place])
        if result_ref.shape[1] > sets:
            result_ref[place, sets:] = jnp.broadcast_to(
                degree_ref[...].astype(jnp.float32), (result_ref.shape[1] - sets, owned)
            )


def both_kernel(mine_ref, theirs_ref, restart_ref, weight_ref, scaled_ref, leaving_ref):
    leaving_ref[...] = weight_ref[...]
    sets = restart_ref.shape[1]
    for place in range(2):
        incoming = mine_ref[place, :sets] + theirs_ref[1 - place, :sets]
        degree = (theirs_ref if place else mine_ref)[0, sets:sets + 1]
        risk = restart_ref[place] + damping * incoming
        scaled_ref[place] = (risk / degree).astype(jnp.bfloat16)


def result_kernel(cols, *refs):
    part_refs, weight_refs, (restart_ref, result_ref) = refs[:cols], refs[cols:cols + 2], refs[cols + 2:]
    col = lax.axis_index("col")
    incoming = [
        times_weight(col, cols, [ref[place] for ref in part_refs], weight_refs[place]) for place in range(2)
    ]
    result_ref[...] = restart_ref[0] + damping * (incoming[0] + incoming[1])


def finish_kernel(last, incoming_ref, restart_ref, degree_ref, result_ref):
    risk = restart_ref[0] + damping * incoming_ref[...]
    if last:
        result_ref[...] = risk
    else:
        result_ref[...] = (risk / degree_ref[...].astype(jnp.float32)).astype(jnp.bfloat16)


def local(tiles, tile_out, tile_in, tile_count, out_degree, seed_ids, prior):
    rows, cols = lax.axis_size("row"), lax.axis_size("col")
    sets, owned = prior.shape
    slots, edge = tiles.shape[2], tiles.shape[3]
    owned_blocks = owned // edge
    in_blocks, out_blocks = cols * owned_blocks, rows * owned_blocks
    degree = out_degree.reshape(1, owned)
    low = jnp.bfloat16

    scaled, out_ids, in_ids, seeds = call(
        scale_kernel,
        [
            jax.ShapeDtypeStruct((sets, owned), low),
            pltpu.SMEM(tile_out.shape, jnp.int32),
            pltpu.SMEM(tile_in.shape, jnp.int32),
            jax.ShapeDtypeStruct((seed_ids.shape[1], sets), jnp.int32),
        ],
        "scale",
        in_specs=[HBM] * 5,
        out_specs=[VMEM, SMEM, SMEM, VMEM],
        scratch_shapes=[
            pltpu.VMEM((sets, owned), jnp.float32),
            pltpu.VMEM((1, owned), jnp.int32),
            pltpu.SemaphoreType.DMA((5,)),
        ],
        flops=16 * slots * edge**3,
        size=6 * sets * owned,
    )(*in_hbm(prior, degree, tile_out, tile_in, seed_ids.T))

    def spread(value):
        return [from_column(value, cols, offset) if offset else value for offset in offsets(cols)]

    parts = spread(scaled)

    weights = call(
        functools.partial(sum_kernel, rows, cols, owned_blocks),
        [jax.ShapeDtypeStruct((cols, 2 * owned, owned), low)] * rows,
        "sum_tiles",
        in_specs=[ANY] + [SMEM] * 3 + [VMEM],
        out_specs=[VMEM] * rows,
        scratch_shapes=[pltpu.VMEM((LANES, out_blocks * in_blocks + 1, edge, edge), jnp.float32)],
        vmem=TILES_VMEM,
        flops=slots * edge * edge,
        size=2 * slots * edge * edge,
    )(scaled, tile_count, out_ids, in_ids, tiles)

    def multiply(parts, lines):
        return call(
            functools.partial(product_kernel, rows, cols),
            jax.ShapeDtypeStruct((rows, lines, owned), jnp.float32),
            "product",
            in_specs=[VMEM] * (cols + rows + 1),
            out_specs=VMEM,
            flops=4 * sets * rows * cols * owned * owned,
            size=4 * rows * cols * owned * owned,
        )(*parts, *weights, degree)

    def count_restart(places, after):
        return call(
            functools.partial(restart_kernel, rows, cols, places),
            jax.ShapeDtypeStruct((places, sets, owned), jnp.float32),
            "restart",
            in_specs=[ANY, VMEM],
            out_specs=VMEM,
            flops=2 * places * sets * owned * seed_ids.shape[1],
            size=4 * places * sets * owned,
        )(after, seeds)

    if rows == 2 and ITERATIONS == 2:
        mine = multiply(parts, sets + DEGREE_LINES)
        theirs = swap_rows(mine)
        restart = count_restart(2, mine)
        both, leaving = call(
            both_kernel,
            [jax.ShapeDtypeStruct((2, sets, owned), low), jax.ShapeDtypeStruct(weights[1].shape, low)],
            "both",
            in_specs=[VMEM] * 4,
            out_specs=[VMEM] * 2,
            size=24 * sets * owned,
        )(mine, theirs, restart, weights[1])
        parts = spread(both)
        other_weight = swap_rows(leaving)
        return call(
            functools.partial(result_kernel, cols),
            jax.ShapeDtypeStruct((sets, owned), jnp.float32),
            "result",
            in_specs=[VMEM] * (cols + 3),
            out_specs=VMEM,
            flops=8 * sets * cols * owned * owned,
            size=8 * cols * owned * owned,
        )(*parts, weights[0], other_weight, restart)

    restart = count_restart(1, scaled)
    for round_index in range(ITERATIONS):
        last = round_index == ITERATIONS - 1
        partial_value = multiply(parts, sets)
        incoming = lax.psum_scatter(partial_value, "row", scatter_dimension=0, tiled=False)
        value = call(
            functools.partial(finish_kernel, last),
            jax.ShapeDtypeStruct((sets, owned), jnp.float32 if last else low),
            "last" if last else "next",
            in_specs=[VMEM] * 3,
            out_specs=VMEM,
            size=12 * sets * owned,
        )(incoming, restart, degree)
        if not last:
            parts = spread(value)
    return value


def solution(mesh):
    placed = (
        P("row", "col", None, None, None),
        P("row", "col", None),
        P("row", "col", None),
        P("row", "col"),
        P(("row", "col")),
        P("seed", None),
        P("seed", ("row", "col")),
    )
    return jax.shard_map(
        local, mesh=mesh, in_specs=placed, out_specs=P("seed", ("row", "col")), check_vma=False
    )
```

time: 21.3 us -> 20 us (0.939)
  waiting for transfers between devices: 7.6 us -> 4.75 us
  Pallas kernels: 4.04 us -> 5.97 us
  starting transfers between devices: 8.78 us -> 8.39 us
    pallas_call x1, Pallas kernels: 1.83 us -> 3.34 us  [local(): call(functools.partial(sum_kernel, rows, cols, owned_blocks), [jax.ShapeD...]
    ppermute x2, waiting for transfers between devices: 2.48 us -> 1.05 us  [swap_rows(): return lax.ppermute(value, 'row', [(0, 1), (1, 0)])]
    ppermute x6, waiting for transfers between devices: 5.11 us -> 3.7 us  [from_column(): lax.ppermute(value, 'col', [(partner(col, offset, cols), col) for col in...]
    ppermute x6, starting transfers between devices: 8.64 us -> 8.1 us  [from_column(): lax.ppermute(value, 'col', [(partner(col, offset, cols), col) for col in...]
    pallas_call x4, Pallas kernels: 1.15 us -> 1.57 us  [the longest x1 0.92 us: local(): call(functools.partial(result_kernel, cols), jax.ShapeDtypeStruct((sets,...]
  transfers between devices with their start and end apart: 8 -> 8, of which waited for: 7 -> 3; matrix products, arithmetic and copies ran while one was open for 0% -> 0% of each run, Pallas kernels for 9% -> 18%
where the time goes in v7:
time: 20 us; the launch traced here: 19.9 us
  starting transfers between devices  8.39 us (42%)
  Pallas kernels  5.97 us (30%)
  waiting for transfers between devices  4.75 us (24%)
  between operations  0.74 us (4%)
    ppermute x6, starting transfers between devices, from_column(): lax.ppermute(value, 'col', [(partner(col, offset, cols), col) for col in...  8.1 us
    ppermute x6, waiting for transfers between devices, from_column(): lax.ppermute(value, 'col', [(partner(col, offset, cols), col) for col in...  3.7 us
    pallas_call x1, Pallas kernels, local(): call(functools.partial(sum_kernel, rows, cols, owned_blocks), [jax.ShapeD...  3.34 us
    pallas_call x1, Pallas kernels, local(): call(scale_kernel, [jax.ShapeDtypeStruct((sets, owned), low), pltpu.SMEM(...  1.07 us
    ppermute x2, waiting for transfers between devices, swap_rows(): return lax.ppermute(value, 'row', [(0, 1), (1, 0)])  1.05 us
    pallas_call x1, Pallas kernels, local(): call(functools.partial(result_kernel, cols), jax.ShapeDtypeStruct((sets,...  0.92 us
  transfers between devices with their start and end apart: 8, of which 3 were waited for; matrix products, arithmetic and copies ran while one was open for 0% of the time, Pallas kernels for 18%

profile of v7, /device:TPU:0, one launch (start us, length us, event | category | flops | bytes accessed | tf_op | source)
XLA Modules:
  0.0 19.9 jit_solution(16863319431062447259)
XLA Ops:
  0.0 0.0 copy-start
  0.0 1.1 %scale.1 = (bf16[128,128]{1,0:T(8,128)(2,1)S(1)}, s32[1,1,384]{2,1,0:T(1,128)S(4)}, s32[1,1,384]{2,1,0:T(1,128)S(4)}, s32[16,128]{1,0:T(8,128)S(1)}) custom-call(f32[128,128]{1,0:T(8,128)} %prior_hbm.1, s32[1,128]{1,0:T(1,128)} %bitcast.2, s32[1,1,384]{2,1,0:T(1,128)} %out_hbm.1, s32[1,1,384]{2,1,0:T(1,128)} %in_hbm.1, s32[16,128]{1,0:T(8,128)} %bitcast.4), custom_call_target="tpu_custom_call" | custom-call | flops 12884901888 | bytes 98304 | tf_op jit(solution)/shard_map/scale/pallas_call | solution.py:204
  1.1 0.0 copy-start.1
  1.1 4.0 %collective-permute-start.2 = (bf16[128,128]{1,0:T(8,128)(2,1)S(1)}, bf16[128,128]{1,0:T(8,128)(2,1)S(1)}, u32[]{:S(2)}, u32[]{:S(2)}) collective-permute-start(bf16[128,128]{1,0:T(8,128)(2,1)S(1)} %get-tuple-element.13.after_ref.refs_0_), channel_id=1, source_target_pairs={{12,0},{8,4},{4,8},{0,12},{13,1},{9,5},{5,9},{1,13},{14,2},{10,6},... | collective-permute-start | bytes 98312 | tf_op jit(solution)/shard_map/ppermute | solution.py:56
  5.0 0.5 %collective-permute-start.1 = (bf16[128,128]{1,0:T(8,128)(2,1)S(1)}, bf16[128,128]{1,0:T(8,128)(2,1)S(1)}, u32[]{:S(2)}, u32[]{:S(2)}) collective-permute-start(bf16[128,128]{1,0:T(8,128)(2,1)S(1)} %get-tuple-element.13.after_ref.refs_0_), channel_id=1, source_target_pairs={{8,0},{12,4},{0,8},{4,12},{9,1},{13,5},{1,9},{5,13},{10,2},{14,6},... | collective-permute-start | bytes 98312 | tf_op jit(solution)/shard_map/ppermute | solution.py:56
  5.6 0.1 collective-permute-start
  6.3 0.0 copy-done
  6.4 3.3 %sum_tiles.1 = (bf16[4,256,128]{2,1,0:T(8,128)(2,1)S(1)}, bf16[4,256,128]{2,1,0:T(8,128)(2,1)S(1)}) custom-call(bf16[128,128]{1,0:T(8,128)(2,1)S(1)} %get-tuple-element.13.after_ref.refs_0_, s32[1,1]{1,0:T(1,128)S(6)} %copy.8.count_ref, s32[1,1,384]{2,1,0:T(1,128)S(4)} %get-tuple-element.14.out_ref, s32[1,1,384]{2,1,0:T(1,128)S(4)} %get-tuple-element.15.in_ref, ...), custom_call_target="tpu_custom_call" | custom-call | flops 6291456 | bytes 12582912 | tf_op jit(solution)/shard_map/sum_tiles/pallas_call | solution.py:229
  9.7 0.0 collective-permute-done.2.refs_3_
  9.7 0.0 collective-permute-done.1.refs_2_
  9.7 0.0 collective-permute-done.refs_1_
  9.7 0.0 copy-done.1
  9.7 0.3 %product.1.after_ref.mine_ref = f32[2,136,128]{2,1,0:T(8,128)S(1)} custom-call(bf16[128,128]{1,0:T(8,128)(2,1)S(1)} %get-tuple-element.13.after_ref.refs_0_, bf16[128,128]{1,0:T(8,128)(2,1)S(1)} %collective-permute-done.refs_1_, bf16[128,128]{1,0:T(8,128)(2,1)S(1)} %collective-permute-done.1.refs_2_, bf16[128,128]{1,0:T(8,128)(2,1)S(1)} %collective-permute-done.2.refs_3_, ...), custom_call_target="tpu_custom_call" | custom-call | flops 67108864 | bytes 524288 | tf_op jit(solution)/shard_map/product/pallas_call | solution.py:242
  10.0 0.1 collective-permute-start.3
  10.1 0.3 %restart.1.restart_ref.refs_6_ = f32[2,128,128]{2,1,0:T(8,128)S(1)} custom-call(f32[2,136,128]{2,1,0:T(8,128)S(1)} %product.1.after_ref.mine_ref, s32[16,128]{1,0:T(8,128)S(1)} %get-tuple-element.18.seeds_ref), custom_call_target="tpu_custom_call" | custom-call | flops 1048576 | bytes 131072 | tf_op jit(solution)/shard_map/restart/pallas_call | solution.py:253
  10.4 1.1 %collective-permute-done.3.theirs_ref = f32[2,136,128]{2,1,0:T(8,128)S(1)} collective-permute-done((f32[2,136,128]{2,1,0:T(8,128)S(1)}, f32[2,136,128]{2,1,0:T(8,128)S(1)}, u32[]{:S(2)}, u32[]{:S(2)}) %collective-permute-start.3) | collective-permute-done | bytes 139296 | tf_op jit(solution)/shard_map/ppermute | solution.py:60
  11.5 0.1 both.1
  11.5 0.2 %collective-permute-start.7 = (bf16[4,256,128]{2,1,0:T(8,128)(2,1)S(1)}, bf16[4,256,128]{2,1,0:T(8,128)(2,1)S(1)}, u32[]{:S(2)}, u32[]{:S(2)}) collective-permute-start(bf16[4,256,128]{2,1,0:T(8,128)(2,1)S(1)} %get-tuple-element.20), channel_id=1, source_target_pairs={{0,16},{16,0},{1,17},{17,1},{2,18},{18,2},{3,19},{19,3},{4,20},{20... | collective-permute-start | bytes 786440 | tf_op jit(solution)/shard_map/ppermute | solution.py:60
  11.7 2.9 %collective-permute-start.6 = (bf16[2,128,128]{2,1,0:T(8,128)(2,1)S(1)}, bf16[2,128,128]{2,1,0:T(8,128)(2,1)S(1)}, u32[]{:S(2)}, u32[]{:S(2)}) collective-permute-start(bf16[2,128,128]{2,1,0:T(8,128)(2,1)S(1)} %get-tuple-element.19.refs_0_), channel_id=1, source_target_pairs={{12,0},{8,4},{4,8},{0,12},{13,1},{9,5},{5,9},{1,13},{14,2},{10,6},... | collective-permute-start | bytes 196616 | tf_op jit(solution)/shard_map/ppermute | solution.py:56
  14.7 0.0 collective-permute-start.5
  14.7 0.6 %collective-permute-start.4 = (bf16[2,128,128]{2,1,0:T(8,128)(2,1)S(1)}, bf16[2,128,128]{2,1,0:T(8,128)(2,1)S(1)}, u32[]{:S(2)}, u32[]{:S(2)}) collective-permute-start(bf16[2,128,128]{2,1,0:T(8,128)(2,1)S(1)} %get-tuple-element.19.refs_0_), channel_id=1, source_target_pairs={{4,0},{0,4},{12,8},{8,12},{5,1},{1,5},{13,9},{9,13},{6,2},{2,6},{1... | collective-permute-start | bytes 196616 | tf_op jit(solution)/shard_map/ppermute | solution.py:56
  15.2 2.0 %collective-permute-done.6.refs_3_ = bf16[2,128,128]{2,1,0:T(8,128)(2,1)S(1)} collective-permute-done((bf16[2,128,128]{2,1,0:T(8,128)(2,1)S(1)}, bf16[2,128,128]{2,1,0:T(8,128)(2,1)S(1)}, u32[]{:S(2)}, u32[]{:S(2)}) %collective-permute-start.6) | collective-permute-done | bytes 65568 | tf_op jit(solution)/shard_map/ppermute | solution.py:56
  17.3 1.7 %collective-permute-done.5.refs_2_ = bf16[2,128,128]{2,1,0:T(8,128)(2,1)S(1)} collective-permute-done((bf16[2,128,128]{2,1,0:T(8,128)(2,1)S(1)}, bf16[2,128,128]{2,1,0:T(8,128)(2,1)S(1)}, u32[]{:S(2)}, u32[]{:S(2)}) %collective-permute-start.5) | collective-permute-done | bytes 65568 | tf_op jit(solution)/shard_map/ppermute | solution.py:56
  18.9 0.0 collective-permute-done.4.refs_1_
  18.9 0.0 collective-permute-done.7.refs_5_
  18.9 0.9 %result.1 = f32[128,128]{1,0:T(8,128)} custom-call(bf16[2,128,128]{2,1,0:T(8,128)(2,1)S(1)} %get-tuple-element.19.refs_0_, bf16[2,128,128]{2,1,0:T(8,128)(2,1)S(1)} %collective-permute-done.4.refs_1_, bf16[2,128,128]{2,1,0:T(8,128)(2,1)S(1)} %collective-permute-done.5.refs_2_, bf16[2,128,128]{2,1,0:T(8,128)(2,1)S(1)} %collective-permute-done.6.refs_3_, ...), custom_call_target="tpu_custom_call" | custom-call | flops 67108864 | bytes 524288 | tf_op jit(solution)/shard_map/result/pallas_call | solution.py:277
Async XLA Ops:
  0.0 6.3 %copy-start = (bf16[1,1,384,128,128]{4,3,2,1,0:T(8,128)(2,1)S(1)}, bf16[1,1,384,128,128]{4,3,2,1,0:T(8,128)(2,1)}, u32[]{:S(2)}) copy-start(bf16[1,1,384,128,128]{4,3,2,1,0:T(8,128)(2,1)} %tiles_ref.1) | copy-start | bytes 37748740
  1.1 8.7 %copy-start.1 = (s32[128]{0:T(128)S(1)}, s32[128]{0:T(128)}, u32[]{:S(2)}) copy-start(s32[128]{0:T(128)} %param.11) | copy-start | bytes 1540
  1.1 8.6 %collective-permute-start.2 = (bf16[128,128]{1,0:T(8,128)(2,1)S(1)}, bf16[128,128]{1,0:T(8,128)(2,1)S(1)}, u32[]{:S(2)}, u32[]{:S(2)}) collective-permute-start(bf16[128,128]{1,0:T(8,128)(2,1)S(1)} %get-tuple-element.13.after_ref.refs_0_), channel_id=1, source_target_pairs={{12,0},{8,4},{4,8},{0,12},{13,1},{9,5},{5,9},{1,13},{14,2},{10,6},... | collective-permute-start | bytes 98312 | tf_op jit(solution)/shard_map/ppermute | solution.py:56
  5.0 4.7 %collective-permute-start.1 = (bf16[128,128]{1,0:T(8,128)(2,1)S(1)}, bf16[128,128]{1,0:T(8,128)(2,1)S(1)}, u32[]{:S(2)}, u32[]{:S(2)}) collective-permute-start(bf16[128,128]{1,0:T(8,128)(2,1)S(1)} %get-tuple-element.13.after_ref.refs_0_), channel_id=1, source_target_pairs={{8,0},{12,4},{0,8},{4,12},{9,1},{13,5},{1,9},{5,13},{10,2},{14,6},... | collective-permute-start | bytes 98312 | tf_op jit(solution)/shard_map/ppermute | solution.py:56
  5.6 4.2 %collective-permute-start = (bf16[128,128]{1,0:T(8,128)(2,1)S(1)}, bf16[128,128]{1,0:T(8,128)(2,1)S(1)}, u32[]{:S(2)}, u32[]{:S(2)}) collective-permute-start(bf16[128,128]{1,0:T(8,128)(2,1)S(1)} %get-tuple-element.13.after_ref.refs_0_), channel_id=1, source_target_pairs={{4,0},{0,4},{12,8},{8,12},{5,1},{1,5},{13,9},{9,13},{6,2},{2,6},{1... | collective-permute-start | bytes 98312 | tf_op jit(solution)/shard_map/ppermute | solution.py:56
  10.0 1.4 %collective-permute-start.3 = (f32[2,136,128]{2,1,0:T(8,128)S(1)}, f32[2,136,128]{2,1,0:T(8,128)S(1)}, u32[]{:S(2)}, u32[]{:S(2)}) collective-permute-start(f32[2,136,128]{2,1,0:T(8,128)S(1)} %product.1.after_ref.mine_ref), channel_id=1, source_target_pairs={{0,16},{16,0},{1,17},{17,1},{2,18},{18,2},{3,19},{19,3},{4,20},{20... | collective-permute-start | bytes 417800 | tf_op jit(solution)/shard_map/ppermute | solution.py:60
  11.5 7.4 %collective-permute-start.7 = (bf16[4,256,128]{2,1,0:T(8,128)(2,1)S(1)}, bf16[4,256,128]{2,1,0:T(8,128)(2,1)S(1)}, u32[]{:S(2)}, u32[]{:S(2)}) collective-permute-start(bf16[4,256,128]{2,1,0:T(8,128)(2,1)S(1)} %get-tuple-element.20), channel_id=1, source_target_pairs={{0,16},{16,0},{1,17},{17,1},{2,18},{18,2},{3,19},{19,3},{4,20},{20... | collective-permute-start | bytes 786440 | tf_op jit(solution)/shard_map/ppermute | solution.py:60
  11.7 5.5 %collective-permute-start.6 = (bf16[2,128,128]{2,1,0:T(8,128)(2,1)S(1)}, bf16[2,128,128]{2,1,0:T(8,128)(2,1)S(1)}, u32[]{:S(2)}, u32[]{:S(2)}) collective-permute-start(bf16[2,128,128]{2,1,0:T(8,128)(2,1)S(1)} %get-tuple-element.19.refs_0_), channel_id=1, source_target_pairs={{12,0},{8,4},{4,8},{0,12},{13,1},{9,5},{5,9},{1,13},{14,2},{10,6},... | collective-permute-start | bytes 196616 | tf_op jit(solution)/shard_map/ppermute | solution.py:56
  14.7 4.3 %collective-permute-start.5 = (bf16[2,128,128]{2,1,0:T(8,128)(2,1)S(1)}, bf16[2,128,128]{2,1,0:T(8,128)(2,1)S(1)}, u32[]{:S(2)}, u32[]{:S(2)}) collective-permute-start(bf16[2,128,128]{2,1,0:T(8,128)(2,1)S(1)} %get-tuple-element.19.refs_0_), channel_id=1, source_target_pairs={{8,0},{12,4},{0,8},{4,12},{9,1},{13,5},{1,9},{5,13},{10,2},{14,6},... | collective-permute-start | bytes 196616 | tf_op jit(solution)/shard_map/ppermute | solution.py:56
  14.7 4.3 %collective-permute-start.4 = (bf16[2,128,128]{2,1,0:T(8,128)(2,1)S(1)}, bf16[2,128,128]{2,1,0:T(8,128)(2,1)S(1)}, u32[]{:S(2)}, u32[]{:S(2)}) collective-permute-start(bf16[2,128,128]{2,1,0:T(8,128)(2,1)S(1)} %get-tuple-element.19.refs_0_), channel_id=1, source_target_pairs={{4,0},{0,4},{12,8},{8,12},{5,1},{1,5},{13,9},{9,13},{6,2},{2,6},{1... | collective-permute-start | bytes 196616 | tf_op jit(solution)/shard_map/ppermute | solution.py:56

commit v8 on v7

--- a/solution.py
+++ b/solution.py
@@ -22,7 +22,7 @@
 SMALL_VMEM = 8 * 1024 * 1024
 LANES = 4
 UNROLL = 8
-DEGREE_LINES = 8
+DEGREE_LINES = 16
 
 
 def in_hbm(*arrays):
@@ -48,16 +48,11 @@
     return (index + offset) % extent
 
 
-def offsets(cols):
-    return list(range(cols))
-
-
-def from_column(value, cols, offset):
-    return lax.ppermute(value, "col", [(partner(col, offset, cols), col) for col in range(cols)])
-
-
-def swap_rows(value):
-    return lax.ppermute(value, "row", [(0, 1), (1, 0)])
+def from_column(value, rows, cols, offset):
+    pairs = [
+        (row * cols + partner(col, offset, cols), row * cols + col) for row in rows for col in range(cols)
+    ]
+    return lax.ppermute(value, ("row", "col"), pairs)
 
 
 def scale_kernel(
@@ -76,15 +71,27 @@
         copy.start()
     for copy in copies[:2]:
         copy.wait()
-    scaled_ref[...] = (prior_ref[...] / degree_ref[...].astype(jnp.float32)).astype(jnp.bfloat16)
+    degree = degree_ref[...].astype(jnp.float32)
+    sets, owned = prior_ref.shape
+    scaled_ref[:sets] = (prior_ref[...] / degree).astype(jnp.bfloat16)
+    extra = scaled_ref.shape[0] - sets
+    if extra:
+        scaled_ref[sets:] = jnp.broadcast_to(degree, (extra, owned)).astype(jnp.bfloat16)
     for copy in copies[2:]:
         copy.wait()
+
+
+def join_kernel(count_ref, mine_ref, theirs_ref, joined_ref, degree_ref):
+    sets = joined_ref.shape[1]
+    for place, ref in enumerate((mine_ref, theirs_ref)):
+        joined_ref[place] = ref[:sets]
+        degree_ref[place] = ref[sets:].astype(jnp.float32)
 
 
 def sum_kernel(
     rows, cols, owned_blocks, after_ref, count_ref, out_ref, in_ref, tiles_ref, *rest
 ):
-    *weight_refs, total = rest
+    weight_ref, total = rest
     in_blocks = cols * owned_blocks
     slots, edge = tiles_ref.shape[2], tiles_ref.shape[3]
     owned = owned_blocks * edge
@@ -123,8 +130,14 @@
                 high = value.astype(jnp.bfloat16)
                 low = (value - high.astype(jnp.float32)).astype(jnp.bfloat16)
                 column, line = source // owned_blocks, source % owned_blocks * edge
-                weight_refs[place][column, line:line + edge, columns] = high
-                weight_refs[place][column, owned + line:owned + line + edge, columns] = low
+                lines = slice(line, line + edge)
+                weight_ref[place, column, lines, columns] = high
+                weight_ref[place, column, lines, owned + block * edge:owned + (block + 1) * edge] = low
+
+
+def leave_kernel(after, *refs):
+    source_ref, leaving_ref = refs[after:]
+    leaving_ref[...] = source_ref[...]
 
 
 def restart_kernel(rows, cols, places, after_ref, seeds_ref, restart_ref):
@@ -140,48 +153,45 @@
         restart_ref[place] = (1.0 - damping) * restart.T
 
 
-def times_weight(col, cols, parts, weight_ref):
+def times_weight(parts, weights):
     incoming = None
-    for part, offset in zip(parts, offsets(cols)):
+    for start in range(0, len(parts), 2):
         term = jnp.dot(
-            jnp.concatenate([part] * 2, axis=1),
-            weight_ref[partner(col, offset, cols)],
+            jnp.concatenate(parts[start:start + 2], axis=1),
+            jnp.concatenate(weights[start:start + 2], axis=0),
             preferred_element_type=jnp.float32,
         )
         incoming = term if incoming is None else incoming + term
-    return incoming
+    owned = incoming.shape[1] // 2
+    return incoming[:, :owned] + incoming[:, owned:]
+
+
+def round_kernel(cols, last, *refs):
+    part_refs, (mine_ref, theirs_ref, restart_ref, degree_ref, *result_refs) = refs[:cols], refs[cols:]
+    col = lax.axis_index("col")
+    columns = [partner(col, offset, cols) for offset in range(cols)]
+    parts = [ref[place] for place in range(2) for ref in part_refs]
+    for block in range(2):
+        weights = [mine_ref[block, column] for column in columns]
+        weights += [theirs_ref[1 - block, column] for column in columns]
+        risk = restart_ref[block] + damping * times_weight(parts, weights)
+        if last:
+            result_refs[block][...] = risk
+        else:
+            result_refs[0][block] = (risk / jnp.maximum(degree_ref[block, :1], 1.0)).astype(jnp.bfloat16)
+
+
+def result_kernel(mine_ref, received_ref, result_ref):
+    result_ref[...] = jnp.where(lax.axis_index("row") == 1, mine_ref[...], received_ref[...])
 
 
 def product_kernel(rows, cols, *refs):
-    part_refs, weight_refs, (degree_ref, result_ref) = refs[:cols], refs[cols:cols + rows], refs[cols + rows:]
+    part_refs, (weight_ref, result_ref) = refs[:cols], refs[cols:]
     col = lax.axis_index("col")
     parts = [ref[...] for ref in part_refs]
-    sets, owned = parts[0].shape
     for place in range(rows):
-        result_ref[place, :sets] = times_weight(col, cols, parts, weight_refs[place])
-        if result_ref.shape[1] > sets:
-            result_ref[place, sets:] = jnp.broadcast_to(
-                degree_ref[...].astype(jnp.float32), (result_ref.shape[1] - sets, owned)
-            )
-
-
-def both_kernel(mine_ref, theirs_ref, restart_ref, weight_ref, scaled_ref, leaving_ref):
-    leaving_ref[...] = weight_ref[...]
-    sets = restart_ref.shape[1]
-    for place in range(2):
-        incoming = mine_ref[place, :sets] + theirs_ref[1 - place, :sets]
-        degree = (theirs_ref if place else mine_ref)[0, sets:sets + 1]
-        risk = restart_ref[place] + damping * incoming
-        scaled_ref[place] = (risk / degree).astype(jnp.bfloat16)
-
-
-def result_kernel(cols, *refs):
-    part_refs, weight_refs, (restart_ref, result_ref) = refs[:cols], refs[cols:cols + 2], refs[cols + 2:]
-    col = lax.axis_index("col")
-    incoming = [
-        times_weight(col, cols, [ref[place] for ref in part_refs], weight_refs[place]) for place in range(2)
-    ]
-    result_ref[...] = restart_ref[0] + damping * (incoming[0] + incoming[1])
+        weights = [weight_ref[place, partner(col, offset, cols)] for offset in range(cols)]
+        result_ref[place] = times_weight(parts, weights)
 
 
 def finish_kernel(last, incoming_ref, restart_ref, degree_ref, result_ref):
@@ -200,11 +210,12 @@
     in_blocks, out_blocks = cols * owned_blocks, rows * owned_blocks
     degree = out_degree.reshape(1, owned)
     low = jnp.bfloat16
+    paired = rows == 2
 
     scaled, out_ids, in_ids, seeds = call(
         scale_kernel,
         [
-            jax.ShapeDtypeStruct((sets, owned), low),
+            jax.ShapeDtypeStruct((sets + DEGREE_LINES if paired else sets, owned), low),
             pltpu.SMEM(tile_out.shape, jnp.int32),
             pltpu.SMEM(tile_in.shape, jnp.int32),
             jax.ShapeDtypeStruct((seed_ids.shape[1], sets), jnp.int32),
@@ -222,32 +233,34 @@
     )(*in_hbm(prior, degree, tile_out, tile_in, seed_ids.T))
 
     def spread(value):
-        return [from_column(value, cols, offset) if offset else value for offset in offsets(cols)]
-
+        talking = [1] if paired else range(rows)
+        return [from_column(value, talking, cols, offset) if offset else value for offset in range(cols)]
+
+    if paired:
+        scaled, degrees = call(
+            join_kernel,
+            [
+                jax.ShapeDtypeStruct((2, sets, owned), low),
+                jax.ShapeDtypeStruct((2, DEGREE_LINES, owned), jnp.float32),
+            ],
+            "join",
+            in_specs=[SMEM] + [VMEM] * 2,
+            out_specs=[VMEM] * 2,
+            size=8 * sets * owned,
+        )(tile_count, scaled, lax.ppermute(scaled, "row", [(0, 1)]))
     parts = spread(scaled)
 
-    weights = call(
+    weight = call(
         functools.partial(sum_kernel, rows, cols, owned_blocks),
-        [jax.ShapeDtypeStruct((cols, 2 * owned, owned), low)] * rows,
+        jax.ShapeDtypeStruct((rows, cols, owned, 2 * owned), low),
         "sum_tiles",
         in_specs=[ANY] + [SMEM] * 3 + [VMEM],
-        out_specs=[VMEM] * rows,
+        out_specs=VMEM,
         scratch_shapes=[pltpu.VMEM((LANES, out_blocks * in_blocks + 1, edge, edge), jnp.float32)],
         vmem=TILES_VMEM,
         flops=slots * edge * edge,
         size=2 * slots * edge * edge,
     )(scaled, tile_count, out_ids, in_ids, tiles)
-
-    def multiply(parts, lines):
-        return call(
-            functools.partial(product_kernel, rows, cols),
-            jax.ShapeDtypeStruct((rows, lines, owned), jnp.float32),
-            "product",
-            in_specs=[VMEM] * (cols + rows + 1),
-            out_specs=VMEM,
-            flops=4 * sets * rows * cols * owned * owned,
-            size=4 * rows * cols * owned * owned,
-        )(*parts, *weights, degree)
 
     def count_restart(places, after):
         return call(
@@ -260,43 +273,61 @@
             size=4 * places * sets * owned,
         )(after, seeds)
 
-    if rows == 2 and ITERATIONS == 2:
-        mine = multiply(parts, sets + DEGREE_LINES)
-        theirs = swap_rows(mine)
-        restart = count_restart(2, mine)
-        both, leaving = call(
-            both_kernel,
-            [jax.ShapeDtypeStruct((2, sets, owned), low), jax.ShapeDtypeStruct(weights[1].shape, low)],
-            "both",
-            in_specs=[VMEM] * 4,
-            out_specs=[VMEM] * 2,
-            size=24 * sets * owned,
-        )(mine, theirs, restart, weights[1])
-        parts = spread(both)
-        other_weight = swap_rows(leaving)
-        return call(
-            functools.partial(result_kernel, cols),
-            jax.ShapeDtypeStruct((sets, owned), jnp.float32),
-            "result",
-            in_specs=[VMEM] * (cols + 3),
-            out_specs=VMEM,
-            flops=8 * sets * cols * owned * owned,
-            size=8 * cols * owned * owned,
-        )(*parts, weights[0], other_weight, restart)
-
-    restart = count_restart(1, scaled)
     for round_index in range(ITERATIONS):
         last = round_index == ITERATIONS - 1
-        partial_value = multiply(parts, sets)
-        incoming = lax.psum_scatter(partial_value, "row", scatter_dimension=0, tiled=False)
-        value = call(
-            functools.partial(finish_kernel, last),
-            jax.ShapeDtypeStruct((sets, owned), jnp.float32 if last else low),
-            "last" if last else "next",
-            in_specs=[VMEM] * 3,
-            out_specs=VMEM,
-            size=12 * sets * owned,
-        )(incoming, restart, degree)
+        if not round_index and paired:
+            leaving = call(
+                functools.partial(leave_kernel, cols),
+                jax.ShapeDtypeStruct(weight.shape, low),
+                "leave",
+                in_specs=[ANY] * cols + [VMEM],
+                out_specs=VMEM,
+                size=4 * weight.size,
+            )(*parts, weight)
+            other_weight = lax.ppermute(leaving, "row", [(0, 1)])
+            restart = count_restart(2, leaving)
+        elif not round_index:
+            restart = count_restart(1, weight)
+        if paired:
+            value = call(
+                functools.partial(round_kernel, cols, last),
+                [jax.ShapeDtypeStruct((sets, owned), jnp.float32)] * 2
+                if last
+                else jax.ShapeDtypeStruct((2, sets, owned), low),
+                "last" if last else "next",
+                in_specs=[VMEM] * (cols + 4),
+                out_specs=[VMEM] * 2 if last else VMEM,
+                flops=16 * sets * cols * owned * owned,
+                size=16 * cols * owned * owned,
+            )(*parts, weight, other_weight, restart, degrees)
+            if last:
+                value = call(
+                    result_kernel,
+                    jax.ShapeDtypeStruct((sets, owned), jnp.float32),
+                    "result",
+                    in_specs=[VMEM] * 2,
+                    out_specs=VMEM,
+                    size=12 * sets * owned,
+                )(value[0], lax.ppermute(value[1], "row", [(1, 0)]))
+        else:
+            partial_value = call(
+                functools.partial(product_kernel, rows, cols),
+                jax.ShapeDtypeStruct((rows, sets, owned), jnp.float32),
+                "product",
+                in_specs=[VMEM] * (cols + 1),
+                out_specs=VMEM,
+                flops=4 * sets * rows * cols * owned * owned,
+                size=4 * rows * cols * owned * owned,
+            )(*parts, weight)
+            incoming = lax.psum_scatter(partial_value, "row", scatter_dimension=0, tiled=False)
+            value = call(
+                functools.partial(finish_kernel, last),
+                jax.ShapeDtypeStruct((sets, owned), jnp.float32 if last else low),
+                "last" if last else "next",
+                in_specs=[VMEM] * 3,
+                out_specs=VMEM,
+                size=12 * sets * owned,
+            )(incoming, restart, degree)
         if not last:
             parts = spread(value)
     return value

time: 20 us -> 35.6 us (1.78); the launches traced: 19.9 us -> 36 us
  starting transfers between devices: 8.39 us -> 17.3 us
  waiting for transfers between devices: 4.75 us -> 11.8 us
    ppermute x8 -> x9, starting transfers between devices: 8.39 us -> 17.3 us  [the longest x1 9.24 us: local(): other_weight = lax.ppermute(leaving, 'row', [(0, 1)])]
    ppermute x8 -> x9, waiting for transfers between devices: 4.75 us -> 11.8 us  [the longest x1 10.4 us: local(): lax.ppermute(value[1], 'row', [(1, 0)])]
    pallas_call x5 -> x7, Pallas kernels: 5.68 us -> 5.86 us  [the longest x1 3.48 us: local(): call(functools.partial(sum_kernel, rows, cols, owned_blocks), jax.ShapeDt...]
  transfers between devices with their start and end apart: 8 -> 9, of which waited for: 3 -> 3; matrix products, arithmetic and copies ran while one was open for 0% -> 0% of each run, Pallas kernels for 18% -> 10%
where the time goes in v8:
time: 35.6 us; the launch traced here: 36 us
  starting transfers between devices  17.3 us (49%)
  waiting for transfers between devices  11.8 us (33%)
  Pallas kernels  6.16 us (17%)
  between operations  0.82 us (2%)
    ppermute x1, waiting for transfers between devices, local(): lax.ppermute(value[1], 'row', [(1, 0)])  10.4 us
    ppermute x1, starting transfers between devices, local(): other_weight = lax.ppermute(leaving, 'row', [(0, 1)])  9.24 us
    ppermute x6, starting transfers between devices, from_column(): return lax.ppermute(value, ('row', 'col'), pairs)  3.98 us
    pallas_call x1, Pallas kernels, local(): call(functools.partial(sum_kernel, rows, cols, owned_blocks), jax.ShapeDt...  3.48 us
    ppermute x1, starting transfers between devices, local(): lax.ppermute(scaled, 'row', [(0, 1)])  2.75 us
    ppermute x1, starting transfers between devices, local(): lax.ppermute(value[1], 'row', [(1, 0)])  1.29 us
    ppermute x1, waiting for transfers between devices, local(): other_weight = lax.ppermute(leaving, 'row', [(0, 1)])  1.19 us
    pallas_call x1, Pallas kernels, local(): call(scale_kernel, [jax.ShapeDtypeStruct((sets + DEGREE_LINES if paired e...  1.07 us
  transfers between devices with their start and end apart: 9, of which 3 were waited for; matrix products, arithmetic and copies ran while one was open for 0% of the time, Pallas kernels for 10%

profile of v8, /device:TPU:0, one launch (start us, length us, event | category | flops | bytes accessed | tf_op | source)
XLA Modules:
  0.0 36.0 jit_solution(13610491419257963366)
XLA Ops:
  0.0 0.0 copy-start
  0.0 1.1 %scale.1 = (bf16[144,128]{1,0:T(8,128)(2,1)S(1)}, s32[1,1,384]{2,1,0:T(1,128)S(4)}, s32[1,1,384]{2,1,0:T(1,128)S(4)}, s32[16,128]{1,0:T(8,128)S(1)}) custom-call(f32[128,128]{1,0:T(8,128)} %prior_hbm.1, s32[1,128]{1,0:T(1,128)} %bitcast.3, s32[1,1,384]{2,1,0:T(1,128)} %out_hbm.1, s32[1,1,384]{2,1,0:T(1,128)} %in_hbm.1, s32[16,128]{1,0:T(8,128)} %bitcast.2), custom_call_target="tpu_custom_call" | custom-call | flops 12884901888 | bytes 98304 | tf_op jit(solution)/shard_map/scale/pallas_call | solution.py:215
  1.1 2.8 %collective-permute-start = (bf16[144,128]{1,0:T(8,128)(2,1)S(1)}, bf16[144,128]{1,0:T(8,128)(2,1)S(1)}, u32[]{:S(2)}, u32[]{:S(2)}) collective-permute-start(bf16[144,128]{1,0:T(8,128)(2,1)S(1)} %get-tuple-element.13.mine_ref), channel_id=1, source_target_pairs={{0,16},{1,17},{2,18},{3,19},{4,20},{5,21},{6,22},{7,23},{8,24},{9,... | collective-permute-start | bytes 110600 | tf_op jit(solution)/shard_map/ppermute | solution.py:250
  4.5 0.2 collective-permute-done.theirs_ref
  4.7 0.7 %collective-permute-start.3 = (bf16[2,128,128]{2,1,0:T(8,128)(2,1)S(1)}, bf16[2,128,128]{2,1,0:T(8,128)(2,1)S(1)}, u32[]{:S(2)}, u32[]{:S(2)}) collective-permute-start(bf16[2,128,128]{2,1,0:T(8,128)(2,1)S(1)} %get-tuple-element.14.after_ref.refs_0_), channel_id=1, source_target_pairs={{28,16},{24,20},{20,24},{16,28},{29,17},{25,21},{21,25},{17,29},{3... | collective-permute-start | bytes 196616 | tf_op jit(solution)/shard_map/ppermute | solution.py:55
  5.4 0.7 %collective-permute-start.2 = (bf16[2,128,128]{2,1,0:T(8,128)(2,1)S(1)}, bf16[2,128,128]{2,1,0:T(8,128)(2,1)S(1)}, u32[]{:S(2)}, u32[]{:S(2)}) collective-permute-start(bf16[2,128,128]{2,1,0:T(8,128)(2,1)S(1)} %get-tuple-element.14.after_ref.refs_0_), channel_id=1, source_target_pairs={{24,16},{28,20},{16,24},{20,28},{25,17},{29,21},{17,25},{21,29},{2... | collective-permute-start | bytes 196616 | tf_op jit(solution)/shard_map/ppermute | solution.py:55
  6.0 0.7 %collective-permute-start.1 = (bf16[2,128,128]{2,1,0:T(8,128)(2,1)S(1)}, bf16[2,128,128]{2,1,0:T(8,128)(2,1)S(1)}, u32[]{:S(2)}, u32[]{:S(2)}) collective-permute-start(bf16[2,128,128]{2,1,0:T(8,128)(2,1)S(1)} %get-tuple-element.14.after_ref.refs_0_), channel_id=1, source_target_pairs={{20,16},{16,20},{28,24},{24,28},{21,17},{17,21},{29,25},{25,29},{2... | collective-permute-start | bytes 196616 | tf_op jit(solution)/shard_map/ppermute | solution.py:55
  6.7 0.0 copy-done
  6.7 3.5 %sum_tiles.1.refs_4_ = bf16[2,4,128,256]{3,2,1,0:T(8,128)(2,1)S(1)} custom-call(bf16[2,128,128]{2,1,0:T(8,128)(2,1)S(1)} %get-tuple-element.14.after_ref.refs_0_, s32[1,1]{1,0:T(1,128)S(6)} %copy.8.count_ref, s32[1,1,384]{2,1,0:T(1,128)S(4)} %get-tuple-element.15.out_ref, s32[1,1,384]{2,1,0:T(1,128)S(4)} %get-tuple-element.16.in_ref, ...), custom_call_target="tpu_custom_call" | custom-call | flops 6291456 | bytes 12582912 | tf_op jit(solution)/shard_map/sum_tiles/pallas_call | solution.py:253
  10.2 0.0 collective-permute-done.3.refs_3_
  10.2 0.0 collective-permute-done.2.refs_2_
  10.2 0.0 collective-permute-done.1.refs_1_
  10.3 9.2 %collective-permute-start.4 = (bf16[2,4,128,256]{3,2,1,0:T(8,128)(2,1)S(1)}, bf16[2,4,128,256]{3,2,1,0:T(8,128)(2,1)S(1)}, u32[]{:S(2)}, u32[]{:S(2)}) collective-permute-start(bf16[2,4,128,256]{3,2,1,0:T(8,128)(2,1)S(1)} %leave.1.after_ref), channel_id=1, source_target_pairs={{0,16},{1,17},{2,18},{3,19},{4,20},{5,21},{6,22},{7,23},{8,24},{9,... | collective-permute-start | bytes 1572872 | tf_op jit(solution)/shard_map/ppermute | solution.py:287
  19.5 0.3 restart.1.refs_6_
  19.8 1.2 %collective-permute-done.4.refs_5_ = bf16[2,4,128,256]{3,2,1,0:T(8,128)(2,1)S(1)} collective-permute-done((bf16[2,4,128,256]{3,2,1,0:T(8,128)(2,1)S(1)}, bf16[2,4,128,256]{3,2,1,0:T(8,128)(2,1)S(1)}, u32[]{:S(2)}, u32[]{:S(2)}) %collective-permute-start.4) | collective-permute-done | bytes 524320 | tf_op jit(solution)/shard_map/ppermute | solution.py:287
  21.0 0.3 next.1.refs_0_
  21.3 0.7 %collective-permute-start.7 = (bf16[2,128,128]{2,1,0:T(8,128)(2,1)S(1)}, bf16[2,128,128]{2,1,0:T(8,128)(2,1)S(1)}, u32[]{:S(2)}, u32[]{:S(2)}) collective-permute-start(bf16[2,128,128]{2,1,0:T(8,128)(2,1)S(1)} %next.1.refs_0_), channel_id=1, source_target_pairs={{28,16},{24,20},{20,24},{16,28},{29,17},{25,21},{21,25},{17,29},{3... | collective-permute-start | bytes 196616 | tf_op jit(solution)/shard_map/ppermute | solution.py:55
  22.0 0.7 %collective-permute-start.6 = (bf16[2,128,128]{2,1,0:T(8,128)(2,1)S(1)}, bf16[2,128,128]{2,1,0:T(8,128)(2,1)S(1)}, u32[]{:S(2)}, u32[]{:S(2)}) collective-permute-start(bf16[2,128,128]{2,1,0:T(8,128)(2,1)S(1)} %next.1.refs_0_), channel_id=1, source_target_pairs={{24,16},{28,20},{16,24},{20,28},{25,17},{29,21},{17,25},{21,29},{2... | collective-permute-start | bytes 196616 | tf_op jit(solution)/shard_map/ppermute | solution.py:55
  22.7 0.7 %collective-permute-start.5 = (bf16[2,128,128]{2,1,0:T(8,128)(2,1)S(1)}, bf16[2,128,128]{2,1,0:T(8,128)(2,1)S(1)}, u32[]{:S(2)}, u32[]{:S(2)}) collective-permute-start(bf16[2,128,128]{2,1,0:T(8,128)(2,1)S(1)} %next.1.refs_0_), channel_id=1, source_target_pairs={{20,16},{16,20},{28,24},{24,28},{21,17},{17,21},{29,25},{25,29},{2... | collective-permute-start | bytes 196616 | tf_op jit(solution)/shard_map/ppermute | solution.py:55
  23.3 0.0 collective-permute-done.7.refs_3_
  23.4 0.0 collective-permute-done.6.refs_2_
  23.4 0.0 collective-permute-done.5.refs_1_
  23.4 0.3 last.1
  23.7 1.3 %collective-permute-start.8 = (f32[128,128]{1,0:T(8,128)S(1)}, f32[128,128]{1,0:T(8,128)S(1)}, u32[]{:S(2)}, u32[]{:S(2)}) collective-permute-start(f32[128,128]{1,0:T(8,128)S(1)} %get-tuple-element.20), channel_id=1, source_target_pairs={{16,0},{17,1},{18,2},{19,3},{20,4},{21,5},{22,6},{23,7},{24,8},{25... | collective-permute-start | bytes 196616 | tf_op jit(solution)/shard_map/ppermute | solution.py:311
  25.0 10.4 %collective-permute-done.8.received_ref = f32[128,128]{1,0:T(8,128)S(1)} collective-permute-done((f32[128,128]{1,0:T(8,128)S(1)}, f32[128,128]{1,0:T(8,128)S(1)}, u32[]{:S(2)}, u32[]{:S(2)}) %collective-permute-start.8) | collective-permute-done | bytes 65568 | tf_op jit(solution)/shard_map/ppermute | solution.py:311
  35.4 0.6 %result.1 = f32[128,128]{1,0:T(8,128)} custom-call(f32[128,128]{1,0:T(8,128)S(1)} %get-tuple-element.19.mine_ref, f32[128,128]{1,0:T(8,128)S(1)} %collective-permute-done.8.received_ref), custom_call_target="tpu_custom_call" | custom-call | bytes 196608 | tf_op jit(solution)/shard_map/result/pallas_call | solution.py:304
  (2 shorter events, 0.0 us)
Async XLA Ops:
  0.0 6.7 %copy-start = (bf16[1,1,384,128,128]{4,3,2,1,0:T(8,128)(2,1)S(1)}, bf16[1,1,384,128,128]{4,3,2,1,0:T(8,128)(2,1)}, u32[]{:S(2)}) copy-start(bf16[1,1,384,128,128]{4,3,2,1,0:T(8,128)(2,1)} %tiles_ref.1) | copy-start | bytes 37748740
  1.1 3.6 %collective-permute-start = (bf16[144,128]{1,0:T(8,128)(2,1)S(1)}, bf16[144,128]{1,0:T(8,128)(2,1)S(1)}, u32[]{:S(2)}, u32[]{:S(2)}) collective-permute-start(bf16[144,128]{1,0:T(8,128)(2,1)S(1)} %get-tuple-element.13.mine_ref), channel_id=1, source_target_pairs={{0,16},{1,17},{2,18},{3,19},{4,20},{5,21},{6,22},{7,23},{8,24},{9,... | collective-permute-start | bytes 110600 | tf_op jit(solution)/shard_map/ppermute | solution.py:250
  4.7 5.5 %collective-permute-start.3 = (bf16[2,128,128]{2,1,0:T(8,128)(2,1)S(1)}, bf16[2,128,128]{2,1,0:T(8,128)(2,1)S(1)}, u32[]{:S(2)}, u32[]{:S(2)}) collective-permute-start(bf16[2,128,128]{2,1,0:T(8,128)(2,1)S(1)} %get-tuple-element.14.after_ref.refs_0_), channel_id=1, source_target_pairs={{28,16},{24,20},{20,24},{16,28},{29,17},{25,21},{21,25},{17,29},{3... | collective-permute-start | bytes 196616 | tf_op jit(solution)/shard_map/ppermute | solution.py:55
  5.4 4.9 %collective-permute-start.2 = (bf16[2,128,128]{2,1,0:T(8,128)(2,1)S(1)}, bf16[2,128,128]{2,1,0:T(8,128)(2,1)S(1)}, u32[]{:S(2)}, u32[]{:S(2)}) collective-permute-start(bf16[2,128,128]{2,1,0:T(8,128)(2,1)S(1)} %get-tuple-element.14.after_ref.refs_0_), channel_id=1, source_target_pairs={{24,16},{28,20},{16,24},{20,28},{25,17},{29,21},{17,25},{21,29},{2... | collective-permute-start | bytes 196616 | tf_op jit(solution)/shard_map/ppermute | solution.py:55
  6.0 4.2 %collective-permute-start.1 = (bf16[2,128,128]{2,1,0:T(8,128)(2,1)S(1)}, bf16[2,128,128]{2,1,0:T(8,128)(2,1)S(1)}, u32[]{:S(2)}, u32[]{:S(2)}) collective-permute-start(bf16[2,128,128]{2,1,0:T(8,128)(2,1)S(1)} %get-tuple-element.14.after_ref.refs_0_), channel_id=1, source_target_pairs={{20,16},{16,20},{28,24},{24,28},{21,17},{17,21},{29,25},{25,29},{2... | collective-permute-start | bytes 196616 | tf_op jit(solution)/shard_map/ppermute | solution.py:55
  10.3 10.7 %collective-permute-start.4 = (bf16[2,4,128,256]{3,2,1,0:T(8,128)(2,1)S(1)}, bf16[2,4,128,256]{3,2,1,0:T(8,128)(2,1)S(1)}, u32[]{:S(2)}, u32[]{:S(2)}) collective-permute-start(bf16[2,4,128,256]{3,2,1,0:T(8,128)(2,1)S(1)} %leave.1.after_ref), channel_id=1, source_target_pairs={{0,16},{1,17},{2,18},{3,19},{4,20},{5,21},{6,22},{7,23},{8,24},{9,... | collective-permute-start | bytes 1572872 | tf_op jit(solution)/shard_map/ppermute | solution.py:287
  21.3 2.0 %collective-permute-start.7 = (bf16[2,128,128]{2,1,0:T(8,128)(2,1)S(1)}, bf16[2,128,128]{2,1,0:T(8,128)(2,1)S(1)}, u32[]{:S(2)}, u32[]{:S(2)}) collective-permute-start(bf16[2,128,128]{2,1,0:T(8,128)(2,1)S(1)} %next.1.refs_0_), channel_id=1, source_target_pairs={{28,16},{24,20},{20,24},{16,28},{29,17},{25,21},{21,25},{17,29},{3... | collective-permute-start | bytes 196616 | tf_op jit(solution)/shard_map/ppermute | solution.py:55
  22.0 1.4 %collective-permute-start.6 = (bf16[2,128,128]{2,1,0:T(8,128)(2,1)S(1)}, bf16[2,128,128]{2,1,0:T(8,128)(2,1)S(1)}, u32[]{:S(2)}, u32[]{:S(2)}) collective-permute-start(bf16[2,128,128]{2,1,0:T(8,128)(2,1)S(1)} %next.1.refs_0_), channel_id=1, source_target_pairs={{24,16},{28,20},{16,24},{20,28},{25,17},{29,21},{17,25},{21,29},{2... | collective-permute-start | bytes 196616 | tf_op jit(solution)/shard_map/ppermute | solution.py:55
  22.7 0.7 %collective-permute-start.5 = (bf16[2,128,128]{2,1,0:T(8,128)(2,1)S(1)}, bf16[2,128,128]{2,1,0:T(8,128)(2,1)S(1)}, u32[]{:S(2)}, u32[]{:S(2)}) collective-permute-start(bf16[2,128,128]{2,1,0:T(8,128)(2,1)S(1)} %next.1.refs_0_), channel_id=1, source_target_pairs={{20,16},{16,20},{28,24},{24,28},{21,17},{17,21},{29,25},{25,29},{2... | collective-permute-start | bytes 196616 | tf_op jit(solution)/shard_map/ppermute | solution.py:55
  23.7 11.7 %collective-permute-start.8 = (f32[128,128]{1,0:T(8,128)S(1)}, f32[128,128]{1,0:T(8,128)S(1)}, u32[]{:S(2)}, u32[]{:S(2)}) collective-permute-start(f32[128,128]{1,0:T(8,128)S(1)} %get-tuple-element.20), channel_id=1, source_target_pairs={{16,0},{17,1},{18,2},{19,3},{20,4},{21,5},{22,6},{23,7},{24,8},{25... | collective-permute-start | bytes 196616 | tf_op jit(solution)/shard_map/ppermute | solution.py:311
